TPU v7x, 128 devices: a whole 4x4x4 slice. The times are simulated.
128 devices in a mesh: shard: 16 (over y, x), ctx: 4 (over z_lo, core), tp: 2 (over z_hi).
Axes of the slice: x: 4, y: 4, z: 4 (z_hi: 2, z_lo: 2; z = z_hi * 2 + z_lo), core: 2. Of those that a mesh axis runs over, the one named last changes fastest.
Arguments:
- tokens: float32 [20480, 960], P(('shard', 'ctx', 'tp')), may hold values from -6 to 6
- segment_ids: int32 [20480], P(('shard', 'ctx', 'tp')), may hold values from 0 to 4, as said below
- positions: int32 [20480], P(('shard', 'ctx', 'tp')), may hold values from 0 to 1023, as said below
- cotangent: float32 [20480, 960], P(('shard', 'ctx', 'tp')), may hold values from -6 to 6
- attn_gain: bfloat16 [2, 960], P(None, 'shard'), may hold values from 0.5 to 1.5
- w_query: bfloat16 [2, 960, 960], P(None, 'shard'), may hold values from -6 to 6
- w_key: bfloat16 [2, 960, 320], P(None, 'shard'), may hold values from -6 to 6
- w_value: bfloat16 [2, 960, 320], P(None, 'shard'), may hold values from -0.1875 to 0.1875
- w_out: bfloat16 [2, 960, 960], P(None, 'shard'), may hold values from -3 to 3
- ffn_gain: bfloat16 [2, 960], P(None, 'shard'), may hold values from 0.5 to 1.5
- w_gate: bfloat16 [2, 960, 2560], P(None, 'shard', 'tp'), may hold values from -0.1875 to 0.1875
- w_up: bfloat16 [2, 960, 2560], P(None, 'shard', 'tp'), may hold values from -0.1875 to 0.1875
- w_down: bfloat16 [2, 960, 2560], P(None, 'shard', 'tp'), may hold values from -0.125 to 0.125
Outputs:
- block_out: float32 [20480, 960], P(('shard', 'ctx', 'tp'))
- input_grad: float32 [20480, 960], P(('shard', 'ctx', 'tp'))
- grad_attn_gain: float32 [2, 960], P(None, 'shard')
- grad_w_query: float32 [2, 960, 960], P(None, 'shard')
- grad_w_key: float32 [2, 960, 320], P(None, 'shard')
- grad_w_value: float32 [2, 960, 320], P(None, 'shard')
- grad_w_out: float32 [2, 960, 960], P(None, 'shard')
- grad_ffn_gain: float32 [2, 960], P(None, 'shard')
- grad_w_gate: float32 [2, 960, 2560], P(None, 'shard', 'tp')
- grad_w_up: float32 [2, 960, 2560], P(None, 'shard', 'tp')
- grad_w_down: float32 [2, 960, 2560], P(None, 'shard', 'tp')
Inputs may be any that keep to these rules, and one draw needn't show every extreme that they name: `segment_ids`: within each block of 1280 consecutive tokens (one index of shard), ids never fall and a sequence's tokens are consecutive; exactly one sequence has 1024 tokens and every other has fewer. positions[t] counts the earlier tokens of t's sequence in its block.
All inputs are finite; a program needn't handle non-finite values.
Results may differ from a plain program's by a relative error of at most 0.023.
Values may be sent and summed in bfloat16 or wider, within the bound.
No kernel may reach another device: no remote copies, remote signals or barrier semaphores. Data moves between devices by JAX's collectives and lax.ppermute only.
A program may use at most 256 MiB of HBM per device.

v0:
```python
import jax
import jax.numpy as jnp
from jax import lax
from jax.sharding import PartitionSpec as P

HEADS = 15
KV_HEADS = 5
HEAD = 64


EPSILON = 1e-05
THETA = 100000.0
MASKED = -1e30


def product(left, right):
    return jnp.dot(left, right, preferred_element_type=jnp.float32)


def by_rows(left, right):
    return lax.dot_general(
        left, right, (((0,), (0,)), ((), ())), preferred_element_type=jnp.float32
    )


def by_columns(left, right):
    return lax.dot_general(
        left, right, (((1,), (1,)), ((), ())), preferred_element_type=jnp.float32
    )


def rope_tables(positions):
    half_head = HEAD // 2
    freqs = THETA ** (-2.0 * jnp.arange(half_head, dtype=jnp.float32) / HEAD)
    angles = positions.astype(jnp.float32)[:, None] * freqs[None, :]
    return (jnp.cos(angles), jnp.sin(angles))


def rotate(values, cosine, sine, direction):
    row_count = values.shape[0]
    split_view = values.reshape(row_count, -1, 2, HEAD // 2)
    first_half = split_view[:, :, 0]
    second_half = split_view[:, :, 1]
    cos_rows = cosine[:, None, :]
    sin_rows = direction * sine[:, None, :]
    turned = jnp.stack(
        [
            first_half * cos_rows - second_half * sin_rows,
            second_half * cos_rows + first_half * sin_rows,
        ],
        axis=2,
    )
    return turned.reshape(row_count, -1)


def rms_forward(values, gain):
    scale = lax.rsqrt(jnp.mean(values * values, axis=-1, keepdims=True) + EPSILON)
    return (values * scale * gain.astype(jnp.float32), scale)


def rms_backward(values, scale, gain, grad_normed):
    weighted = grad_normed * gain.astype(jnp.float32)
    grad_values = scale * weighted - values * (scale * scale * scale) * jnp.mean(
        weighted * values, axis=-1, keepdims=True
    )
    grad_gain = jnp.sum(grad_normed * values * scale, axis=0)
    return (grad_values, grad_gain)


def head_rows(matrix, group, row_count):
    view = matrix.reshape(row_count, KV_HEADS, HEADS // KV_HEADS, HEAD)[:, group]
    return jnp.transpose(view, (1, 0, 2)).reshape(-1, HEAD)


def head_back(block, row_count):
    return jnp.transpose(block.reshape(HEADS // KV_HEADS, row_count, HEAD), (1, 0, 2)).reshape(
        row_count, -1
    )


def masked_scores(query_block, key_block, visible):
    raw = by_columns(query_block, key_block) * HEAD ** (-0.5)
    shaped = raw.reshape(HEADS // KV_HEADS, visible.shape[0], -1)
    return jnp.where(visible[None], shaped, MASKED).reshape(raw.shape)


def shards(
    tokens,
    segment_ids,
    positions,
    cotangent,
    attn_gain,
    w_query,
    w_key,
    w_value,
    w_out,
    ffn_gain,
    w_gate,
    w_up,
    w_down,
):
    layer_total = attn_gain.shape[0]
    row_count = tokens.shape[0]
    cosine, sine = rope_tables(positions)
    stream = tokens
    saved = []
    for layer in range(layer_total):
        weights = (
            lax.all_gather(attn_gain[layer], "shard", axis=0, tiled=True),
            lax.all_gather(w_query[layer], "shard", axis=0, tiled=True),
            lax.all_gather(w_key[layer], "shard", axis=0, tiled=True),
            lax.all_gather(w_value[layer], "shard", axis=0, tiled=True),
            lax.all_gather(w_out[layer], "shard", axis=0, tiled=True),
            lax.all_gather(ffn_gain[layer], "shard", axis=0, tiled=True),
            lax.all_gather(w_gate[layer], "shard", axis=0, tiled=True),
            lax.all_gather(w_up[layer], "shard", axis=0, tiled=True),
            lax.all_gather(w_down[layer], "shard", axis=0, tiled=True),
        )
        (
            gain_one,
            query_weight,
            key_weight,
            value_weight,
            out_weight,
            gain_two,
            gate_weight,
            up_weight,
            down_weight,
        ) = weights
        normed_one, scale_one = rms_forward(stream, gain_one)
        normed_one = normed_one.astype(jnp.bfloat16)
        query = rotate(product(normed_one, query_weight), cosine, sine, 1.0).astype(jnp.bfloat16)
        key_rows = rotate(product(normed_one, key_weight), cosine, sine, 1.0).astype(jnp.bfloat16)
        value_rows = product(normed_one, value_weight).astype(jnp.bfloat16)
        key_all, value_all, segment_all, position_all = (
            lax.all_gather(key_rows, ("ctx", "tp"), axis=0, tiled=True),
            lax.all_gather(value_rows, ("ctx", "tp"), axis=0, tiled=True),
            lax.all_gather(segment_ids, ("ctx", "tp"), axis=0, tiled=True),
            lax.all_gather(positions, ("ctx", "tp"), axis=0, tiled=True),
        )
        visible = (segment_ids[:, None] == segment_all[None, :]) & (
            position_all[None, :] <= positions[:, None]
        )
        attended_parts = []
        log_totals = []
        for group in range(KV_HEADS):
            query_block = head_rows(query, group, row_count)
            key_block = key_all[:, group * HEAD : (group + 1) * HEAD]
            value_block = value_all[:, group * HEAD : (group + 1) * HEAD]
            scores = masked_scores(query_block, key_block, visible)
            top = jnp.max(scores, axis=-1, keepdims=True)
            log_total = top + jnp.log(jnp.sum(jnp.exp(scores - top), axis=-1, keepdims=True))
            probs = jnp.exp(scores - log_total).astype(jnp.bfloat16)
            attended_parts.append(head_back(product(probs, value_block), row_count))
            log_totals.append(log_total)
        attended = jnp.concatenate(attended_parts, axis=1).astype(jnp.bfloat16)
        mixed = stream + by_columns(attended, out_weight)
        normed_two, scale_two = rms_forward(mixed, gain_two)
        normed_two = normed_two.astype(jnp.bfloat16)
        normed_pair = lax.all_gather(normed_two, "tp", axis=0, tiled=True)
        gate = product(normed_pair, gate_weight)
        up_value = product(normed_pair, up_weight)
        sigma = jax.nn.sigmoid(gate)
        swish = gate * sigma
        hidden = (swish * up_value).astype(jnp.bfloat16)
        ffn_out = lax.psum_scatter(
            by_columns(hidden, down_weight), "tp", scatter_dimension=0, tiled=True
        )
        saved.append(
            (
                stream,
                scale_one,
                normed_one,
                query,
                key_all,
                value_all,
                visible,
                log_totals,
                attended,
                mixed,
                scale_two,
                normed_pair,
                gate,
                up_value,
                sigma,
                swish,
                hidden,
            )
        )
        stream = mixed + ffn_out
    grad_stream = cotangent
    grad_layers = [None] * layer_total
    for layer in reversed(range(layer_total)):
        weights = (
            lax.all_gather(attn_gain[layer], "shard", axis=0, tiled=True),
            lax.all_gather(w_query[layer], "shard", axis=0, tiled=True),
            lax.all_gather(w_key[layer], "shard", axis=0, tiled=True),
            lax.all_gather(w_value[layer], "shard", axis=0, tiled=True),
            lax.all_gather(w_out[layer], "shard", axis=0, tiled=True),
            lax.all_gather(ffn_gain[layer], "shard", axis=0, tiled=True),
            lax.all_gather(w_gate[layer], "shard", axis=0, tiled=True),
            lax.all_gather(w_up[layer], "shard", axis=0, tiled=True),
            lax.all_gather(w_down[layer], "shard", axis=0, tiled=True),
        )
        (
            gain_one,
            query_weight,
            key_weight,
            value_weight,
            out_weight,
            gain_two,
            gate_weight,
            up_weight,
            down_weight,
        ) = weights
        (
            layer_input,
            scale_one,
            normed_one,
            query,
            key_all,
            value_all,
            visible,
            log_totals,
            attended,
            mixed,
            scale_two,
            normed_pair,
            gate,
            up_value,
            sigma,
            swish,
            hidden,
        ) = saved[layer]
        grad_out_b = grad_stream.astype(jnp.bfloat16)
        grad_out_pair = lax.all_gather(grad_out_b, "tp", axis=0, tiled=True)
        grad_hidden = product(grad_out_pair, down_weight)
        grad_down = by_rows(grad_out_pair, hidden)
        grad_up_in = (grad_hidden * swish).astype(jnp.bfloat16)
        grad_gate_in = (grad_hidden * up_value * sigma * (1.0 + gate * (1.0 - sigma))).astype(
            jnp.bfloat16
        )
        grad_gate = by_rows(normed_pair, grad_gate_in)
        grad_up = by_rows(normed_pair, grad_up_in)
        grad_normed_two = lax.psum_scatter(
            (by_columns(grad_gate_in, gate_weight) + by_columns(grad_up_in, up_weight)).astype(
                jnp.bfloat16
            ),
            "tp",
            scatter_dimension=0,
            tiled=True,
        ).astype(jnp.float32)
        grad_mixed_norm, grad_gain_two = rms_backward(mixed, scale_two, gain_two, grad_normed_two)
        grad_mixed = grad_stream + grad_mixed_norm
        grad_mixed_b = grad_mixed.astype(jnp.bfloat16)
        grad_attended = product(grad_mixed_b, out_weight)
        grad_out_weight = by_rows(grad_mixed_b, attended)
        grad_attended_b = grad_attended.astype(jnp.bfloat16)
        query_parts = []
        key_parts = []
        value_parts = []
        for group in range(KV_HEADS):
            query_block = head_rows(query, group, row_count)
            grad_block = head_rows(grad_attended_b, group, row_count)
            key_block = key_all[:, group * HEAD : (group + 1) * HEAD]
            value_block = value_all[:, group * HEAD : (group + 1) * HEAD]
            scores = masked_scores(query_block, key_block, visible)
            probs_exact = jnp.exp(scores - log_totals[group])
            probs = probs_exact.astype(jnp.bfloat16)
            grad_probs = by_columns(grad_block, value_block)
            delta = jnp.sum(probs_exact * grad_probs, axis=-1, keepdims=True)
            grad_scores = (probs_exact * (grad_probs - delta) * HEAD ** (-0.5)).astype(jnp.bfloat16)
            query_parts.append(head_back(product(grad_scores, key_block), row_count))
            key_parts.append(by_rows(grad_scores, query_block))
            value_parts.append(by_rows(probs, grad_block))
        grad_query = jnp.concatenate(query_parts, axis=1)
        key_value_terms = jnp.concatenate(key_parts + value_parts, axis=1)
        key_value_grad = lax.psum_scatter(
            key_value_terms.astype(jnp.bfloat16), ("ctx", "tp"), scatter_dimension=0, tiled=True
        ).astype(jnp.float32)
        key_width = key_weight.shape[1]
        grad_query_b = rotate(grad_query, cosine, sine, -1.0).astype(jnp.bfloat16)
        grad_key_b = rotate(key_value_grad[:, :key_width], cosine, sine, -1.0).astype(jnp.bfloat16)
        grad_value_b = key_value_grad[:, key_width:].astype(jnp.bfloat16)
        grad_query_weight = by_rows(normed_one, grad_query_b)
        grad_key_weight = by_rows(normed_one, grad_key_b)
        grad_value_weight = by_rows(normed_one, grad_value_b)
        grad_normed_one = (
            by_columns(grad_query_b, query_weight)
            + by_columns(grad_key_b, key_weight)
            + by_columns(grad_value_b, value_weight)
        )
        grad_input_norm, grad_gain_one = rms_backward(
            layer_input, scale_one, gain_one, grad_normed_one
        )
        grad_stream = grad_mixed + grad_input_norm
        grad_layers[layer] = (
            lax.psum_scatter(grad_gain_one, ("shard", "ctx"), scatter_dimension=0, tiled=True),
            lax.psum_scatter(grad_query_weight, ("shard", "ctx"), scatter_dimension=0, tiled=True),
            lax.psum_scatter(grad_key_weight, ("shard", "ctx"), scatter_dimension=0, tiled=True),
            lax.psum_scatter(grad_value_weight, ("shard", "ctx"), scatter_dimension=0, tiled=True),
            lax.psum_scatter(grad_out_weight, ("shard", "ctx"), scatter_dimension=0, tiled=True),
            lax.psum_scatter(grad_gain_two, ("shard", "ctx"), scatter_dimension=0, tiled=True),
            lax.psum_scatter(grad_gate, ("shard", "ctx"), scatter_dimension=0, tiled=True),
            lax.psum_scatter(grad_up, ("shard", "ctx"), scatter_dimension=0, tiled=True),
            lax.psum_scatter(grad_down, ("shard", "ctx"), scatter_dimension=0, tiled=True),
        )
    stacked = tuple(
        (
            jnp.stack([grad_layers[layer][index] for layer in range(layer_total)])
            for index in range(9)
        )
    )
    (
        gain_one_grads,
        query_grads,
        key_grads,
        value_grads,
        out_grads,
        gain_two_grads,
        gate_grads,
        up_grads,
        down_grads,
    ) = stacked
    (
        gain_one_grads,
        query_grads,
        key_grads,
        value_grads,
        out_grads,
        gain_two_grads,
        gate_grads,
        up_grads,
        down_grads,
    ) = (
        lax.all_gather(gain_one_grads.astype(jnp.bfloat16), "ctx", axis=1, tiled=True).astype(
            gain_one_grads.dtype
        ),
        lax.all_gather(query_grads.astype(jnp.bfloat16), "ctx", axis=1, tiled=True).astype(
            query_grads.dtype
        ),
        lax.all_gather(key_grads.astype(jnp.bfloat16), "ctx", axis=1, tiled=True).astype(
            key_grads.dtype
        ),
        lax.all_gather(value_grads.astype(jnp.bfloat16), "ctx", axis=1, tiled=True).astype(
            value_grads.dtype
        ),
        lax.all_gather(out_grads.astype(jnp.bfloat16), "ctx", axis=1, tiled=True).astype(
            out_grads.dtype
        ),
        lax.all_gather(gain_two_grads.astype(jnp.bfloat16), "ctx", axis=1, tiled=True).astype(
            gain_two_grads.dtype
        ),
        lax.all_gather(gate_grads.astype(jnp.bfloat16), "ctx", axis=1, tiled=True).astype(
            gate_grads.dtype
        ),
        lax.all_gather(up_grads.astype(jnp.bfloat16), "ctx", axis=1, tiled=True).astype(
            up_grads.dtype
        ),
        lax.all_gather(down_grads.astype(jnp.bfloat16), "ctx", axis=1, tiled=True).astype(
            down_grads.dtype
        ),
    )
    gain_one_grads, query_grads, key_grads, value_grads, out_grads, gain_two_grads = (
        lax.psum(gain_one_grads.astype(jnp.bfloat16), "tp").astype(jnp.float32),
        lax.psum(query_grads.astype(jnp.bfloat16), "tp").astype(jnp.float32),
        lax.psum(key_grads.astype(jnp.bfloat16), "tp").astype(jnp.float32),
        lax.psum(value_grads.astype(jnp.bfloat16), "tp").astype(jnp.float32),
        lax.psum(out_grads.astype(jnp.bfloat16), "tp").astype(jnp.float32),
        lax.psum(gain_two_grads.astype(jnp.bfloat16), "tp").astype(jnp.float32),
    )
    return (
        stream,
        grad_stream,
        gain_one_grads,
        query_grads,
        key_grads,
        value_grads,
        out_grads,
        gain_two_grads,
        gate_grads,
        up_grads,
        down_grads,
    )


def solution(mesh):
    return jax.shard_map(
        shards,
        mesh=mesh,
        in_specs=(
            P(("shard", "ctx", "tp"), None),
            P(("shard", "ctx", "tp")),
            P(("shard", "ctx", "tp")),
            P(("shard", "ctx", "tp"), None),
            P(None, "shard"),
            P(None, "shard", None),
            P(None, "shard", None),
            P(None, "shard", None),
            P(None, "shard", None),
            P(None, "shard"),
            P(None, "shard", "tp"),
            P(None, "shard", "tp"),
            P(None, "shard", "tp"),
        ),
        out_specs=(
            P(("shard", "ctx", "tp"), None),
            P(("shard", "ctx", "tp"), None),
            P(None, "shard"),
            P(None, "shard", None),
            P(None, "shard", None),
            P(None, "shard", None),
            P(None, "shard", None),
            P(None, "shard"),
            P(None, "shard", "tp"),
            P(None, "shard", "tp"),
            P(None, "shard", "tp"),
        ),
        check_vma=False,
    )
```

profile of v0, /device:TPU:1, one launch (start us, length us, event | category | flops | bytes accessed | tf_op | source)
XLA Modules:
  0.0 2043.8 jit_solution(7758924523808409855)
XLA Ops:
  18.9 35.8 %all-reduce.40 = (bf16[960]{0:T(1024)(128)(2,1)S(1)}, bf16[960]{0:T(1024)(128)(2,1)S(1)}, bf16[960]{0:T(1024)(128)(2,1)}, bf16[960]{0:T(1024)(128)(2,1)}) all-reduce(bf16[960]{0:T(1024)(128)(2,1)S(1)} %dynamic-update-slice.2, bf16[960]{0:T(1024)(128)(2,1)S(1)} %dynamic-update-slice.3, ...), channel_id=2, replica_groups=mesh['shard'=16,'ctx'=4,'tp'=2] {'shard'}, use_global_device_ids=true, to_apply=%add.2 | all-reduce | flops 3840 | bytes 15360
  56.1 21.5 %all-gather.2 = bf16[1,960,320]{2,0,1:T(2,128)(2,1)} all-gather(bf16[1,60,320]{2,0,1:T(2,128)(2,1)S(1)} %get-tuple-element.145), channel_id=4, replica_groups=mesh['shard'=16,'ctx'=4,'tp'=2] {'shard'}, dimensions={1}, use_global_device_ids=true | all-gather | bytes 652800 | tf_op jit(solution)/shard_map/all_gather | solution.py:111
  82.2 46.3 %all_gather.136 = bf16[1280,320]{1,0:T(8,128)(2,1)} all-gather(bf16[160,320]{1,0:T(8,128)(2,1)S(1)} %copy.130), channel_id=1, replica_groups=mesh['shard'=16,'ctx'=4,'tp'=2] {'ctx','tp'}, dimensions={0}, use_global_device_ids=true | all-gather | bytes 921600 | tf_op jit(solution)/shard_map/all_gather | solution.py:136
  129.9 24.4 %all-gather.3 = bf16[1,960,320]{2,0,1:T(2,128)(2,1)S(1)} all-gather(bf16[1,60,320]{2,0,1:T(2,128)(2,1)S(1)} %get-tuple-element.143), channel_id=5, replica_groups=mesh['shard'=16,'ctx'=4,'tp'=2] {'shard'}, dimensions={1}, use_global_device_ids=true | all-gather | bytes 652800 | tf_op jit(solution)/shard_map/all_gather | solution.py:112
  157.1 39.5 %all_gather.138 = bf16[1280,320]{1,0:T(8,128)(2,1)} all-gather(bf16[160,320]{1,0:T(8,128)(2,1)S(1)} %convolution_convert_fusion.21), channel_id=1, replica_groups=mesh['shard'=16,'ctx'=4,'tp'=2] {'ctx','tp'}, dimensions={0}, use_global_device_ids=true | all-gather | bytes 921600 | tf_op jit(solution)/shard_map/all_gather | solution.py:137
  197.9 30.4 %all-reduce.38 = (s32[1280]{0:T(1024)S(1)}, s32[1280]{0:T(1024)S(1)}) all-reduce(s32[1280]{0:T(1024)S(1)} %dynamic-update-slice.1, s32[1280]{0:T(1024)S(1)} %dynamic-update-slice), channel_id=1, replica_groups=mesh['shard'=16,'ctx'=4,'tp'=2] {'ctx','tp'}, use_global_device_ids=true, to_apply=%add.1 | all-reduce | flops 2560 | bytes 20480
  264.9 11.8 all_gather.141
  276.7 4.9 fusion.46
  281.6 5.7 multiply_convert_fusion.15
  290.5 4.8 fusion.38
  298.2 24.6 %all-gather.11 = bf16[1,960,320]{2,0,1:T(2,128)(2,1)} all-gather(bf16[1,60,320]{2,0,1:T(2,128)(2,1)S(1)} %copy-done.128), channel_id=13, replica_groups=mesh['shard'=16,'ctx'=4,'tp'=2] {'shard'}, dimensions={1}, use_global_device_ids=true | all-gather | bytes 652800 | tf_op jit(solution)/shard_map/all_gather | solution.py:111
  322.8 4.8 copy.143
  327.5 26.3 %all-gather.12 = bf16[1,960,320]{2,0,1:T(2,128)(2,1)} all-gather(bf16[1,60,320]{2,0,1:T(2,128)(2,1)S(1)} %copy-done.129), channel_id=14, replica_groups=mesh['shard'=16,'ctx'=4,'tp'=2] {'shard'}, dimensions={1}, use_global_device_ids=true | all-gather | bytes 652800 | tf_op jit(solution)/shard_map/all_gather | solution.py:112
  359.6 9.3 all_gather.157
  368.9 4.9 fusion.24
  373.8 14.7 reduce-scatter.39.cloned.1.call-done
  393.7 33.1 %all_gather.148 = bf16[1280,320]{1,0:T(8,128)(2,1)} all-gather(bf16[160,320]{1,0:T(8,128)(2,1)} %copy.145), channel_id=1, replica_groups=mesh['shard'=16,'ctx'=4,'tp'=2] {'ctx','tp'}, dimensions={0}, use_global_device_ids=true | all-gather | bytes 921600 | tf_op jit(solution)/shard_map/all_gather | solution.py:136
  426.8 13.5 all-gather.41.cloned.1.call-done
  447.7 33.5 %all_gather.150 = bf16[1280,320]{1,0:T(8,128)(2,1)} all-gather(bf16[160,320]{1,0:T(8,128)(2,1)S(1)} %convolution_convert_fusion.20), channel_id=1, replica_groups=mesh['shard'=16,'ctx'=4,'tp'=2] {'ctx','tp'}, dimensions={0}, use_global_device_ids=true | all-gather | bytes 921600 | tf_op jit(solution)/shard_map/all_gather | solution.py:137
  524.9 10.9 all_gather.153
  535.8 13.5 all-gather.47.cloned.1.call-done
  549.3 4.8 fusion.30
  554.1 52.7 %all-gather.45.cloned.1.call-done = bf16[1,960,1280]{2,0,1:T(2,128)(2,1)} async-done(((bf16[1,60,1280]{2,0,1:T(2,128)(2,1)}), bf16[1,960,1280]{2,0,1:T(2,128)(2,1)}) %all-gather.45.cloned.1.call-update) | async-done | bytes 2457616 | tf_op jit(solution)/shard_map/all_gather | solution.py:115
  606.8 6.3 multiply_convert_fusion.13
  618.1 4.8 fusion.26
  625.3 5.2 fusion.307
  640.1 26.9 %reduce-scatter.41.cloned.1.call-done = f32[160,960]{1,0:T(8,128)} async-done(((f32[320,960]{1,0:T(8,128)}), f32[160,960]{1,0:T(8,128)}) %reduce-scatter.41.cloned.1.call-update) | async-done | bytes 614416 | tf_op jit(solution)/shard_map/reduce_scatter | solution.py:166
  741.0 23.9 %reduce-scatter.47.cloned.1.call-done = bf16[160,640]{1,0:T(8,128)(2,1)} async-done(((bf16[1280,640]{1,0:T(8,128)(2,1)}), bf16[160,640]{1,0:T(8,128)(2,1)}) %reduce-scatter.47.cloned.1.call-update) | async-done | bytes 204816
  771.7 10.6 all_gather.158
  791.7 4.9 fusion.310
  804.0 6.4 reduce-scatter.45.cloned.1.call-done
  877.0 28.5 %reduce-scatter.49.cloned.1.call-done = bf16[160,640]{1,0:T(8,128)(2,1)} async-done(((bf16[1280,640]{1,0:T(8,128)(2,1)}), bf16[160,640]{1,0:T(8,128)(2,1)}) %reduce-scatter.49.cloned.1.call-update) | async-done | bytes 204816
  909.9 581.4 %fusion.268 = (f32[16,960]{1,0:T(8,128)S(1)}, f32[16,960]{1,0:T(8,128)S(1)}, f32[16,320]{1,0:T(8,128)S(1)}, f32[16,320]{1,0:T(8,128)S(1)}, f32[16,320]{1,0:T(8,1...) fusion(f32[960,960]{1,0:T(8,128)} %fusion.303, ...), kind=kCustom, calls=%all-reduce-scatter.14 | all-reduce-scatter fusion | flops 13107201 | bytes 49971712
  1503.4 8.1 collective-permute-start.18
  1527.0 269.0 %all-reduce.39 = (bf16[960]{0:T(1024)(128)(2,1)S(1)}, bf16[960]{0:T(1024)(128)(2,1)S(1)}, bf16[960]{0:T(1024)(128)(2,1)S(1)}, bf16[960]{0:T(1024)(128)(2,1)S(1)}) all-reduce(f32[960]{0:T(1024)S(1)} %copy-done.164, f32[960]{0:T(1024)S(1)} %get-tuple-element.33, ...), channel_id=27, replica_groups=mesh['shard'=16,'ctx'=4,'tp'=2] {'shard','ctx'}, use_global_device_ids=true, to_apply=%region_47.48.clone | all-reduce | flops 3840 | bytes 23040
  1797.2 11.4 all-gather.19
  1808.7 5.0 all-gather.18
  1813.8 5.3 all-reduce.41
  1851.6 4.9 collective-permute-start.26
  1861.9 5.0 all_gather.162
  1867.0 5.8 all_gather.161
  1889.5 13.1 collective-permute-start.3
  1910.8 5.1 collective-permute-start.6
  1922.4 6.4 all_gather.163
  1941.5 6.2 all_gather.160
  1998.2 5.5 all_gather.167
  2013.2 6.8 all_gather.166
  2022.9 6.1 all_gather.165
  (918 shorter events, 489.3 us)
Async XLA Ops:
  7.2 221.4 %all-gather.31.cloned.1.call-start = ((), (), s32[]{:S(2)}) async-start(), calls=%async_computation.10 | async-start | bytes 4177920 | tf_op jit(solution)/shard_map/all_gather | solution.py:110
  9.6 250.6 %all-gather.33.cloned.1.call-start = ((), (), s32[]{:S(2)}) async-start(), calls=%async_computation.11 | async-start | bytes 4177920 | tf_op jit(solution)/shard_map/all_gather | solution.py:113
  12.0 264.7 %all-gather.35.cloned.1.call-start = ((), (), s32[]{:S(2)}) async-start(), calls=%async_computation.12 | async-start | bytes 5222400 | tf_op jit(solution)/shard_map/all_gather | solution.py:115
  13.3 268.2 %all-gather.37.cloned.1.call-start = ((), (), s32[]{:S(2)}) async-start(), calls=%async_computation.13 | async-start | bytes 5222400 | tf_op jit(solution)/shard_map/all_gather | solution.py:116
  14.7 275.8 %all-gather.39.cloned.1.call-start = ((), (), s32[]{:S(2)}) async-start(), calls=%async_computation.14 | async-start | bytes 5222400 | tf_op jit(solution)/shard_map/all_gather | solution.py:117
  16.0 352.9 %all-gather.49.cloned.1.call-start = ((), (), s32[]{:S(2)}) async-start(), calls=%async_computation.19 | async-start | bytes 5222400 | tf_op jit(solution)/shard_map/all_gather | solution.py:117
  16.6 371.8 %reduce-scatter.39.cloned.1.call-start = ((), (), s32[]{:S(2)}) async-start(), calls=%async_computation.6 | async-start | bytes 1966080 | tf_op jit(solution)/shard_map/reduce_scatter | solution.py:166
  295.3 144.9 %all-gather.41.cloned.1.call-start = ((), (), s32[]{:S(2)}) async-start(), calls=%async_computation.15 | async-start | bytes 4177920 | tf_op jit(solution)/shard_map/all_gather | solution.py:110
  296.1 224.5 %all-gather.43.cloned.1.call-start = ((), (), s32[]{:S(2)}) async-start(), calls=%async_computation.16 | async-start | bytes 4177920 | tf_op jit(solution)/shard_map/all_gather | solution.py:113
  296.8 252.5 %all-gather.47.cloned.1.call-start = ((), (), s32[]{:S(2)}) async-start(), calls=%async_computation.18 | async-start | bytes 5222400 | tf_op jit(solution)/shard_map/all_gather | solution.py:116
  297.4 309.4 %all-gather.45.cloned.1.call-start = ((), (), s32[]{:S(2)}) async-start(), calls=%async_computation.17 | async-start | bytes 5222400 | tf_op jit(solution)/shard_map/all_gather | solution.py:115
  298.1 340.0 %reduce-scatter.43.cloned.1.call-start = ((), (), s32[]{:S(2)}) async-start(), calls=%async_computation.8 | async-start | bytes 983040 | tf_op jit(solution)/shard_map/reduce_scatter | solution.py:245
  618.0 49.0 %reduce-scatter.41.cloned.1.call-start = ((), (), s32[]{:S(2)}) async-start(), calls=%async_computation.7 | async-start | bytes 1966080 | tf_op jit(solution)/shard_map/reduce_scatter | solution.py:166
  622.9 142.0 %reduce-scatter.47.cloned.1.call-start = ((), (), s32[]{:S(2)}) async-start(), calls=%async_computation.20 | async-start | bytes 1843200
  716.7 93.7 %reduce-scatter.45.cloned.1.call-start = ((), (), s32[]{:S(2)}) async-start(), calls=%async_computation.9 | async-start | bytes 983040 | tf_op jit(solution)/shard_map/reduce_scatter | solution.py:245
  789.6 115.8 %reduce-scatter.49.cloned.1.call-start = ((), (), s32[]{:S(2)}) async-start(), calls=%async_computation.21 | async-start | bytes 1843200
  857.3 1172.8 %all-reduce.46.cloned.1.call-start = ((), (), s32[]{:S(2)}) async-start(), calls=%async_computation.22 | async-start | bytes 1351680 | tf_op jit(solution)/shard_map/psum | solution.py:366
  1497.1 325.0 %collective-permute-start.16 = (bf16[16,320]{1,0:T(8,128)(2,1)}, bf16[16,320]{1,0:T(8,128)(2,1)}, u32[]{:S(2)}, u32[]{:S(2)}) collective-permute-start(bf16[16,320]{1,0:T(8,128)(2,1)} %convert.536), channel_id=1, source_target_pairs={{0,2},{2,4},{4,6},{6,8},{8,10},{10,12},{12,14},{14,16},{16,18},{18... | collective-permute-start | bytes 30728
  1501.5 322.0 %collective-permute-start.17 = (bf16[16,320]{1,0:T(8,128)(2,1)}, bf16[16,320]{1,0:T(8,128)(2,1)}, u32[]{:S(2)}, u32[]{:S(2)}) collective-permute-start(bf16[16,320]{1,0:T(8,128)(2,1)} %convert.536), channel_id=1, source_target_pairs={{0,4},{2,6},{4,8},{6,10},{8,12},{10,14},{12,16},{14,18},{16,20},{1... | collective-permute-start | bytes 30728
  1503.4 321.4 %collective-permute-start.18 = (bf16[16,320]{1,0:T(8,128)(2,1)}, bf16[16,320]{1,0:T(8,128)(2,1)}, u32[]{:S(2)}, u32[]{:S(2)}) collective-permute-start(bf16[16,320]{1,0:T(8,128)(2,1)} %convert.536), channel_id=1, source_target_pairs={{0,6},{2,8},{4,10},{6,12},{8,14},{10,16},{12,18},{14,20},{16,22},{... | collective-permute-start | bytes 30728
  1518.2 302.1 %collective-permute-start.19 = (bf16[15,320]{1,0:T(8,128)(2,1)}, bf16[15,320]{1,0:T(8,128)(2,1)}, u32[]{:S(2)}, u32[]{:S(2)}) collective-permute-start(bf16[15,320]{1,0:T(8,128)(2,1)} %slice.428), channel_id=1, source_target_pairs={{0,8},{2,10},{4,12},{6,14},{8,16},{10,18},{12,20},{14,22},{16,24},... | collective-permute-start | bytes 28808
  1521.2 311.4 %collective-permute-start.20 = (bf16[16,320]{1,0:T(8,128)(2,1)}, bf16[16,320]{1,0:T(8,128)(2,1)S(1)}, u32[]{:S(2)}, u32[]{:S(2)}) collective-permute-start(bf16[16,320]{1,0:T(8,128)(2,1)} %convert.537), channel_id=1, source_target_pairs={{0,2},{2,4},{4,6},{6,8},{8,10},{10,12},{12,14},{14,16},{16,18},{18... | collective-permute-start | bytes 30728
  1844.2 31.4 %collective-permute-start.24 = (bf16[16,960]{1,0:T(8,128)(2,1)S(1)}, bf16[16,960]{1,0:T(8,128)(2,1)S(1)}, u32[]{:S(2)}, u32[]{:S(2)}) collective-permute-start(bf16[16,960]{1,0:T(8,128)(2,1)S(1)} %copy-done.151), channel_id=1, source_target_pairs={{0,2},{2,4},{4,6},{6,8},{8,10},{10,12},{12,14},{14,16},{16,18},{18... | collective-permute-start | bytes 92168
  1849.5 28.0 %collective-permute-start.25 = (bf16[16,960]{1,0:T(8,128)(2,1)S(1)}, bf16[16,960]{1,0:T(8,128)(2,1)S(1)}, u32[]{:S(2)}, u32[]{:S(2)}) collective-permute-start(bf16[16,960]{1,0:T(8,128)(2,1)S(1)} %copy-done.151), channel_id=1, source_target_pairs={{0,4},{2,6},{4,8},{6,10},{8,12},{10,14},{12,16},{14,18},{16,20},{1... | collective-permute-start | bytes 92168
  1851.6 27.4 %collective-permute-start.26 = (bf16[16,960]{1,0:T(8,128)(2,1)S(1)}, bf16[16,960]{1,0:T(8,128)(2,1)S(1)}, u32[]{:S(2)}, u32[]{:S(2)}) collective-permute-start(bf16[16,960]{1,0:T(8,128)(2,1)S(1)} %copy-done.151), channel_id=1, source_target_pairs={{0,6},{2,8},{4,10},{6,12},{8,14},{10,16},{12,18},{14,20},{16,22},{... | collective-permute-start | bytes 92168
  1858.1 27.1 %collective-permute-start.28 = (bf16[16,960]{1,0:T(8,128)(2,1)S(1)}, bf16[16,960]{1,0:T(8,128)(2,1)S(1)}, u32[]{:S(2)}, u32[]{:S(2)}) collective-permute-start(bf16[16,960]{1,0:T(8,128)(2,1)S(1)} %copy-done.150), channel_id=1, source_target_pairs={{0,2},{2,4},{4,6},{6,8},{8,10},{10,12},{12,14},{14,16},{16,18},{18... | collective-permute-start | bytes 92168
  1875.6 27.0 %collective-permute-start.30 = (bf16[16,960]{1,0:T(8,128)(2,1)S(1)}, bf16[16,960]{1,0:T(8,128)(2,1)S(1)}, u32[]{:S(2)}, u32[]{:S(2)}) collective-permute-start(bf16[16,960]{1,0:T(8,128)(2,1)S(1)} %copy-done.150), channel_id=1, source_target_pairs={{0,6},{2,8},{4,10},{6,12},{8,14},{10,16},{12,18},{14,20},{16,22},{... | collective-permute-start | bytes 92168
  1879.0 31.7 %collective-permute-start = (bf16[16,960]{1,0:T(8,128)(2,1)S(1)}, bf16[16,960]{1,0:T(8,128)(2,1)S(1)}, u32[]{:S(2)}, u32[]{:S(2)}) collective-permute-start(bf16[16,960]{1,0:T(8,128)(2,1)S(1)} %copy-done.149), channel_id=1, source_target_pairs={{0,2},{2,4},{4,6},{6,8},{8,10},{10,12},{12,14},{14,16},{16,18},{18... | collective-permute-start | bytes 92168
  1882.4 33.4 %collective-permute-start.1 = (bf16[16,960]{1,0:T(8,128)(2,1)S(1)}, bf16[16,960]{1,0:T(8,128)(2,1)S(1)}, u32[]{:S(2)}, u32[]{:S(2)}) collective-permute-start(bf16[16,960]{1,0:T(8,128)(2,1)S(1)} %copy-done.149), channel_id=1, source_target_pairs={{0,4},{2,6},{4,8},{6,10},{8,12},{10,14},{12,16},{14,18},{16,20},{1... | collective-permute-start | bytes 92168
  1885.2 34.7 %collective-permute-start.2 = (bf16[16,960]{1,0:T(8,128)(2,1)S(1)}, bf16[16,960]{1,0:T(8,128)(2,1)S(1)}, u32[]{:S(2)}, u32[]{:S(2)}) collective-permute-start(bf16[16,960]{1,0:T(8,128)(2,1)S(1)} %copy-done.149), channel_id=1, source_target_pairs={{0,6},{2,8},{4,10},{6,12},{8,14},{10,16},{12,18},{14,20},{16,22},{... | collective-permute-start | bytes 92168
  1902.7 28.7 %collective-permute-start.4 = (bf16[16,960]{1,0:T(8,128)(2,1)S(1)}, bf16[16,960]{1,0:T(8,128)(2,1)S(1)}, u32[]{:S(2)}, u32[]{:S(2)}) collective-permute-start(bf16[16,960]{1,0:T(8,128)(2,1)S(1)} %copy-done.148), channel_id=1, source_target_pairs={{0,2},{2,4},{4,6},{6,8},{8,10},{10,12},{12,14},{14,16},{16,18},{18... | collective-permute-start | bytes 92168
  1907.8 27.4 %collective-permute-start.5 = (bf16[16,960]{1,0:T(8,128)(2,1)S(1)}, bf16[16,960]{1,0:T(8,128)(2,1)S(1)}, u32[]{:S(2)}, u32[]{:S(2)}) collective-permute-start(bf16[16,960]{1,0:T(8,128)(2,1)S(1)} %copy-done.148), channel_id=1, source_target_pairs={{0,4},{2,6},{4,8},{6,10},{8,12},{10,14},{12,16},{14,18},{16,20},{1... | collective-permute-start | bytes 92168
  1910.8 26.7 %collective-permute-start.6 = (bf16[16,960]{1,0:T(8,128)(2,1)S(1)}, bf16[16,960]{1,0:T(8,128)(2,1)S(1)}, u32[]{:S(2)}, u32[]{:S(2)}) collective-permute-start(bf16[16,960]{1,0:T(8,128)(2,1)S(1)} %copy-done.148), channel_id=1, source_target_pairs={{0,6},{2,8},{4,10},{6,12},{8,14},{10,16},{12,18},{14,20},{16,22},{... | collective-permute-start | bytes 92168
  1915.8 34.5 %collective-permute-start.48 = (bf16[16,1280]{1,0:T(8,128)(2,1)S(1)}, bf16[16,1280]{1,0:T(8,128)(2,1)S(1)}, u32[]{:S(2)}, u32[]{:S(2)}) collective-permute-start(bf16[16,1280]{1,0:T(8,128)(2,1)S(1)} %copy-done.135), channel_id=1, source_target_pairs={{0,2},{2,4},{4,6},{6,8},{8,10},{10,12},{12,14},{14,16},{16,18},{18... | collective-permute-start | bytes 122888
  1928.8 25.2 %collective-permute-start.49 = (bf16[16,1280]{1,0:T(8,128)(2,1)S(1)}, bf16[16,1280]{1,0:T(8,128)(2,1)S(1)}, u32[]{:S(2)}, u32[]{:S(2)}) collective-permute-start(bf16[16,1280]{1,0:T(8,128)(2,1)S(1)} %copy-done.135), channel_id=1, source_target_pairs={{0,4},{2,6},{4,8},{6,10},{8,12},{10,14},{12,16},{14,18},{16,20},{1... | collective-permute-start | bytes 122888
  1931.4 25.3 %collective-permute-start.50 = (bf16[16,1280]{1,0:T(8,128)(2,1)S(1)}, bf16[16,1280]{1,0:T(8,128)(2,1)S(1)}, u32[]{:S(2)}, u32[]{:S(2)}) collective-permute-start(bf16[16,1280]{1,0:T(8,128)(2,1)S(1)} %copy-done.135), channel_id=1, source_target_pairs={{0,6},{2,8},{4,10},{6,12},{8,14},{10,16},{12,18},{14,20},{16,22},{... | collective-permute-start | bytes 122888
  1937.5 26.5 %collective-permute-start.52 = (bf16[16,1280]{1,0:T(8,128)(2,1)S(1)}, bf16[16,1280]{1,0:T(8,128)(2,1)S(1)}, u32[]{:S(2)}, u32[]{:S(2)}) collective-permute-start(bf16[16,1280]{1,0:T(8,128)(2,1)S(1)} %copy-done.134), channel_id=1, source_target_pairs={{0,2},{2,4},{4,6},{6,8},{8,10},{10,12},{12,14},{14,16},{16,18},{18... | collective-permute-start | bytes 122888
  1947.8 18.4 collective-permute-start.53
  1950.3 18.9 collective-permute-start.54
  1956.8 18.4 collective-permute-start.40
  1960.8 18.4 collective-permute-start.41
  1969.2 18.8 collective-permute-start.44
  1972.9 18.5 collective-permute-start.45
  1981.1 25.6 %collective-permute-start.32 = (bf16[16,1280]{1,0:T(8,128)(2,1)S(1)}, bf16[16,1280]{1,0:T(8,128)(2,1)S(1)}, u32[]{:S(2)}, u32[]{:S(2)}) collective-permute-start(bf16[16,1280]{1,0:T(8,128)(2,1)S(1)} %convert.530), channel_id=1, source_target_pairs={{0,2},{2,4},{4,6},{6,8},{8,10},{10,12},{12,14},{14,16},{16,18},{18... | collective-permute-start | bytes 122888
  1985.2 25.7 %collective-permute-start.33 = (bf16[16,1280]{1,0:T(8,128)(2,1)S(1)}, bf16[16,1280]{1,0:T(8,128)(2,1)S(1)}, u32[]{:S(2)}, u32[]{:S(2)}) collective-permute-start(bf16[16,1280]{1,0:T(8,128)(2,1)S(1)} %convert.530), channel_id=1, source_target_pairs={{0,4},{2,6},{4,8},{6,10},{8,12},{10,14},{12,16},{14,18},{16,20},{1... | collective-permute-start | bytes 122888
  1988.0 24.6 %collective-permute-start.34 = (bf16[16,1280]{1,0:T(8,128)(2,1)S(1)}, bf16[16,1280]{1,0:T(8,128)(2,1)S(1)}, u32[]{:S(2)}, u32[]{:S(2)}) collective-permute-start(bf16[16,1280]{1,0:T(8,128)(2,1)S(1)} %convert.530), channel_id=1, source_target_pairs={{0,6},{2,8},{4,10},{6,12},{8,14},{10,16},{12,18},{14,20},{16,22},{... | collective-permute-start | bytes 122888
  1993.4 28.7 %collective-permute-start.36 = (bf16[16,1280]{1,0:T(8,128)(2,1)S(1)}, bf16[16,1280]{1,0:T(8,128)(2,1)S(1)}, u32[]{:S(2)}, u32[]{:S(2)}) collective-permute-start(bf16[16,1280]{1,0:T(8,128)(2,1)S(1)} %convert.531), channel_id=1, source_target_pairs={{0,2},{2,4},{4,6},{6,8},{8,10},{10,12},{12,14},{14,16},{16,18},{18... | collective-permute-start | bytes 122888
  2003.7 18.4 collective-permute-start.37
  (213 other events, 5696.6 us)
Sparse Core Ops, SparseCore 0:
  10.7 54.4 all-gather.30
  68.0 50.1 all-gather.32
  120.9 55.9 all-gather.34
  178.9 54.4 all-gather.36
  235.9 54.4 all-gather.38
  293.0 62.3 all-gather.48
  357.8 30.6 reduce-scatter.38
  390.8 49.4 all-gather.40
  442.6 49.9 all-gather.42
  494.8 54.4 all-gather.46
  552.3 54.4 all-gather.44
  618.1 19.8 reduce-scatter.42
  640.4 26.5 reduce-scatter.40
  716.8 48.0 reduce-scatter.46
  789.8 20.5 reduce-scatter.44
  857.4 48.0 reduce-scatter.48
  1947.9 38.6 all-reduce.45
where the time goes:
time: 2050 us; the launch traced here: 2040 us
  blocking collectives  1270 us (62%)
  matrix products  219 us (11%)
  waiting for transfers between devices  187 us (9%)
  starting transfers between devices  174 us (8%)
  local copies, waits for them, and re-layouts  115 us (6%)
  other arithmetic  56 us (3%)
  between operations  20.5 us (1%)
    unnamed x4, blocking collectives  917 us
    unnamed x58, starting transfers between devices  173 us
    dot_general x34, matrix products, by_columns(): lax.dot_general(left, right, (((1,), (1,)), ((), ())), preferred_element_...  84.5 us
    all_gather x2, blocking collectives, shards(): lax.all_gather(key_rows, ('ctx', 'tp'), axis=0, tiled=True)  79.3 us
    all_gather x2, blocking collectives, shards(): lax.all_gather(value_rows, ('ctx', 'tp'), axis=0, tiled=True)  73 us
    dot_general x34, matrix products, product(): return jnp.dot(left, right, preferred_element_type=jnp.float32)  70.4 us
    dot_general x34, matrix products, by_rows(): lax.dot_general(left, right, (((0,), (0,)), ((), ())), preferred_element_...  64.5 us
    unnamed x443, local copies, waits for them, and re-layouts  57.8 us
  transfers between devices with their start and end apart: 73, of which 11 were waited for; matrix products, arithmetic and copies ran while one was open for 12% of the time, Pallas kernels for 0%

commit v1 on v0

v1 whole, which is shorter than its diff:
```python
import jax
import jax.numpy as jnp
from jax import lax
from jax.sharding import Mesh, PartitionSpec as P

D = 960
HEADS = 15
KV_HEADS = 5
HEAD = 64
QW = HEADS * HEAD
KVW = KV_HEADS * HEAD

EPSILON = 1e-05
THETA = 100000.0
MASKED = -1e30

Y, X, ZL, CORE, TP = 4, 4, 2, 2, 2
XY = ("y", "x")
PER = D // (Y * X)
PAD = 64
DP = PAD * Y * X
QKV_HALF = (QW + 2 * KVW) // 2
QKV_PAD = 896
OUT_HALF = QW // 2
OUT_PAD = 512
ATT = QKV_PAD + OUT_PAD
BF = jnp.bfloat16
F32 = jnp.float32


def product(left, right):
    return jnp.dot(left, right, preferred_element_type=F32)


def by_rows(left, right):
    return lax.dot_general(left, right, (((0,), (0,)), ((), ())), preferred_element_type=F32)


def by_columns(left, right):
    return lax.dot_general(left, right, (((1,), (1,)), ((), ())), preferred_element_type=F32)


def ring(size, step):
    return [(i, (i + step) % size) for i in range(size)]


def z_ring(step):
    pairs = []
    for low in range(ZL):
        for high in range(TP):
            there = (high * ZL + low + step) % (ZL * TP)
            pairs.append((low * TP + high, (there % ZL) * TP + there // ZL))
    return pairs


def swap(values, axis):
    return lax.ppermute(values, axis, [(0, 1), (1, 0)])


def z_send(values, step):
    return lax.ppermute(values, ("zl", "tp"), z_ring(step))


STEPS = (2, 1, 3)


def gather_group(values):
    mine = jnp.concatenate([values] + [z_send(values, step) for step in STEPS], axis=0)
    return jnp.concatenate([mine, swap(mine, "core")], axis=0)


def scatter_group(terms):
    half = terms.shape[0] // 2
    rows = half // 4
    total = terms[:half].astype(F32) + swap(terms[half:].astype(BF), "core").astype(F32)
    out = total[:rows]
    for at, step in enumerate(STEPS):
        block = total[(at + 1) * rows : (at + 2) * rows].astype(BF)
        out = out + z_send(block, -step).astype(F32)
    return out


def line_gather(values, axis):
    at = lax.axis_index(axis)
    out = jnp.zeros((4,) + values.shape, values.dtype)
    out = lax.dynamic_update_index_in_dim(out, values, at, 0)
    for step in STEPS:
        got = lax.ppermute(values, axis, ring(4, step))
        out = lax.dynamic_update_index_in_dim(out, got, (at - step) % 4, 0)
    return out


def plane_gather(values, cut):
    first = line_gather(line_gather(values[:, :cut], "x"), "y")
    second = line_gather(line_gather(values[:, cut:], "y"), "x")
    first = first.reshape(DP, -1)
    second = jnp.swapaxes(second, 0, 1).reshape(DP, -1)
    return first, second


def line_scatter(values, axis):
    at = lax.axis_index(axis)
    out = lax.dynamic_index_in_dim(values, at, 0, False).astype(F32)
    for step in STEPS:
        block = lax.dynamic_index_in_dim(values, (at + step) % 4, 0, False)
        out = out + lax.ppermute(block, axis, ring(4, step)).astype(F32)
    return out


def plane_scatter(values, cut):
    view = values.reshape(Y, X, PAD, values.shape[1])
    first = line_scatter(jnp.swapaxes(view[..., :cut], 0, 1), "x").astype(BF)
    second = line_scatter(view[..., cut:], "y").astype(BF)
    first = line_scatter(first, "y")
    second = line_scatter(second, "x")
    return jnp.concatenate([first, second], axis=1)


def reduce_grads(keep, give, cut, over_tp):
    total = (keep.astype(F32) + swap(give.astype(BF), "core").astype(F32)).astype(BF)
    total = plane_scatter(total, cut).astype(BF)
    total = total.astype(F32) + swap(total, "zl").astype(F32)
    total = total.astype(BF)
    return total


def finish(total, tp_width):
    part = total[:, :tp_width]
    part = (part.astype(F32) + swap(part, "tp").astype(F32)).astype(BF)
    if tp_width < total.shape[1]:
        part = jnp.concatenate([part, total[:, tp_width:]], axis=1)
    return part, swap(part, "core")


def rope_tables(positions):
    half_head = HEAD // 2
    freqs = THETA ** (-2.0 * jnp.arange(half_head, dtype=F32) / HEAD)
    angles = positions.astype(F32)[:, None] * freqs[None, :]
    return (jnp.cos(angles), jnp.sin(angles))


def rotate(values, cosine, sine, direction):
    row_count = values.shape[0]
    split_view = values.reshape(row_count, -1, 2, HEAD // 2)
    first_half = split_view[:, :, 0]
    second_half = split_view[:, :, 1]
    cos_rows = cosine[:, None, :]
    sin_rows = direction * sine[:, None, :]
    turned = jnp.stack(
        [
            first_half * cos_rows - second_half * sin_rows,
            second_half * cos_rows + first_half * sin_rows,
        ],
        axis=2,
    )
    return turned.reshape(row_count, -1)


def rms_forward(values, gain):
    mean = jnp.sum(values * values, axis=-1, keepdims=True) * (1.0 / D)
    scale = lax.rsqrt(mean + EPSILON)
    return (values * scale * gain, scale)


def rms_backward(values, scale, gain, grad_normed):
    weighted = grad_normed * gain
    mean = jnp.sum(weighted * values, axis=-1, keepdims=True) * (1.0 / D)
    grad_values = scale * weighted - values * (scale * scale * scale) * mean
    gain_terms = (grad_normed * values * scale).astype(BF)
    ones = jnp.ones((values.shape[0], OUT_PAD - OUT_HALF), BF)
    return (grad_values, by_rows(gain_terms, ones))


def head_rows(matrix, group, row_count):
    view = matrix.reshape(row_count, KV_HEADS, HEADS // KV_HEADS, HEAD)[:, group]
    return jnp.transpose(view, (1, 0, 2)).reshape(-1, HEAD)


def head_back(block, row_count):
    return jnp.transpose(block.reshape(HEADS // KV_HEADS, row_count, HEAD), (1, 0, 2)).reshape(
        row_count, -1
    )


def masked_scores(query_block, key_block, visible):
    raw = by_columns(query_block, key_block) * HEAD ** (-0.5)
    shaped = raw.reshape(HEADS // KV_HEADS, visible.shape[0], -1)
    return jnp.where(visible[None], shaped, MASKED).reshape(raw.shape)


def attention(query, key_all, value_all, visible):
    row_count = query.shape[0]
    parts = []
    log_totals = []
    for group in range(KV_HEADS):
        query_block = head_rows(query, group, row_count)
        key_block = key_all[:, group * HEAD : (group + 1) * HEAD]
        value_block = value_all[:, group * HEAD : (group + 1) * HEAD]
        scores = masked_scores(query_block, key_block, visible)
        top = jnp.max(scores, axis=-1, keepdims=True)
        log_total = top + jnp.log(jnp.sum(jnp.exp(scores - top), axis=-1, keepdims=True))
        probs = jnp.exp(scores - log_total).astype(BF)
        parts.append(head_back(product(probs, value_block), row_count))
        log_totals.append(log_total)
    return jnp.concatenate(parts, axis=1).astype(BF), log_totals


def attention_back(query, key_all, value_all, visible, log_totals, grad_attended_b):
    row_count = query.shape[0]
    query_parts, key_parts, value_parts = [], [], []
    for group in range(KV_HEADS):
        query_block = head_rows(query, group, row_count)
        grad_block = head_rows(grad_attended_b, group, row_count)
        key_block = key_all[:, group * HEAD : (group + 1) * HEAD]
        value_block = value_all[:, group * HEAD : (group + 1) * HEAD]
        scores = masked_scores(query_block, key_block, visible)
        probs_exact = jnp.exp(scores - log_totals[group])
        probs = probs_exact.astype(BF)
        grad_probs = by_columns(grad_block, value_block)
        delta = jnp.sum(probs_exact * grad_probs, axis=-1, keepdims=True)
        grad_scores = (probs_exact * (grad_probs - delta) * HEAD ** (-0.5)).astype(BF)
        query_parts.append(head_back(product(grad_scores, key_block), row_count))
        key_parts.append(by_rows(grad_scores, query_block))
        value_parts.append(by_rows(probs, grad_block))
    return (
        jnp.concatenate(query_parts, axis=1),
        jnp.concatenate(key_parts + value_parts, axis=1).astype(BF),
    )


def pad_features(values):
    rows = values.shape[0]
    view = values.reshape(rows, Y * X, PER)
    return jnp.pad(view, ((0, 0), (0, 0), (0, PAD - PER))).reshape(rows, DP)


def cut_features(values):
    rows = values.shape[0]
    return values.reshape(rows, Y * X, PAD)[:, :, :PER].reshape(rows, D)


def shards(
    tokens,
    segment_ids,
    positions,
    cotangent,
    attn_gain,
    w_query,
    w_key,
    w_value,
    w_out,
    ffn_gain,
    w_gate,
    w_up,
    w_down,
):
    layers = attn_gain.shape[0]
    rows = tokens.shape[0]
    hid = w_gate.shape[2] // 2
    first_core = lax.axis_index("core") == 0

    def pick(low, high):
        return jnp.where(first_core, low, high), jnp.where(first_core, high, low)

    def halves(whole, width):
        return pick(whole[..., :width], whole[..., width:])

    def join(mine, other):
        low, high = pick(mine, other)
        return jnp.concatenate([low, high], axis=-1)

    def tall(values):
        return jnp.pad(values, ((0, PAD - PER), (0, 0)))

    gain_columns = jnp.stack(
        [attn_gain[layer] for layer in range(layers)] + [ffn_gain[layer] for layer in range(layers)],
        axis=1,
    )
    gain_columns = jnp.pad(gain_columns, ((0, 0), (0, OUT_PAD - OUT_HALF - 2 * layers)))
    packs = []
    for layer in range(layers):
        qkv = jnp.concatenate([w_query[layer], w_key[layer], w_value[layer]], axis=1)
        qkv_mine = jnp.pad(halves(qkv, QKV_HALF)[0], ((0, 0), (0, QKV_PAD - QKV_HALF)))
        out_mine = halves(w_out[layer], OUT_HALF)[0]
        packs.append(jnp.concatenate([qkv_mine, out_mine, gain_columns], axis=1))
        packs.append(
            jnp.concatenate(
                [halves(w[layer], hid)[0] for w in (w_gate, w_up, w_down)], axis=1
            )
        )
    packs = [tall(pack) for pack in packs]
    cut = 768
    early = plane_gather(packs[0], cut)
    early_other = tuple(swap(part, "core") for part in early)
    rest = lax.all_gather(jnp.concatenate(packs[1:], axis=1), XY, axis=0, tiled=True)
    rest_other = swap(rest, "core")

    def early_weights(parts):
        left, right = parts
        out = right[:, QKV_PAD - cut :]
        return jnp.concatenate([left, right[:, : QKV_PAD - cut]], axis=1), out

    def att_weights(whole, base):
        return whole[:, base : base + QKV_PAD], whole[:, base + QKV_PAD : base + ATT]

    def ffn_weights(whole, base):
        return whole[:, base : base + 2 * hid], whole[:, base + 2 * hid : base + 3 * hid]

    att_mine = [early_weights(early), att_weights(rest, 3 * hid)]
    att_other = [early_weights(early_other), att_weights(rest_other, 3 * hid)]
    ffn_mine = [ffn_weights(rest, 0), ffn_weights(rest, 3 * hid + ATT)]
    ffn_other = [ffn_weights(rest_other, 0), ffn_weights(rest_other, 3 * hid + ATT)]

    chooser = jnp.eye(8, OUT_PAD - OUT_HALF, dtype=BF)
    gains = by_columns(chooser, att_mine[0][1][:, OUT_HALF:])
    gain_ones = [gains[layer : layer + 1] for layer in range(layers)]
    gain_twos = [gains[layers + layer : layers + layer + 1] for layer in range(layers)]

    cosine, sine = rope_tables(positions)
    stamps = gather_group(jnp.stack([segment_ids, positions], axis=1))
    segment_all, position_all = stamps[:, 0], stamps[:, 1]
    visible = (segment_ids[:, None] == segment_all[None, :]) & (
        position_all[None, :] <= positions[:, None]
    )
    stream = pad_features(tokens)
    saved = []
    for layer in range(layers):
        qkv_m, out_m = att_mine[layer]
        qkv_o, out_o = att_other[layer]
        gu_m, down_m = ffn_mine[layer]
        gu_o, down_o = ffn_other[layer]
        normed_one, scale_one = rms_forward(stream, gain_ones[layer])
        normed_one = normed_one.astype(BF)
        qkv = join(
            product(normed_one, qkv_m)[:, :QKV_HALF], product(normed_one, qkv_o)[:, :QKV_HALF]
        )
        turned = rotate(qkv[:, : QW + KVW], cosine, sine, 1.0).astype(BF)
        query = turned[:, :QW]
        key_value = jnp.concatenate([turned[:, QW:], qkv[:, QW + KVW :].astype(BF)], axis=1)
        key_value = gather_group(key_value)
        key_all, value_all = key_value[:, :KVW], key_value[:, KVW:]
        attended, log_totals = attention(query, key_all, value_all, visible)
        att_m, att_o = halves(attended, OUT_HALF)
        mixed = (
            stream
            + by_columns(att_m, out_m[:, :OUT_HALF])
            + by_columns(att_o, out_o[:, :OUT_HALF])
        )
        normed_two, scale_two = rms_forward(mixed, gain_twos[layer])
        normed_two = normed_two.astype(BF)
        normed_pair = jnp.concatenate([normed_two, swap(normed_two, "tp")], axis=0)
        hiddens = []
        kept = []
        for weight in (gu_m, gu_o):
            both = product(normed_pair, weight)
            gate, up_value = both[:, :hid], both[:, hid:]
            sigma = jax.nn.sigmoid(gate)
            hidden = (gate * sigma * up_value).astype(BF)
            hiddens.append(hidden)
            kept.append((gate, up_value, hidden))
        partial = by_columns(hiddens[0], down_m) + by_columns(hiddens[1], down_o)
        saved.append(
            (
                stream,
                scale_one,
                normed_one,
                query,
                key_all,
                value_all,
                log_totals,
                att_m,
                att_o,
                mixed,
                scale_two,
                normed_pair,
                kept,
            )
        )
        stream = mixed + partial[:rows] + swap(partial[rows:].astype(BF), "tp").astype(F32)
    block_out = cut_features(stream)

    grad_stream = pad_features(cotangent)
    results = [None] * layers
    for layer in reversed(range(layers)):
        qkv_m, out_m = att_mine[layer]
        qkv_o, out_o = att_other[layer]
        gu_m, down_m = ffn_mine[layer]
        gu_o, down_o = ffn_other[layer]
        (
            layer_input,
            scale_one,
            normed_one,
            query,
            key_all,
            value_all,
            log_totals,
            att_m,
            att_o,
            mixed,
            scale_two,
            normed_pair,
            kept,
        ) = saved[layer]
        grad_out_b = grad_stream.astype(BF)
        grad_pair = jnp.concatenate([grad_out_b, swap(grad_out_b, "tp")], axis=0)
        partial = 0.0
        ffn_grads = []
        for (gate, up_value, hidden), gu, down in (
            (kept[0], gu_m, down_m),
            (kept[1], gu_o, down_o),
        ):
            grad_hidden = product(grad_pair, down)
            sigma = jax.nn.sigmoid(gate)
            grad_up_in = (grad_hidden * gate * sigma).astype(BF)
            grad_gate_in = (
                grad_hidden * up_value * sigma * (1.0 + gate * (1.0 - sigma))
            ).astype(BF)
            grad_gu = jnp.concatenate([grad_gate_in, grad_up_in], axis=1)
            partial = partial + by_columns(grad_gu, gu)
            ffn_grads.append(
                jnp.concatenate(
                    [
                        by_rows(normed_pair, grad_gu).astype(BF),
                        by_rows(grad_pair, hidden).astype(BF),
                    ],
                    axis=1,
                )
            )
        grad_normed_two = partial[:rows] + swap(partial[rows:].astype(BF), "tp").astype(F32)
        grad_mixed_norm, gain_two_column = rms_backward(
            mixed, scale_two, gain_twos[layer], grad_normed_two
        )
        grad_mixed = grad_stream + grad_mixed_norm
        grad_mixed_b = grad_mixed.astype(BF)
        grad_attended_b = join(
            product(grad_mixed_b, out_m)[:, :OUT_HALF], product(grad_mixed_b, out_o)[:, :OUT_HALF]
        ).astype(BF)
        out_grads = [
            jnp.concatenate(
                [by_rows(grad_mixed_b, att), gain_two_column * weight], axis=1
            ).astype(BF)
            for att, weight in ((att_m, 1.0), (att_o, 1.0))
        ]
        grad_query, key_value_terms = attention_back(
            query, key_all, value_all, visible, log_totals, grad_attended_b
        )
        key_value_grad = scatter_group(key_value_terms)
        grad_qkv = jnp.concatenate(
            [
                rotate(
                    jnp.concatenate([grad_query, key_value_grad[:, :KVW]], axis=1),
                    cosine,
                    sine,
                    -1.0,
                ),
                key_value_grad[:, KVW:],
            ],
            axis=1,
        ).astype(BF)
        grad_m, grad_o = halves(grad_qkv, QKV_HALF)
        wide = ((0, 0), (0, QKV_PAD - QKV_HALF))
        grad_m, grad_o = jnp.pad(grad_m, wide), jnp.pad(grad_o, wide)
        grad_normed_one = by_columns(grad_m, qkv_m) + by_columns(grad_o, qkv_o)
        grad_input_norm, gain_one_column = rms_backward(
            layer_input, scale_one, gain_ones[layer], grad_normed_one
        )
        grad_stream = grad_mixed + grad_input_norm
        qkv_grads = [
            jnp.concatenate(
                [
                    by_rows(normed_one, part[:, :QKV_HALF]),
                    gain_one_column,
                    jnp.zeros((DP, QKV_PAD - QKV_HALF - OUT_PAD + OUT_HALF), F32),
                ],
                axis=1,
            ).astype(BF)
            for part in (grad_m, grad_o)
        ]
        one = reduce_grads(
            jnp.concatenate([out_grads[0], ffn_grads[0]], axis=1),
            jnp.concatenate([out_grads[1], ffn_grads[1]], axis=1),
            1152,
            OUT_PAD,
        )
        two = reduce_grads(qkv_grads[0], qkv_grads[1], 512, QKV_PAD)
        results[layer] = (finish(one, OUT_PAD), finish(two, QKV_PAD))

    stacked = [[] for _ in range(9)]
    for layer in range(layers):
        (one_m, one_o), (two_m, two_o) = results[layer]
        qkv = join(two_m[:PER, :QKV_HALF], two_o[:PER, :QKV_HALF]).astype(F32)
        out = join(one_m[:PER, :OUT_HALF], one_o[:PER, :OUT_HALF]).astype(F32)
        gain_one = jnp.where(first_core, two_m[:PER, QKV_HALF], two_o[:PER, QKV_HALF])
        gain_two = jnp.where(first_core, one_m[:PER, OUT_HALF], one_o[:PER, OUT_HALF])
        ffn = [
            join(
                one_m[:PER, OUT_PAD + at * hid : OUT_PAD + (at + 1) * hid],
                one_o[:PER, OUT_PAD + at * hid : OUT_PAD + (at + 1) * hid],
            ).astype(F32)
            for at in range(3)
        ]
        for at, value in enumerate(
            [
                gain_one.astype(F32),
                qkv[:, :QW],
                qkv[:, QW : QW + KVW],
                qkv[:, QW + KVW :],
                out,
                gain_two.astype(F32),
            ]
            + ffn
        ):
            stacked[at].append(value)
    return (block_out, cut_features(grad_stream)) + tuple(jnp.stack(part) for part in stacked)


def solution(mesh):
    fine = Mesh(mesh.devices.reshape(Y, X, ZL, CORE, TP), ("y", "x", "zl", "core", "tp"))
    every = ("y", "x", "zl", "core", "tp")
    return jax.shard_map(
        shards,
        mesh=fine,
        in_specs=(
            P(every, None),
            P(every),
            P(every),
            P(every, None),
            P(None, XY),
            P(None, XY, None),
            P(None, XY, None),
            P(None, XY, None),
            P(None, XY, None),
            P(None, XY),
            P(None, XY, "tp"),
            P(None, XY, "tp"),
            P(None, XY, "tp"),
        ),
        out_specs=(
            P(every, None),
            P(every, None),
            P(None, XY),
            P(None, XY, None),
            P(None, XY, None),
            P(None, XY, None),
            P(None, XY, None),
            P(None, XY),
            P(None, XY, "tp"),
            P(None, XY, "tp"),
            P(None, XY, "tp"),
        ),
        check_vma=False,
    )
```

time: 2050 us -> 916 us (0.45)
  blocking collectives: 1270 us -> 0 us
  local copies, waits for them, and re-layouts: 115 us -> 228 us
    unnamed x4 -> x0, blocking collectives: 917 us -> none
    all_gather x21 -> x0, blocking collectives: 350 us -> none  [the longest x2 79.3 us: shards(): lax.all_gather(key_rows, ('ctx', 'tp'), axis=0, tiled=True)]
    ppermute x0 -> x107, waiting for transfers between devices: none -> 199 us  [the longest x48 84.5 us: line_scatter(): out = out + lax.ppermute(block, axis, ring(4, step)).astype(F32)]
    ppermute x0 -> x107, starting transfers between devices: none -> 182 us  [the longest x32 86.4 us: swap(): return lax.ppermute(values, axis, [(0, 1), (1, 0)])]
    unnamed x58 -> x0, starting transfers between devices: 173 us -> none
    all_gather x10 -> x1, waiting for transfers between devices: 82.8 us -> 0.02 us  [shards(): lax.all_gather(jnp.concatenate(packs[1:], axis=1), XY, axis=0, tiled=True)]
    unnamed x75 -> x1, waiting for transfers between devices: 56.2 us -> 0.02 us
    reduce_scatter x4 -> x0, waiting for transfers between devices: 48.2 us -> none  [the longest x2 41.6 us: shards(): lax.psum_scatter(by_columns(hidden, down_weight), 'tp', scatter_dimension...]
  transfers between devices with their start and end apart: 73 -> 108, of which waited for: 11 -> 50; matrix products, arithmetic and copies ran while one was open for 12% -> 32% of each run, Pallas kernels for 0% -> 0%
where the time goes in v1:
time: 916 us; the launch traced here: 903 us
  local copies, waits for them, and re-layouts  228 us (25%)
  matrix products  210 us (23%)
  waiting for transfers between devices  199 us (22%)
  starting transfers between devices  182 us (20%)
  other arithmetic  65.4 us (7%)
  between operations  18.7 us (2%)
    ppermute x32, starting transfers between devices, swap(): return lax.ppermute(values, axis, [(0, 1), (1, 0)])  86.4 us
    ppermute x48, waiting for transfers between devices, line_scatter(): out = out + lax.ppermute(block, axis, ring(4, step)).astype(F32)  84.5 us
    dot_general x37, matrix products, by_columns(): lax.dot_general(left, right, (((1,), (1,)), ((), ())), preferred_element_...  80 us
    dot_general x36, matrix products, product(): return jnp.dot(left, right, preferred_element_type=F32)  70.9 us
    dot_general x40, matrix products, by_rows(): lax.dot_general(left, right, (((0,), (0,)), ((), ())), preferred_element_...  59 us
    ppermute x48, starting transfers between devices, line_scatter(): out = out + lax.ppermute(block, axis, ring(4, step)).astype(F32)  54.9 us
    unnamed x488, local copies, waits for them, and re-layouts  51 us
    ppermute x15, waiting for transfers between devices, z_send(): return lax.ppermute(values, ('zl', 'tp'), z_ring(step))  43.8 us
  transfers between devices with their start and end apart: 108, of which 50 were waited for; matrix products, arithmetic and copies ran while one was open for 32% of the time, Pallas kernels for 0%

profile of v1, /device:TPU:1, one launch (start us, length us, event | category | flops | bytes accessed | tf_op | source)
XLA Modules:
  0.0 902.5 jit_solution(1619883002082834856)
XLA Ops:
  15.2 4.5 collective-permute-start
  34.7 3.6 collective-permute-done.10
  47.7 5.5 collective-permute-done.7
  64.2 13.5 %collective-permute-done.14 = bf16[4,64,768]{2,1,0:T(8,128)(2,1)S(1)} collective-permute-done((bf16[4,64,768]{2,1,0:T(8,128)(2,1)S(1)}, bf16[4,64,768]{2,1,0:T(8,128)(2,1)S(1)}, u32[]{:S(2)}, u32[]{:S(2)}) %collective-permute-start.14) | collective-permute-done | bytes 393248 | tf_op jit(solution)/shard_map/ppermute | solution.py:88
  79.4 10.1 %collective-permute-start.16 = (bf16[1024,768]{1,0:T(8,128)(2,1)}, bf16[1024,768]{1,0:T(8,128)(2,1)}, u32[]{:S(2)}, u32[]{:S(2)}) collective-permute-start(bf16[1024,768]{1,0:T(8,128)(2,1)} %bitcast.33), channel_id=1, source_target_pairs={{0,2},{2,0},{1,3},{3,1},{4,6},{6,4},{5,7},{7,5},{8,10},{10,8},{9,1... | collective-permute-start | bytes 4718600 | tf_op jit(solution)/shard_map/ppermute | solution.py:57
  92.1 8.3 collective-permute-start.17
  121.7 4.7 collective-permute-done.19
  162.3 9.2 %collective-permute-done.22 = bf16[160,1024]{1,0:T(8,128)(2,1)S(1)} collective-permute-done((bf16[160,1024]{1,0:T(8,128)(2,1)S(1)}, bf16[160,1024]{1,0:T(8,128)(2,1)S(1)}, u32[]{:S(2)}, u32[]{:S(2)}) %collective-permute-start.22) | collective-permute-done | bytes 327712 | tf_op jit(solution)/shard_map/ppermute | solution.py:57
  185.0 8.3 collective-permute-done.24
  215.8 5.7 collective-permute-done.26
  295.7 3.2 reshape.1093
  334.5 4.1 convolution_convert_fusion
  341.8 4.2 convolution_convert_fusion.1
  346.0 3.2 convolution_convert_fusion.29
  451.1 8.1 concatenate.365
  464.3 8.1 concatenate.364
  480.9 6.4 collective-permute-done.36
  487.3 7.1 collective-permute-done.34
  512.2 5.6 collective-permute-done.37
  573.2 4.1 multiply_reduce_fusion.1
  605.7 7.1 collective-permute-done.42
  612.7 7.4 collective-permute-done.40
  628.8 4.0 fusion.67
  643.0 8.0 concatenate.358
  651.0 8.1 concatenate.357
  662.8 6.0 add_convert_fusion.3
  692.0 3.3 collective-permute-done.51
  705.3 8.2 collective-permute-done.53
  713.4 4.9 collective-permute-start.75
  721.4 4.9 collective-permute-done.46
  728.0 5.0 collective-permute-done.44
  743.3 3.3 collective-permute-start.73
  746.7 4.8 collective-permute-start.57
  751.5 3.9 add_convert_fusion
  757.9 6.2 collective-permute-start.74
  770.6 12.7 %collective-permute-done.92 = bf16[4,64,1152]{2,1,0:T(8,128)(2,1)S(1)} collective-permute-done((bf16[4,64,1152]{2,1,0:T(8,128)(2,1)S(1)}, bf16[4,64,1152]{2,1,0:T(8,128)(2,1)S(1)}, u32[]{:S(2)}, u32[]{:S(2)}) %collective-permute-start.92) | collective-permute-done | bytes 589856 | tf_op jit(solution)/shard_map/ppermute | solution.py:106
  786.2 8.6 collective-permute-done.98
  795.2 3.3 collective-permute-start.103
  798.7 8.1 collective-permute-start.101
  806.9 3.2 collective-permute-done.101
  812.3 3.7 collective-permute-done.104
  828.2 6.4 collective-permute-done.78
  834.6 12.4 %collective-permute-done.76 = bf16[4,64,1152]{2,1,0:T(8,128)(2,1)S(1)} collective-permute-done((bf16[4,64,1152]{2,1,0:T(8,128)(2,1)S(1)}, bf16[4,64,1152]{2,1,0:T(8,128)(2,1)S(1)}, u32[]{:S(2)}, u32[]{:S(2)}) %collective-permute-start.76) | collective-permute-done | bytes 589856 | tf_op jit(solution)/shard_map/ppermute | solution.py:106
  848.9 3.2 collective-permute-done.82
  857.0 4.2 collective-permute-done.86
  862.6 13.1 %collective-permute-start.106 = (bf16[64,2432]{1,0:T(8,128)(2,1)S(1)}, bf16[64,2432]{1,0:T(8,128)(2,1)S(1)}, u32[]{:S(2)}, u32[]{:S(2)}) collective-permute-start(bf16[64,2432]{1,0:T(8,128)(2,1)S(1)} %pad_maximum_fusion.40), channel_id=1, source_target_pairs={{0,2},{2,0},{1,3},{3,1},{4,6},{6,4},{5,7},{7,5},{8,10},{10,8},{9,1... | collective-permute-start | bytes 933896 | tf_op jit(solution)/shard_map/ppermute | solution.py:57
  877.2 4.0 collective-permute-done.89
  881.3 6.6 collective-permute-start.90
  (1134 shorter events, 581.9 us)
Async XLA Ops:
  7.2 122.2 %all-gather.2.cloned.1.call-start = ((), (), s32[]{:S(2)}) async-start(), calls=%async_computation | async-start | bytes 11419648 | tf_op jit(solution)/shard_map/all_gather | solution.py:295
  15.2 100.4 %collective-permute-start = (s32[160,2]{0,1:T(2,128)S(1)}, s32[160,2]{0,1:T(2,128)S(1)}, u32[]{:S(2)}, u32[]{:S(2)}) collective-permute-start(s32[160,2]{0,1:T(2,128)S(1)} %pad_add_fusion.1), channel_id=1, source_target_pairs={{0,1},{1,0},{4,5},{5,4},{2,3},{3,2},{6,7},{7,6},{8,9},{9,8},{12,13... | collective-permute-start | bytes 3848 | tf_op jit(solution)/shard_map/ppermute | solution.py:61
  19.7 96.9 %collective-permute-start.1 = (s32[160,2]{0,1:T(2,128)S(1)}, s32[160,2]{0,1:T(2,128)S(1)}, u32[]{:S(2)}, u32[]{:S(2)}) collective-permute-start(s32[160,2]{0,1:T(2,128)S(1)} %pad_add_fusion.1), channel_id=1, source_target_pairs={{0,4},{1,5},{4,1},{5,0},{2,6},{3,7},{6,3},{7,2},{8,12},{9,13},{12,... | collective-permute-start | bytes 3848 | tf_op jit(solution)/shard_map/ppermute | solution.py:61
  20.5 96.1 %collective-permute-start.2 = (s32[160,2]{0,1:T(2,128)S(1)}, s32[160,2]{0,1:T(2,128)S(1)}, u32[]{:S(2)}, u32[]{:S(2)}) collective-permute-start(s32[160,2]{0,1:T(2,128)S(1)} %pad_add_fusion.1), channel_id=1, source_target_pairs={{0,5},{1,4},{4,0},{5,1},{2,7},{3,6},{6,2},{7,3},{8,13},{9,12},{12,... | collective-permute-start | bytes 3848 | tf_op jit(solution)/shard_map/ppermute | solution.py:61
  44.3 13.8 %collective-permute-start.8 = (bf16[4,64,640]{2,1,0:T(8,128)(2,1)S(1)}, bf16[4,64,640]{2,1,0:T(8,128)(2,1)S(1)}, u32[]{:S(2)}, u32[]{:S(2)}) collective-permute-start(bf16[4,64,640]{2,1,0:T(8,128)(2,1)S(1)} %bitcast_dynamic-update-slice_fusion.12), channel_id=1, source_target_pairs={{0,8},{8,16},{16,24},{24,0},{1,9},{9,17},{17,25},{25,1},{2,10},{10... | collective-permute-start | bytes 983048 | tf_op jit(solution)/shard_map/ppermute | solution.py:88
  58.1 19.7 %collective-permute-start.14 = (bf16[4,64,768]{2,1,0:T(8,128)(2,1)S(1)}, bf16[4,64,768]{2,1,0:T(8,128)(2,1)S(1)}, u32[]{:S(2)}, u32[]{:S(2)}) collective-permute-start(bf16[4,64,768]{2,1,0:T(8,128)(2,1)S(1)} %bitcast_dynamic-update-slice_fusion.8), channel_id=1, source_target_pairs={{0,32},{32,64},{64,96},{96,0},{1,33},{33,65},{65,97},{97,1},{2,34}... | collective-permute-start | bytes 1179656 | tf_op jit(solution)/shard_map/ppermute | solution.py:88
  61.4 17.2 %collective-permute-start.15 = (bf16[4,64,768]{2,1,0:T(8,128)(2,1)S(1)}, bf16[4,64,768]{2,1,0:T(8,128)(2,1)S(1)}, u32[]{:S(2)}, u32[]{:S(2)}) collective-permute-start(bf16[4,64,768]{2,1,0:T(8,128)(2,1)S(1)} %bitcast_dynamic-update-slice_fusion.8), channel_id=1, source_target_pairs={{0,96},{32,0},{64,32},{96,64},{1,97},{33,1},{65,33},{97,65},{2,98}... | collective-permute-start | bytes 1179656 | tf_op jit(solution)/shard_map/ppermute | solution.py:88
  77.7 14.3 %collective-permute-start.9 = (bf16[4,64,640]{2,1,0:T(8,128)(2,1)S(1)}, bf16[4,64,640]{2,1,0:T(8,128)(2,1)S(1)}, u32[]{:S(2)}, u32[]{:S(2)}) collective-permute-start(bf16[4,64,640]{2,1,0:T(8,128)(2,1)S(1)} %bitcast_dynamic-update-slice_fusion.12), channel_id=1, source_target_pairs={{0,24},{8,0},{16,8},{24,16},{1,25},{9,1},{17,9},{25,17},{2,26},{10... | collective-permute-start | bytes 983048 | tf_op jit(solution)/shard_map/ppermute | solution.py:88
  79.4 28.2 %collective-permute-start.16 = (bf16[1024,768]{1,0:T(8,128)(2,1)}, bf16[1024,768]{1,0:T(8,128)(2,1)}, u32[]{:S(2)}, u32[]{:S(2)}) collective-permute-start(bf16[1024,768]{1,0:T(8,128)(2,1)} %bitcast.33), channel_id=1, source_target_pairs={{0,2},{2,0},{1,3},{3,1},{4,6},{6,4},{5,7},{7,5},{8,10},{10,8},{9,1... | collective-permute-start | bytes 4718600 | tf_op jit(solution)/shard_map/ppermute | solution.py:57
  92.1 14.4 %collective-permute-start.17 = (bf16[1024,640]{1,0:T(8,128)(2,1)S(1)}, bf16[1024,640]{1,0:T(8,128)(2,1)}, u32[]{:S(2)}, u32[]{:S(2)}) collective-permute-start(bf16[1024,640]{1,0:T(8,128)(2,1)S(1)} %bitcast.687), channel_id=1, source_target_pairs={{0,2},{2,0},{1,3},{3,1},{4,6},{6,4},{5,7},{7,5},{8,10},{10,8},{9,1... | collective-permute-start | bytes 3932168 | tf_op jit(solution)/shard_map/ppermute | solution.py:57
  113.9 12.5 %collective-permute-start.19 = (bf16[160,640]{1,0:T(8,128)(2,1)S(1)}, bf16[160,640]{1,0:T(8,128)(2,1)S(1)}, u32[]{:S(2)}, u32[]{:S(2)}) collective-permute-start(bf16[160,640]{1,0:T(8,128)(2,1)S(1)} %get-tuple-element.57), channel_id=1, source_target_pairs={{0,4},{1,5},{4,1},{5,0},{2,6},{3,7},{6,3},{7,2},{8,12},{9,13},{12,... | collective-permute-start | bytes 614408 | tf_op jit(solution)/shard_map/ppermute | solution.py:61
  129.4 48.7 %collective-permute-start.23 = (bf16[1024,5248]{1,0:T(8,128)(2,1)}, bf16[1024,5248]{1,0:T(8,128)(2,1)}, u32[]{:S(2)}, u32[]{:S(2)}) collective-permute-start(bf16[1024,5248]{1,0:T(8,128)(2,1)} %all-gather.2.cloned.1.call-done), channel_id=1, source_target_pairs={{0,2},{2,0},{1,3},{3,1},{4,6},{6,4},{5,7},{7,5},{8,10},{10,8},{9,1... | collective-permute-start | bytes 32243720 | tf_op jit(solution)/shard_map/ppermute | solution.py:57
  223.6 22.3 %collective-permute-start.28 = (bf16[640,640]{1,0:T(8,128)(2,1)}, bf16[640,640]{1,0:T(8,128)(2,1)}, u32[]{:S(2)}, u32[]{:S(2)}) collective-permute-start(bf16[640,640]{1,0:T(8,128)(2,1)} %pad_maximum_fusion.13), channel_id=1, source_target_pairs={{0,2},{2,0},{1,3},{3,1},{4,6},{6,4},{5,7},{7,5},{8,10},{10,8},{9,1... | collective-permute-start | bytes 2457608 | tf_op jit(solution)/shard_map/ppermute | solution.py:57
  294.1 14.1 %collective-permute-start.29 = (bf16[160,1024]{1,0:T(8,128)(2,1)}, bf16[160,1024]{1,0:T(8,128)(2,1)}, u32[]{:S(2)}, u32[]{:S(2)}) collective-permute-start(bf16[160,1024]{1,0:T(8,128)(2,1)} %multiply_convert_fusion.26), channel_id=1, source_target_pairs={{0,1},{1,0},{2,3},{3,2},{4,5},{5,4},{6,7},{7,6},{8,9},{9,8},{10,11... | collective-permute-start | bytes 983048 | tf_op jit(solution)/shard_map/ppermute | solution.py:57
  327.1 22.1 %collective-permute-start.32 = (bf16[160,1024]{1,0:T(8,128)(2,1)S(1)}, bf16[160,1024]{1,0:T(8,128)(2,1)S(1)}, u32[]{:S(2)}, u32[]{:S(2)}) collective-permute-start(bf16[160,1024]{1,0:T(8,128)(2,1)S(1)} %slice.1545), channel_id=1, source_target_pairs={{0,1},{1,0},{2,3},{3,2},{4,5},{5,4},{6,7},{7,6},{8,9},{9,8},{10,11... | collective-permute-start | bytes 983048 | tf_op jit(solution)/shard_map/ppermute | solution.py:57
  333.0 16.5 %collective-permute-start.30 = (bf16[160,1024]{1,0:T(8,128)(2,1)S(1)}, bf16[160,1024]{1,0:T(8,128)(2,1)S(1)}, u32[]{:S(2)}, u32[]{:S(2)}) collective-permute-start(bf16[160,1024]{1,0:T(8,128)(2,1)S(1)} %slice.1546), channel_id=1, source_target_pairs={{0,1},{1,0},{2,3},{3,2},{4,5},{5,4},{6,7},{7,6},{8,9},{9,8},{10,11... | collective-permute-start | bytes 983048 | tf_op jit(solution)/shard_map/ppermute | solution.py:57
  444.7 30.5 %collective-permute-start.33 = (bf16[640,640]{0,1:T(8,128)(2,1)}, bf16[640,640]{0,1:T(8,128)(2,1)}, u32[]{:S(2)}, u32[]{:S(2)}) collective-permute-start(bf16[640,640]{0,1:T(8,128)(2,1)} %slice.1089), channel_id=1, source_target_pairs={{0,2},{2,0},{1,3},{3,1},{4,6},{6,4},{5,7},{7,5},{8,10},{10,8},{9,1... | collective-permute-start | bytes 2457608 | tf_op jit(solution)/shard_map/ppermute | solution.py:57
  459.2 292.2 %collective-permute-start.91 = (bf16[1024,2432]{1,0:T(8,128)(2,1)}, bf16[1024,2432]{1,0:T(8,128)(2,1)}, u32[]{:S(2)}, u32[]{:S(2)}) collective-permute-start(bf16[1024,2432]{1,0:T(8,128)(2,1)} %concatenate.365), channel_id=1, source_target_pairs={{0,2},{2,0},{1,3},{3,1},{4,6},{6,4},{5,7},{7,5},{8,10},{10,8},{9,1... | collective-permute-start | bytes 14942216 | tf_op jit(solution)/shard_map/ppermute | solution.py:57
  480.0 14.4 %collective-permute-start.34 = (bf16[160,640]{0,1:T(8,128)(2,1)S(1)}, bf16[160,640]{0,1:T(8,128)(2,1)S(1)}, u32[]{:S(2)}, u32[]{:S(2)}) collective-permute-start(bf16[160,640]{0,1:T(8,128)(2,1)S(1)} %get-tuple-element.107), channel_id=1, source_target_pairs={{0,1},{1,0},{4,5},{5,4},{2,3},{3,2},{6,7},{7,6},{8,9},{9,8},{12,13... | collective-permute-start | bytes 614408 | tf_op jit(solution)/shard_map/ppermute | solution.py:61
  604.9 15.2 %collective-permute-start.40 = (bf16[160,640]{0,1:T(8,128)(2,1)S(1)}, bf16[160,640]{0,1:T(8,128)(2,1)S(1)}, u32[]{:S(2)}, u32[]{:S(2)}) collective-permute-start(bf16[160,640]{0,1:T(8,128)(2,1)S(1)} %get-tuple-element.104), channel_id=1, source_target_pairs={{0,1},{1,0},{4,5},{5,4},{2,3},{3,2},{6,7},{7,6},{8,9},{9,8},{12,13... | collective-permute-start | bytes 614408 | tf_op jit(solution)/shard_map/ppermute | solution.py:61
  632.8 29.9 %collective-permute-start.43 = (bf16[1024,896]{0,1:T(8,128)(2,1)}, bf16[1024,896]{0,1:T(8,128)(2,1)}, u32[]{:S(2)}, u32[]{:S(2)}) collective-permute-start(bf16[1024,896]{0,1:T(8,128)(2,1)} %get-tuple-element.213), channel_id=1, source_target_pairs={{0,2},{2,0},{1,3},{3,1},{4,6},{6,4},{5,7},{7,5},{8,10},{10,8},{9,1... | collective-permute-start | bytes 5505032 | tf_op jit(solution)/shard_map/ppermute | solution.py:57
  634.3 28.5 %collective-permute-start.59 = (bf16[1024,896]{0,1:T(8,128)(2,1)}, bf16[1024,896]{0,1:T(8,128)(2,1)}, u32[]{:S(2)}, u32[]{:S(2)}) collective-permute-start(bf16[1024,896]{0,1:T(8,128)(2,1)} %get-tuple-element.214), channel_id=1, source_target_pairs={{0,2},{2,0},{1,3},{3,1},{4,6},{6,4},{5,7},{7,5},{8,10},{10,8},{9,1... | collective-permute-start | bytes 5505032 | tf_op jit(solution)/shard_map/ppermute | solution.py:57
  683.4 11.8 %collective-permute-start.51 = (bf16[4,64,384]{2,1,0:T(8,128)(2,1)S(1)}, bf16[4,64,384]{2,1,0:T(8,128)(2,1)S(1)}, u32[]{:S(2)}, u32[]{:S(2)}) collective-permute-start(bf16[4,64,384]{2,1,0:T(8,128)(2,1)S(1)} %get-tuple-element.112), channel_id=1, source_target_pairs={{0,32},{32,64},{64,96},{96,0},{1,33},{33,65},{65,97},{97,1},{2,34}... | collective-permute-start | bytes 589832 | tf_op jit(solution)/shard_map/ppermute | solution.py:106
  685.0 11.7 %collective-permute-start.50 = (bf16[4,64,384]{2,1,0:T(8,128)(2,1)S(1)}, bf16[4,64,384]{2,1,0:T(8,128)(2,1)S(1)}, u32[]{:S(2)}, u32[]{:S(2)}) collective-permute-start(bf16[4,64,384]{2,1,0:T(8,128)(2,1)S(1)} %get-tuple-element.110), channel_id=1, source_target_pairs={{0,64},{32,96},{64,0},{96,32},{1,65},{33,97},{65,1},{97,33},{2,66}... | collective-permute-start | bytes 589832 | tf_op jit(solution)/shard_map/ppermute | solution.py:106
  699.5 18.9 %collective-permute-start.62 = (bf16[4,64,512]{2,1,0:T(8,128)(2,1)S(1)}, bf16[4,64,512]{2,1,0:T(8,128)(2,1)S(1)}, u32[]{:S(2)}, u32[]{:S(2)}) collective-permute-start(bf16[4,64,512]{2,1,0:T(8,128)(2,1)S(1)} %get-tuple-element.103), channel_id=1, source_target_pairs={{0,24},{8,0},{16,8},{24,16},{1,25},{9,1},{17,9},{25,17},{2,26},{10... | collective-permute-start | bytes 786440 | tf_op jit(solution)/shard_map/ppermute | solution.py:106
  702.2 16.9 %collective-permute-start.61 = (bf16[4,64,512]{2,1,0:T(8,128)(2,1)S(1)}, bf16[4,64,512]{2,1,0:T(8,128)(2,1)S(1)}, u32[]{:S(2)}, u32[]{:S(2)}) collective-permute-start(bf16[4,64,512]{2,1,0:T(8,128)(2,1)S(1)} %get-tuple-element.102), channel_id=1, source_target_pairs={{0,8},{8,16},{16,24},{24,0},{1,9},{9,17},{17,25},{25,1},{2,10},{10... | collective-permute-start | bytes 786440 | tf_op jit(solution)/shard_map/ppermute | solution.py:106
  702.2 17.7 %collective-permute-start.60 = (bf16[4,64,512]{2,1,0:T(8,128)(2,1)S(1)}, bf16[4,64,512]{2,1,0:T(8,128)(2,1)S(1)}, u32[]{:S(2)}, u32[]{:S(2)}) collective-permute-start(bf16[4,64,512]{2,1,0:T(8,128)(2,1)S(1)} %get-tuple-element.101), channel_id=1, source_target_pairs={{0,16},{8,24},{16,0},{24,8},{1,17},{9,25},{17,1},{25,9},{2,18},{10... | collective-permute-start | bytes 786440 | tf_op jit(solution)/shard_map/ppermute | solution.py:106
  713.4 105.1 %collective-permute-start.75 = (bf16[1024,2432]{1,0:T(8,128)(2,1)}, bf16[1024,2432]{1,0:T(8,128)(2,1)S(1)}, u32[]{:S(2)}, u32[]{:S(2)}) collective-permute-start(bf16[1024,2432]{1,0:T(8,128)(2,1)} %concatenate.358), channel_id=1, source_target_pairs={{0,2},{2,0},{1,3},{3,1},{4,6},{6,4},{5,7},{7,5},{8,10},{10,8},{9,1... | collective-permute-start | bytes 14942216 | tf_op jit(solution)/shard_map/ppermute | solution.py:57
  719.9 13.2 %collective-permute-start.44 = (bf16[4,64,512]{2,1,0:T(8,128)(2,1)S(1)}, bf16[4,64,512]{2,1,0:T(8,128)(2,1)S(1)}, u32[]{:S(2)}, u32[]{:S(2)}) collective-permute-start(bf16[4,64,512]{2,1,0:T(8,128)(2,1)S(1)} %get-tuple-element.98), channel_id=1, source_target_pairs={{0,16},{8,24},{16,0},{24,8},{1,17},{9,25},{17,1},{25,9},{2,18},{10... | collective-permute-start | bytes 786440 | tf_op jit(solution)/shard_map/ppermute | solution.py:106
  743.3 13.0 %collective-permute-start.73 = (bf16[64,896]{1,0:T(8,128)(2,1)S(1)}, bf16[64,896]{1,0:T(8,128)(2,1)S(1)}, u32[]{:S(2)}, u32[]{:S(2)}) collective-permute-start(bf16[64,896]{1,0:T(8,128)(2,1)S(1)} %add_convert_fusion.11), channel_id=1, source_target_pairs={{0,1},{1,0},{2,3},{3,2},{4,5},{5,4},{6,7},{7,6},{8,9},{9,8},{10,11... | collective-permute-start | bytes 344072 | tf_op jit(solution)/shard_map/ppermute | solution.py:57
  756.0 27.8 %collective-permute-start.100 = (bf16[4,64,1280]{2,1,0:T(8,128)(2,1)S(1)}, bf16[4,64,1280]{2,1,0:T(8,128)(2,1)S(1)}, u32[]{:S(2)}, u32[]{:S(2)}) collective-permute-start(bf16[4,64,1280]{2,1,0:T(8,128)(2,1)S(1)} %get-tuple-element.62), channel_id=1, source_target_pairs={{0,96},{32,0},{64,32},{96,64},{1,97},{33,1},{65,33},{97,65},{2,98}... | collective-permute-start | bytes 1966088 | tf_op jit(solution)/shard_map/ppermute | solution.py:106
  756.3 12.4 %collective-permute-start.94 = (bf16[4,64,1152]{2,1,0:T(8,128)(2,1)S(1)}, bf16[4,64,1152]{2,1,0:T(8,128)(2,1)S(1)}, u32[]{:S(2)}, u32[]{:S(2)}) collective-permute-start(bf16[4,64,1152]{2,1,0:T(8,128)(2,1)S(1)} %get-tuple-element.80), channel_id=1, source_target_pairs={{0,24},{8,0},{16,8},{24,16},{1,25},{9,1},{17,9},{25,17},{2,26},{10... | collective-permute-start | bytes 1769480 | tf_op jit(solution)/shard_map/ppermute | solution.py:106
  756.4 14.1 %collective-permute-start.93 = (bf16[4,64,1152]{2,1,0:T(8,128)(2,1)S(1)}, bf16[4,64,1152]{2,1,0:T(8,128)(2,1)S(1)}, u32[]{:S(2)}, u32[]{:S(2)}) collective-permute-start(bf16[4,64,1152]{2,1,0:T(8,128)(2,1)S(1)} %get-tuple-element.81), channel_id=1, source_target_pairs={{0,8},{8,16},{16,24},{24,0},{1,9},{9,17},{17,25},{25,1},{2,10},{10... | collective-permute-start | bytes 1769480 | tf_op jit(solution)/shard_map/ppermute | solution.py:106
  766.3 17.0 %collective-permute-start.92 = (bf16[4,64,1152]{2,1,0:T(8,128)(2,1)S(1)}, bf16[4,64,1152]{2,1,0:T(8,128)(2,1)S(1)}, u32[]{:S(2)}, u32[]{:S(2)}) collective-permute-start(bf16[4,64,1152]{2,1,0:T(8,128)(2,1)S(1)} %get-tuple-element.79), channel_id=1, source_target_pairs={{0,16},{8,24},{16,0},{24,8},{1,17},{9,25},{17,1},{25,9},{2,18},{10... | collective-permute-start | bytes 1769480 | tf_op jit(solution)/shard_map/ppermute | solution.py:106
  768.7 16.4 %collective-permute-start.99 = (bf16[4,64,1280]{2,1,0:T(8,128)(2,1)S(1)}, bf16[4,64,1280]{2,1,0:T(8,128)(2,1)S(1)}, u32[]{:S(2)}, u32[]{:S(2)}) collective-permute-start(bf16[4,64,1280]{2,1,0:T(8,128)(2,1)S(1)} %get-tuple-element.63), channel_id=1, source_target_pairs={{0,32},{32,64},{64,96},{96,0},{1,33},{33,65},{65,97},{97,1},{2,34}... | collective-permute-start | bytes 1966088 | tf_op jit(solution)/shard_map/ppermute | solution.py:106
  770.5 24.4 %collective-permute-start.98 = (bf16[4,64,1280]{2,1,0:T(8,128)(2,1)S(1)}, bf16[4,64,1280]{2,1,0:T(8,128)(2,1)S(1)}, u32[]{:S(2)}, u32[]{:S(2)}) collective-permute-start(bf16[4,64,1280]{2,1,0:T(8,128)(2,1)S(1)} %get-tuple-element.61), channel_id=1, source_target_pairs={{0,64},{32,96},{64,0},{96,32},{1,65},{33,97},{65,1},{97,33},{2,66}... | collective-permute-start | bytes 1966088 | tf_op jit(solution)/shard_map/ppermute | solution.py:106
  783.6 14.9 %collective-permute-start.97 = (bf16[64,1152]{1,0:T(8,128)(2,1)S(1)}, bf16[64,1152]{1,0:T(8,128)(2,1)S(1)}, u32[]{:S(2)}, u32[]{:S(2)}) collective-permute-start(bf16[64,1152]{1,0:T(8,128)(2,1)S(1)} %get-tuple-element.139), channel_id=1, source_target_pairs={{0,96},{32,0},{64,32},{96,64},{1,97},{33,1},{65,33},{97,65},{2,98}... | collective-permute-start | bytes 442376 | tf_op jit(solution)/shard_map/ppermute | solution.py:106
  783.8 14.9 %collective-permute-start.96 = (bf16[64,1152]{1,0:T(8,128)(2,1)S(1)}, bf16[64,1152]{1,0:T(8,128)(2,1)S(1)}, u32[]{:S(2)}, u32[]{:S(2)}) collective-permute-start(bf16[64,1152]{1,0:T(8,128)(2,1)S(1)} %get-tuple-element.140), channel_id=1, source_target_pairs={{0,32},{32,64},{64,96},{96,0},{1,33},{33,65},{65,97},{97,1},{2,34}... | collective-permute-start | bytes 442376 | tf_op jit(solution)/shard_map/ppermute | solution.py:106
  785.2 21.6 %collective-permute-start.95 = (bf16[64,1152]{1,0:T(8,128)(2,1)S(1)}, bf16[64,1152]{1,0:T(8,128)(2,1)S(1)}, u32[]{:S(2)}, u32[]{:S(2)}) collective-permute-start(bf16[64,1152]{1,0:T(8,128)(2,1)S(1)} %get-tuple-element.138), channel_id=1, source_target_pairs={{0,64},{32,96},{64,0},{96,32},{1,65},{33,97},{65,1},{97,33},{2,66}... | collective-permute-start | bytes 442376 | tf_op jit(solution)/shard_map/ppermute | solution.py:106
  795.2 11.7 %collective-permute-start.103 = (bf16[64,1280]{1,0:T(8,128)(2,1)S(1)}, bf16[64,1280]{1,0:T(8,128)(2,1)S(1)}, u32[]{:S(2)}, u32[]{:S(2)}) collective-permute-start(bf16[64,1280]{1,0:T(8,128)(2,1)S(1)} %get-tuple-element.120), channel_id=1, source_target_pairs={{0,24},{8,0},{16,8},{24,16},{1,25},{9,1},{17,9},{25,17},{2,26},{10... | collective-permute-start | bytes 491528 | tf_op jit(solution)/shard_map/ppermute | solution.py:106
  820.5 14.1 %collective-permute-start.78 = (bf16[4,64,1152]{2,1,0:T(8,128)(2,1)S(1)}, bf16[4,64,1152]{2,1,0:T(8,128)(2,1)S(1)}, u32[]{:S(2)}, u32[]{:S(2)}) collective-permute-start(bf16[4,64,1152]{2,1,0:T(8,128)(2,1)S(1)} %get-tuple-element.77), channel_id=1, source_target_pairs={{0,24},{8,0},{16,8},{24,16},{1,25},{9,1},{17,9},{25,17},{2,26},{10... | collective-permute-start | bytes 1769480 | tf_op jit(solution)/shard_map/ppermute | solution.py:106
  823.1 11.5 %collective-permute-start.77 = (bf16[4,64,1152]{2,1,0:T(8,128)(2,1)S(1)}, bf16[4,64,1152]{2,1,0:T(8,128)(2,1)S(1)}, u32[]{:S(2)}, u32[]{:S(2)}) collective-permute-start(bf16[4,64,1152]{2,1,0:T(8,128)(2,1)S(1)} %get-tuple-element.78), channel_id=1, source_target_pairs={{0,8},{8,16},{16,24},{24,0},{1,9},{9,17},{17,25},{25,1},{2,10},{10... | collective-permute-start | bytes 1769480 | tf_op jit(solution)/shard_map/ppermute | solution.py:106
  823.2 23.9 %collective-permute-start.76 = (bf16[4,64,1152]{2,1,0:T(8,128)(2,1)S(1)}, bf16[4,64,1152]{2,1,0:T(8,128)(2,1)S(1)}, u32[]{:S(2)}, u32[]{:S(2)}) collective-permute-start(bf16[4,64,1152]{2,1,0:T(8,128)(2,1)S(1)} %get-tuple-element.76), channel_id=1, source_target_pairs={{0,16},{8,24},{16,0},{24,8},{1,17},{9,25},{17,1},{25,9},{2,18},{10... | collective-permute-start | bytes 1769480 | tf_op jit(solution)/shard_map/ppermute | solution.py:106
  826.7 22.2 %collective-permute-start.84 = (bf16[4,64,1280]{2,1,0:T(8,128)(2,1)S(1)}, bf16[4,64,1280]{2,1,0:T(8,128)(2,1)S(1)}, u32[]{:S(2)}, u32[]{:S(2)}) collective-permute-start(bf16[4,64,1280]{2,1,0:T(8,128)(2,1)S(1)} %get-tuple-element.59), channel_id=1, source_target_pairs={{0,96},{32,0},{64,32},{96,64},{1,97},{33,1},{65,33},{97,65},{2,98}... | collective-permute-start | bytes 1966088 | tf_op jit(solution)/shard_map/ppermute | solution.py:106
  826.7 22.2 %collective-permute-start.83 = (bf16[4,64,1280]{2,1,0:T(8,128)(2,1)S(1)}, bf16[4,64,1280]{2,1,0:T(8,128)(2,1)S(1)}, u32[]{:S(2)}, u32[]{:S(2)}) collective-permute-start(bf16[4,64,1280]{2,1,0:T(8,128)(2,1)S(1)} %get-tuple-element.60), channel_id=1, source_target_pairs={{0,32},{32,64},{64,96},{96,0},{1,33},{33,65},{65,97},{97,1},{2,34}... | collective-permute-start | bytes 1966088 | tf_op jit(solution)/shard_map/ppermute | solution.py:106
  834.6 17.5 %collective-permute-start.82 = (bf16[4,64,1280]{2,1,0:T(8,128)(2,1)S(1)}, bf16[4,64,1280]{2,1,0:T(8,128)(2,1)S(1)}, u32[]{:S(2)}, u32[]{:S(2)}) collective-permute-start(bf16[4,64,1280]{2,1,0:T(8,128)(2,1)S(1)} %get-tuple-element.58), channel_id=1, source_target_pairs={{0,64},{32,96},{64,0},{96,32},{1,65},{33,97},{65,1},{97,33},{2,66}... | collective-permute-start | bytes 1966088 | tf_op jit(solution)/shard_map/ppermute | solution.py:106
  861.3 14.4 %collective-permute-start.88 = (bf16[64,2432]{1,0:T(8,128)(2,1)S(1)}, bf16[64,2432]{1,0:T(8,128)(2,1)S(1)}, u32[]{:S(2)}, u32[]{:S(2)}) collective-permute-start(bf16[64,2432]{1,0:T(8,128)(2,1)S(1)} %pad_maximum_fusion.37), channel_id=1, source_target_pairs={{0,4},{4,0},{1,5},{5,1},{2,6},{6,2},{3,7},{7,3},{8,12},{12,8},{9,1... | collective-permute-start | bytes 933896 | tf_op jit(solution)/shard_map/ppermute | solution.py:57
  862.6 14.6 %collective-permute-start.106 = (bf16[64,2432]{1,0:T(8,128)(2,1)S(1)}, bf16[64,2432]{1,0:T(8,128)(2,1)S(1)}, u32[]{:S(2)}, u32[]{:S(2)}) collective-permute-start(bf16[64,2432]{1,0:T(8,128)(2,1)S(1)} %pad_maximum_fusion.40), channel_id=1, source_target_pairs={{0,2},{2,0},{1,3},{3,1},{4,6},{6,4},{5,7},{7,5},{8,10},{10,8},{9,1... | collective-permute-start | bytes 933896 | tf_op jit(solution)/shard_map/ppermute | solution.py:57
  (289 other events, 1654.9 us)
Sparse Core Ops, SparseCore 0:
  15.3 103.0 all-gather.1

commit v2 on v1

--- a/solution.py
+++ b/solution.py
@@ -1,6 +1,8 @@
 import jax
 import jax.numpy as jnp
 from jax import lax
+from jax.experimental import pallas as pl
+from jax.experimental.pallas import tpu as pltpu
 from jax.sharding import Mesh, PartitionSpec as P
 
 D = 960
@@ -80,24 +82,6 @@
     return out
 
 
-def line_gather(values, axis):
-    at = lax.axis_index(axis)
-    out = jnp.zeros((4,) + values.shape, values.dtype)
-    out = lax.dynamic_update_index_in_dim(out, values, at, 0)
-    for step in STEPS:
-        got = lax.ppermute(values, axis, ring(4, step))
-        out = lax.dynamic_update_index_in_dim(out, got, (at - step) % 4, 0)
-    return out
-
-
-def plane_gather(values, cut):
-    first = line_gather(line_gather(values[:, :cut], "x"), "y")
-    second = line_gather(line_gather(values[:, cut:], "y"), "x")
-    first = first.reshape(DP, -1)
-    second = jnp.swapaxes(second, 0, 1).reshape(DP, -1)
-    return first, second
-
-
 def line_scatter(values, axis):
     at = lax.axis_index(axis)
     out = lax.dynamic_index_in_dim(values, at, 0, False).astype(F32)
@@ -116,12 +100,24 @@
     return jnp.concatenate([first, second], axis=1)
 
 
-def reduce_grads(keep, give, cut, over_tp):
-    total = (keep.astype(F32) + swap(give.astype(BF), "core").astype(F32)).astype(BF)
-    total = plane_scatter(total, cut).astype(BF)
-    total = total.astype(F32) + swap(total, "zl").astype(F32)
-    total = total.astype(BF)
-    return total
+def core_sum(keep, give):
+    return (keep.astype(F32) + swap(give.astype(BF), "core").astype(F32)).astype(BF)
+
+
+def low_sum(part):
+    part = part.astype(BF)
+    return (part.astype(F32) + swap(part, "zl").astype(F32)).astype(BF)
+
+
+def diagonal(lefts, rights):
+    tall = jnp.concatenate(lefts, axis=0)
+    width = sum(right.shape[1] for right in rights)
+    blocks, at = [], 0
+    for right in rights:
+        left_over = width - at - right.shape[1]
+        blocks.append(jnp.pad(right, ((0, 0), (at, left_over))))
+        at += right.shape[1]
+    return by_rows(tall, jnp.concatenate(blocks, axis=0)).astype(BF)
 
 
 def finish(total, tp_width):
@@ -130,6 +126,10 @@
     if tp_width < total.shape[1]:
         part = jnp.concatenate([part, total[:, tp_width:]], axis=1)
     return part, swap(part, "core")
+
+
+def scatter_plane(total):
+    return lax.psum_scatter(total, XY, scatter_dimension=0, tiled=True)
 
 
 def rope_tables(positions):
@@ -166,66 +166,113 @@
     weighted = grad_normed * gain
     mean = jnp.sum(weighted * values, axis=-1, keepdims=True) * (1.0 / D)
     grad_values = scale * weighted - values * (scale * scale * scale) * mean
-    gain_terms = (grad_normed * values * scale).astype(BF)
-    ones = jnp.ones((values.shape[0], OUT_PAD - OUT_HALF), BF)
-    return (grad_values, by_rows(gain_terms, ones))
-
-
-def head_rows(matrix, group, row_count):
-    view = matrix.reshape(row_count, KV_HEADS, HEADS // KV_HEADS, HEAD)[:, group]
-    return jnp.transpose(view, (1, 0, 2)).reshape(-1, HEAD)
-
-
-def head_back(block, row_count):
-    return jnp.transpose(block.reshape(HEADS // KV_HEADS, row_count, HEAD), (1, 0, 2)).reshape(
-        row_count, -1
+    return (grad_values, (grad_normed * values * scale).astype(BF))
+
+
+SHARE = HEADS // KV_HEADS
+VM = pl.BlockSpec(memory_space=pltpu.VMEM)
+
+
+def head_stack(ref, group):
+    return jnp.concatenate(
+        [
+            ref[:, (group * SHARE + at) * HEAD : (group * SHARE + at + 1) * HEAD]
+            for at in range(SHARE)
+        ],
+        axis=0,
     )
 
 
-def masked_scores(query_block, key_block, visible):
-    raw = by_columns(query_block, key_block) * HEAD ** (-0.5)
-    shaped = raw.reshape(HEADS // KV_HEADS, visible.shape[0], -1)
-    return jnp.where(visible[None], shaped, MASKED).reshape(raw.shape)
-
-
-def attention(query, key_all, value_all, visible):
-    row_count = query.shape[0]
-    parts = []
-    log_totals = []
+def mask_bias(codes):
+    segment_q, position_q, segment_k, position_k = codes
+    seen = (segment_k[...] == segment_q[...]) & (position_k[...] <= position_q[...])
+    return jnp.where(seen, 0.0, MASKED)
+
+
+def attend_kernel(q_ref, kv_ref, sq, pq, sk, pk, att_ref, lse_ref, bias_ref):
+    rows = q_ref.shape[0]
+    bias_ref[...] = mask_bias((sq, pq, sk, pk))
     for group in range(KV_HEADS):
-        query_block = head_rows(query, group, row_count)
-        key_block = key_all[:, group * HEAD : (group + 1) * HEAD]
-        value_block = value_all[:, group * HEAD : (group + 1) * HEAD]
-        scores = masked_scores(query_block, key_block, visible)
-        top = jnp.max(scores, axis=-1, keepdims=True)
-        log_total = top + jnp.log(jnp.sum(jnp.exp(scores - top), axis=-1, keepdims=True))
-        probs = jnp.exp(scores - log_total).astype(BF)
-        parts.append(head_back(product(probs, value_block), row_count))
-        log_totals.append(log_total)
-    return jnp.concatenate(parts, axis=1).astype(BF), log_totals
-
-
-def attention_back(query, key_all, value_all, visible, log_totals, grad_attended_b):
-    row_count = query.shape[0]
-    query_parts, key_parts, value_parts = [], [], []
+        query = head_stack(q_ref, group) * BF(HEAD ** (-0.5))
+        key = kv_ref[:, group * HEAD : (group + 1) * HEAD]
+        value = kv_ref[:, KVW + group * HEAD : KVW + (group + 1) * HEAD]
+        scores = by_columns(key, query) + bias_ref[...]
+        top = jnp.max(scores, axis=0, keepdims=True)
+        terms = jnp.exp(scores - top)
+        total = jnp.sum(terms, axis=0, keepdims=True)
+        lse_ref[group : group + 1, :] = top + jnp.log(total)
+        out = (by_rows(value, terms.astype(BF)) * (1.0 / total)).T
+        for at in range(SHARE):
+            head = group * SHARE + at
+            att_ref[:, head * HEAD : (head + 1) * HEAD] = out[
+                at * rows : (at + 1) * rows
+            ].astype(BF)
+
+
+def attend_back_kernel(
+    q_ref, kv_ref, da_ref, lse_ref, sq, pq, sk, pk, dq_ref, dkv_ref, bias_ref
+):
+    rows = q_ref.shape[0]
+    bias_ref[...] = mask_bias((sq, pq, sk, pk))
     for group in range(KV_HEADS):
-        query_block = head_rows(query, group, row_count)
-        grad_block = head_rows(grad_attended_b, group, row_count)
-        key_block = key_all[:, group * HEAD : (group + 1) * HEAD]
-        value_block = value_all[:, group * HEAD : (group + 1) * HEAD]
-        scores = masked_scores(query_block, key_block, visible)
-        probs_exact = jnp.exp(scores - log_totals[group])
-        probs = probs_exact.astype(BF)
-        grad_probs = by_columns(grad_block, value_block)
-        delta = jnp.sum(probs_exact * grad_probs, axis=-1, keepdims=True)
-        grad_scores = (probs_exact * (grad_probs - delta) * HEAD ** (-0.5)).astype(BF)
-        query_parts.append(head_back(product(grad_scores, key_block), row_count))
-        key_parts.append(by_rows(grad_scores, query_block))
-        value_parts.append(by_rows(probs, grad_block))
-    return (
-        jnp.concatenate(query_parts, axis=1),
-        jnp.concatenate(key_parts + value_parts, axis=1).astype(BF),
-    )
+        query = head_stack(q_ref, group) * BF(HEAD ** (-0.5))
+        grad = head_stack(da_ref, group)
+        key = kv_ref[:, group * HEAD : (group + 1) * HEAD]
+        value = kv_ref[:, KVW + group * HEAD : KVW + (group + 1) * HEAD]
+        probs = jnp.exp(by_columns(key, query) + bias_ref[...] - lse_ref[group : group + 1, :])
+        grad_probs = by_columns(value, grad)
+        delta = jnp.sum(probs * grad_probs, axis=0, keepdims=True)
+        grad_scores = (probs * (grad_probs - delta)).astype(BF)
+        dkv_ref[:, group * HEAD : (group + 1) * HEAD] = product(grad_scores, query).astype(BF)
+        dkv_ref[:, KVW + group * HEAD : KVW + (group + 1) * HEAD] = product(
+            probs.astype(BF), grad
+        ).astype(BF)
+        out = (by_rows(key, grad_scores) * (HEAD ** (-0.5))).T
+        for at in range(SHARE):
+            head = group * SHARE + at
+            dq_ref[:, head * HEAD : (head + 1) * HEAD] = out[at * rows : (at + 1) * rows]
+
+
+def attention(query, key_value, codes):
+    rows, keys = query.shape[0], key_value.shape[0]
+    return pl.pallas_call(
+        attend_kernel,
+        out_shape=(
+            jax.ShapeDtypeStruct((rows, QW), BF),
+            jax.ShapeDtypeStruct((8, SHARE * rows), F32),
+        ),
+        in_specs=[VM] * 6,
+        out_specs=(VM, VM),
+        scratch_shapes=[pltpu.VMEM((keys, SHARE * rows), F32)],
+        compiler_params=pltpu.CompilerParams(vmem_limit_bytes=40 * 2**20),
+        cost_estimate=pl.CostEstimate(
+            flops=16 * HEADS * HEAD * rows * keys,
+            bytes_accessed=4 * 2**20,
+            transcendentals=HEADS * rows * keys,
+        ),
+        name="attend",
+    )(query, key_value, *codes)
+
+
+def attention_back(query, key_value, grad_attended_b, log_totals, codes):
+    rows, keys = query.shape[0], key_value.shape[0]
+    return pl.pallas_call(
+        attend_back_kernel,
+        out_shape=(
+            jax.ShapeDtypeStruct((rows, QW), F32),
+            jax.ShapeDtypeStruct((keys, 2 * KVW), BF),
+        ),
+        in_specs=[VM] * 8,
+        out_specs=(VM, VM),
+        scratch_shapes=[pltpu.VMEM((keys, SHARE * rows), F32)],
+        compiler_params=pltpu.CompilerParams(vmem_limit_bytes=48 * 2**20),
+        cost_estimate=pl.CostEstimate(
+            flops=40 * HEADS * HEAD * rows * keys,
+            bytes_accessed=6 * 2**20,
+            transcendentals=HEADS * rows * keys,
+        ),
+        name="attend_back",
+    )(query, key_value, grad_attended_b, log_totals, *codes)
 
 
 def pad_features(values):
@@ -289,27 +336,19 @@
             )
         )
     packs = [tall(pack) for pack in packs]
-    cut = 768
-    early = plane_gather(packs[0], cut)
-    early_other = tuple(swap(part, "core") for part in early)
-    rest = lax.all_gather(jnp.concatenate(packs[1:], axis=1), XY, axis=0, tiled=True)
-    rest_other = swap(rest, "core")
-
-    def early_weights(parts):
-        left, right = parts
-        out = right[:, QKV_PAD - cut :]
-        return jnp.concatenate([left, right[:, : QKV_PAD - cut]], axis=1), out
-
-    def att_weights(whole, base):
-        return whole[:, base : base + QKV_PAD], whole[:, base + QKV_PAD : base + ATT]
-
-    def ffn_weights(whole, base):
-        return whole[:, base : base + 2 * hid], whole[:, base + 2 * hid : base + 3 * hid]
-
-    att_mine = [early_weights(early), att_weights(rest, 3 * hid)]
-    att_other = [early_weights(early_other), att_weights(rest_other, 3 * hid)]
-    ffn_mine = [ffn_weights(rest, 0), ffn_weights(rest, 3 * hid + ATT)]
-    ffn_other = [ffn_weights(rest_other, 0), ffn_weights(rest_other, 3 * hid + ATT)]
+    att_mine, att_other, ffn_mine, ffn_other = [], [], [], []
+    for layer in range(layers):
+        whole = lax.all_gather(
+            jnp.concatenate(packs[2 * layer : 2 * layer + 2], axis=1), XY, axis=0, tiled=True
+        )
+        att = whole[:, :ATT]
+        ffn = whole[:, ATT:]
+        for part, att_list, ffn_list in (
+            ((att, ffn), att_mine, ffn_mine),
+            ((swap(att, "core"), swap(ffn, "core")), att_other, ffn_other),
+        ):
+            att_list.append((part[0][:, :QKV_PAD], part[0][:, QKV_PAD:]))
+            ffn_list.append((part[1][:, : 2 * hid], part[1][:, 2 * hid :]))
 
     chooser = jnp.eye(8, OUT_PAD - OUT_HALF, dtype=BF)
     gains = by_columns(chooser, att_mine[0][1][:, OUT_HALF:])
@@ -318,9 +357,11 @@
 
     cosine, sine = rope_tables(positions)
     stamps = gather_group(jnp.stack([segment_ids, positions], axis=1))
-    segment_all, position_all = stamps[:, 0], stamps[:, 1]
-    visible = (segment_ids[:, None] == segment_all[None, :]) & (
-        position_all[None, :] <= positions[:, None]
+    codes = (
+        jnp.tile(segment_ids, SHARE)[None, :],
+        jnp.tile(positions, SHARE)[None, :],
+        stamps[:, :1],
+        stamps[:, 1:],
     )
     stream = pad_features(tokens)
     saved = []
@@ -338,8 +379,7 @@
         query = turned[:, :QW]
         key_value = jnp.concatenate([turned[:, QW:], qkv[:, QW + KVW :].astype(BF)], axis=1)
         key_value = gather_group(key_value)
-        key_all, value_all = key_value[:, :KVW], key_value[:, KVW:]
-        attended, log_totals = attention(query, key_all, value_all, visible)
+        attended, log_totals = attention(query, key_value, codes)
         att_m, att_o = halves(attended, OUT_HALF)
         mixed = (
             stream
@@ -365,8 +405,7 @@
                 scale_one,
                 normed_one,
                 query,
-                key_all,
-                value_all,
+                key_value,
                 log_totals,
                 att_m,
                 att_o,
@@ -391,8 +430,7 @@
             scale_one,
             normed_one,
             query,
-            key_all,
-            value_all,
+            key_value,
             log_totals,
             att_m,
             att_o,
@@ -417,17 +455,14 @@
             ).astype(BF)
             grad_gu = jnp.concatenate([grad_gate_in, grad_up_in], axis=1)
             partial = partial + by_columns(grad_gu, gu)
-            ffn_grads.append(
-                jnp.concatenate(
-                    [
-                        by_rows(normed_pair, grad_gu).astype(BF),
-                        by_rows(grad_pair, hidden).astype(BF),
-                    ],
-                    axis=1,
-                )
-            )
-        grad_normed_two = partial[:rows] + swap(partial[rows:].astype(BF), "tp").astype(F32)
-        grad_mixed_norm, gain_two_column = rms_backward(
+            ffn_grads.append(diagonal([normed_pair, grad_pair], [grad_gu, hidden]))
+        arrived = swap(partial[rows:].astype(BF), "tp")
+        if layer == 0:
+            arrived, ffn_grads, pending = lax.optimization_barrier((arrived, ffn_grads, pending))
+            later = scatter_plane(pending)
+            ffn_sum = core_sum(ffn_grads[0], ffn_grads[1])
+        grad_normed_two = partial[:rows] + arrived.astype(F32)
+        grad_mixed_norm, gain_two_terms = rms_backward(
             mixed, scale_two, gain_twos[layer], grad_normed_two
         )
         grad_mixed = grad_stream + grad_mixed_norm
@@ -435,15 +470,12 @@
         grad_attended_b = join(
             product(grad_mixed_b, out_m)[:, :OUT_HALF], product(grad_mixed_b, out_o)[:, :OUT_HALF]
         ).astype(BF)
-        out_grads = [
-            jnp.concatenate(
-                [by_rows(grad_mixed_b, att), gain_two_column * weight], axis=1
-            ).astype(BF)
-            for att, weight in ((att_m, 1.0), (att_o, 1.0))
-        ]
         grad_query, key_value_terms = attention_back(
-            query, key_all, value_all, visible, log_totals, grad_attended_b
-        )
+            query, key_value, grad_attended_b, log_totals, codes
+        )
+        if layer == 0:
+            ffn_sum, key_value_terms = lax.optimization_barrier((ffn_sum, key_value_terms))
+            ffn_sum = plane_scatter(ffn_sum, 1024)
         key_value_grad = scatter_group(key_value_terms)
         grad_qkv = jnp.concatenate(
             [
@@ -461,41 +493,53 @@
         wide = ((0, 0), (0, QKV_PAD - QKV_HALF))
         grad_m, grad_o = jnp.pad(grad_m, wide), jnp.pad(grad_o, wide)
         grad_normed_one = by_columns(grad_m, qkv_m) + by_columns(grad_o, qkv_o)
-        grad_input_norm, gain_one_column = rms_backward(
+        grad_input_norm, gain_one_terms = rms_backward(
             layer_input, scale_one, gain_ones[layer], grad_normed_one
         )
         grad_stream = grad_mixed + grad_input_norm
-        qkv_grads = [
-            jnp.concatenate(
+        ones = jnp.ones((rows, OUT_PAD - OUT_HALF), BF)
+        att_grads = [
+            diagonal(
+                [normed_one, gain_one_terms, grad_mixed_b, gain_two_terms],
                 [
-                    by_rows(normed_one, part[:, :QKV_HALF]),
-                    gain_one_column,
-                    jnp.zeros((DP, QKV_PAD - QKV_HALF - OUT_PAD + OUT_HALF), F32),
+                    grad_part[:, :QKV_HALF],
+                    jnp.ones((rows, QKV_PAD - QKV_HALF), BF),
+                    att_part,
+                    ones,
                 ],
-                axis=1,
-            ).astype(BF)
-            for part in (grad_m, grad_o)
+            )
+            for grad_part, att_part in ((grad_m, att_m), (grad_o, att_o))
         ]
-        one = reduce_grads(
-            jnp.concatenate([out_grads[0], ffn_grads[0]], axis=1),
-            jnp.concatenate([out_grads[1], ffn_grads[1]], axis=1),
-            1152,
-            OUT_PAD,
-        )
-        two = reduce_grads(qkv_grads[0], qkv_grads[1], 512, QKV_PAD)
-        results[layer] = (finish(one, OUT_PAD), finish(two, QKV_PAD))
+        if layer > 0:
+            grad_stream, keep, give = lax.optimization_barrier(
+                (
+                    grad_stream,
+                    jnp.concatenate([att_grads[0], ffn_grads[0]], axis=1),
+                    jnp.concatenate([att_grads[1], ffn_grads[1]], axis=1),
+                )
+            )
+            pending = core_sum(keep, give)
+        else:
+            later = low_sum(later)
+            ffn_sum = low_sum(ffn_sum)
+            att_sum = low_sum(plane_scatter(core_sum(att_grads[0], att_grads[1]), 768))
+            results[1] = finish(later, ATT)
+            results[0] = finish(jnp.concatenate([att_sum, ffn_sum], axis=1), ATT)
 
     stacked = [[] for _ in range(9)]
     for layer in range(layers):
-        (one_m, one_o), (two_m, two_o) = results[layer]
-        qkv = join(two_m[:PER, :QKV_HALF], two_o[:PER, :QKV_HALF]).astype(F32)
-        out = join(one_m[:PER, :OUT_HALF], one_o[:PER, :OUT_HALF]).astype(F32)
-        gain_one = jnp.where(first_core, two_m[:PER, QKV_HALF], two_o[:PER, QKV_HALF])
-        gain_two = jnp.where(first_core, one_m[:PER, OUT_HALF], one_o[:PER, OUT_HALF])
+        mine, other = results[layer]
+        mine, other = mine[:PER], other[:PER]
+        qkv = join(mine[:, :QKV_HALF], other[:, :QKV_HALF]).astype(F32)
+        out = join(
+            mine[:, QKV_PAD : QKV_PAD + OUT_HALF], other[:, QKV_PAD : QKV_PAD + OUT_HALF]
+        ).astype(F32)
+        gain_one = pick(mine[:, QKV_HALF], other[:, QKV_HALF])[0]
+        gain_two = pick(mine[:, QKV_PAD + OUT_HALF], other[:, QKV_PAD + OUT_HALF])[0]
         ffn = [
             join(
-                one_m[:PER, OUT_PAD + at * hid : OUT_PAD + (at + 1) * hid],
-                one_o[:PER, OUT_PAD + at * hid : OUT_PAD + (at + 1) * hid],
+                mine[:, ATT + at * hid : ATT + (at + 1) * hid],
+                other[:, ATT + at * hid : ATT + (at + 1) * hid],
             ).astype(F32)
             for at in range(3)
         ]

time: 916 us -> 618 us (0.67)
  local copies, waits for them, and re-layouts: 228 us -> 90.4 us
  matrix products: 210 us -> 101 us
  starting transfers between devices: 182 us -> 100 us
  Pallas kernels: 0 us -> 32.8 us
    all_gather x1 -> x2, waiting for transfers between devices: 0.02 us -> 65.7 us  [shards(): lax.all_gather(jnp.concatenate(packs[2 * layer:2 * layer + 2], axis=1), X...]
    dot_general x37 -> x17, matrix products: 80 us -> 32.4 us  [by_columns(): lax.dot_general(left, right, (((1,), (1,)), ((), ())), preferred_element_...]
    dot_general x36 -> x16, matrix products: 70.9 us -> 28.5 us  [product(): return jnp.dot(left, right, preferred_element_type=F32)]
    reshape x40 -> x0, local copies, waits for them, and re-layouts: 40.8 us -> none  [the longest x20 17.6 us: head_rows(): return jnp.transpose(view, (1, 0, 2)).reshape(-1, HEAD)]
    ppermute x48 -> x24, waiting for transfers between devices: 84.5 us -> 45.8 us  [line_scatter(): out = out + lax.ppermute(block, axis, ring(4, step)).astype(F32)]
    concatenate x7 -> x0, local copies, waits for them, and re-layouts: 36 us -> none  [the longest x2 16.2 us: shards(): jnp.concatenate([out_grads[0], ffn_grads[0]], axis=1)]
    transpose x34 -> x0, local copies, waits for them, and re-layouts: 34.6 us -> none  [the longest x24 23.2 us: head_rows(): return jnp.transpose(view, (1, 0, 2)).reshape(-1, HEAD)]
    ppermute x32 -> x27, starting transfers between devices: 86.4 us -> 51.9 us  [swap(): return lax.ppermute(values, axis, [(0, 1), (1, 0)])]
  transfers between devices with their start and end apart: 108 -> 69, of which waited for: 50 -> 34; matrix products, arithmetic and copies ran while one was open for 32% -> 31% of each run, Pallas kernels for 0% -> 4%
where the time goes in v2:
time: 618 us; the launch traced here: 607 us
  waiting for transfers between devices  195 us (32%)
  matrix products  101 us (16%)
  starting transfers between devices  100 us (16%)
  local copies, waits for them, and re-layouts  90.4 us (15%)
  other arithmetic  70.9 us (11%)
  Pallas kernels  32.8 us (5%)
  between operations  16.6 us (3%)
    all_gather x2, waiting for transfers between devices, shards(): lax.all_gather(jnp.concatenate(packs[2 * layer:2 * layer + 2], axis=1), X...  65.7 us
    ppermute x27, waiting for transfers between devices, swap(): return lax.ppermute(values, axis, [(0, 1), (1, 0)])  55.9 us
    ppermute x27, starting transfers between devices, swap(): return lax.ppermute(values, axis, [(0, 1), (1, 0)])  51.9 us
    ppermute x24, waiting for transfers between devices, line_scatter(): out = out + lax.ppermute(block, axis, ring(4, step)).astype(F32)  45.8 us
    dot_general x8, matrix products, by_rows(): lax.dot_general(left, right, (((0,), (0,)), ((), ())), preferred_element_...  40 us
    dot_general x17, matrix products, by_columns(): lax.dot_general(left, right, (((1,), (1,)), ((), ())), preferred_element_...  32.4 us
    ppermute x24, starting transfers between devices, line_scatter(): out = out + lax.ppermute(block, axis, ring(4, step)).astype(F32)  30.1 us
    dot_general x16, matrix products, product(): return jnp.dot(left, right, preferred_element_type=F32)  28.5 us
  transfers between devices with their start and end apart: 69, of which 34 were waited for; matrix products, arithmetic and copies ran while one was open for 31% of the time, Pallas kernels for 4%

profile of v2, /device:TPU:1, one launch (start us, length us, event | category | flops | bytes accessed | tf_op | source)
XLA Modules:
  0.0 607.4 jit_solution(6502564041773389763)
XLA Ops:
  16.8 65.7 %all-gather.3.cloned.1.call-done = bf16[1024,3328]{1,0:T(8,128)(2,1)} async-done(((bf16[64,3328]{1,0:T(8,128)(2,1)}), bf16[1024,3328]{1,0:T(8,128)(2,1)}) %all-gather.3.cloned.1.call-update) | async-done | bytes 6815760 | tf_op jit(solution)/shard_map/all_gather | solution.py:341
  82.4 3.6 slice.811
  88.8 3.2 multiply_reduce_fusion
  95.3 4.4 slice.827
  118.6 5.5 collective-permute-done.1
  138.7 5.9 attend.2
  152.4 7.3 %collective-permute-done.9 = bf16[160,1024]{1,0:T(8,128)(2,1)S(1)} collective-permute-done((bf16[160,1024]{1,0:T(8,128)(2,1)S(1)}, bf16[160,1024]{1,0:T(8,128)(2,1)S(1)}, u32[]{:S(2)}, u32[]{:S(2)}) %collective-permute-start.9) | collective-permute-done | bytes 327712 | tf_op jit(solution)/shard_map/ppermute | solution.py:59
  162.9 3.2 fusion.47
  174.1 13.8 %collective-permute-start.18 = (bf16[1024,1920]{1,0:T(8,128)(2,1)}, bf16[1024,1920]{1,0:T(8,128)(2,1)}, u32[]{:S(2)}, u32[]{:S(2)}) collective-permute-start(bf16[1024,1920]{1,0:T(8,128)(2,1)} %slice.860), channel_id=1, source_target_pairs={{0,2},{2,0},{1,3},{3,1},{4,6},{6,4},{5,7},{7,5},{8,10},{10,8},{9,1... | collective-permute-start | bytes 11796488 | tf_op jit(solution)/shard_map/ppermute | solution.py:59
  202.6 3.3 collective-permute-done.14
  205.9 4.5 collective-permute-done.13
  223.3 5.8 attend.3
  237.2 3.2 reshape.588
  250.8 3.1 fusion.39
  253.9 3.2 collective-permute-done.20
  267.5 3.0 collective-permute-start.19
  270.6 3.2 collective-permute-done.21
  274.0 6.8 %collective-permute-done.19 = bf16[160,1024]{1,0:T(8,128)(2,1)S(1)} collective-permute-done((bf16[160,1024]{1,0:T(8,128)(2,1)S(1)}, bf16[160,1024]{1,0:T(8,128)(2,1)S(1)}, u32[]{:S(2)}, u32[]{:S(2)}) %collective-permute-start.19) | collective-permute-done | bytes 327712 | tf_op jit(solution)/shard_map/ppermute | solution.py:59
  284.6 10.5 %attend_back.2 = (f32[160,960]{1,0:T(8,128)S(1)}, bf16[1280,640]{1,0:T(8,128)(2,1)S(1)}) custom-call(bf16[160,960]{1,0:T(8,128)(2,1)S(1)} %copy.142.q_ref, bf16[1280,640]{1,0:T(8,128)(2,1)S(1)} %copy-done.3, bf16[160,960]{1,0:T(8,128)(2,1)S(1)} %pad_maximum_fusion.47.da_ref, f32[8,480]{1,0:T(8,128)S(1)} %get-tuple-element.30.lse_ref, ...), custom_call_target="tpu_custom_call" | custom-call | flops 7864320000 | bytes 6291456 | tf_op jit(solution)/shard_map/attend_back/pallas_call | solution.py:259
  297.4 6.8 %convolution_convert_fusion.6 = bf16[1024,1920]{1,0:T(8,128)(2,1)} fusion(bf16[320,640]{1,0:T(8,128)(2,1)S(1)} %get-tuple-element.112, bf16[320,1280]{1,0:T(8,128)(2,1)S(1)} %pad_maximum_fusion.23, bf16[160,1024]{1,0:T(8,128)(2,1)S(1)} %collective-permute-done.20, bf16[160,1024]{1,0:T(8,128)(2,1)S(1)} %convert_element_type.548, ...), kind=kOutput, calls=%fused_computation.31 | convolution fusion | flops 2533621760 | bytes 6471680 | tf_op jit(solution)/shard_map/dot_general | solution.py:38
  307.8 6.8 %convolution_convert_fusion.7 = bf16[1024,1920]{1,0:T(8,128)(2,1)} fusion(bf16[320,640]{1,0:T(8,128)(2,1)S(1)} %get-tuple-element.113, bf16[320,1280]{1,0:T(8,128)(2,1)S(1)} %pad_maximum_fusion.22, bf16[160,1024]{1,0:T(8,128)(2,1)S(1)} %collective-permute-done.20, bf16[160,1024]{1,0:T(8,128)(2,1)S(1)} %convert_element_type.548, ...), kind=kOutput, calls=%fused_computation.32 | convolution fusion | flops 2533621760 | bytes 6471680 | tf_op jit(solution)/shard_map/dot_general | solution.py:38
  329.9 4.2 convolution_convert_fusion.2
  334.2 4.3 convolution_convert_fusion.3
  338.5 5.0 pad_maximum_fusion.1
  343.5 6.4 %pad_maximum_fusion = bf16[1024,3328]{1,0:T(8,128)(2,1)} fusion(bf16[1024,1920]{1,0:T(8,128)(2,1)} %convolution_convert_fusion.7, bf16[1024,1408]{1,0:T(8,128)(2,1)} %convolution_convert_fusion.3), kind=kLoop, calls=%fused_computation.2 | loop fusion | flops 13631488 | bytes 13631488 | tf_op jit(solution)/shard_map/concatenate | solution.py:517
  351.8 9.8 %collective-permute-done.26 = bf16[160,1024]{1,0:T(8,128)(2,1)S(1)} collective-permute-done((bf16[160,1024]{1,0:T(8,128)(2,1)S(1)}, bf16[160,1024]{1,0:T(8,128)(2,1)S(1)}, u32[]{:S(2)}, u32[]{:S(2)}) %collective-permute-start.26) | collective-permute-done | bytes 327712 | tf_op jit(solution)/shard_map/ppermute | solution.py:59
  374.7 4.6 convolution_convert_fusion.5
  379.3 4.7 convolution_convert_fusion.4
  384.0 9.4 %add_convert_fusion = bf16[1024,3328]{1,0:T(8,128)(2,1)} fusion(bf16[1024,3328]{1,0:T(8,128)(2,1)} %collective-permute-done.28, bf16[1024,3328]{1,0:T(8,128)(2,1)} %pad_maximum_fusion), kind=kLoop, calls=%fused_computation | loop fusion | flops 13631488 | bytes 20447232 | tf_op jit(solution)/shard_map/convert_element_type | solution.py:104
  402.1 10.5 %attend_back.3 = (f32[160,960]{1,0:T(8,128)S(1)}, bf16[1280,640]{1,0:T(8,128)(2,1)S(1)}) custom-call(bf16[160,960]{1,0:T(8,128)(2,1)S(1)} %copy.131.q_ref, bf16[1280,640]{1,0:T(8,128)(2,1)S(1)} %copy-done.1, bf16[160,960]{1,0:T(8,128)(2,1)S(1)} %pad_maximum_fusion.48.da_ref, f32[8,480]{1,0:T(8,128)S(1)} %get-tuple-element.37.lse_ref, ...), custom_call_target="tpu_custom_call" | custom-call | flops 7864320000 | bytes 6291456 | tf_op jit(solution)/shard_map/attend_back/pallas_call | solution.py:259
  412.7 5.2 add_convert_fusion.1
  425.4 3.6 collective-permute-done.31
  429.0 4.8 collective-permute-done.33
  444.9 4.2 convolution_convert_fusion
  462.2 7.7 %collective-permute-done.55 = bf16[4,64,896]{2,1,0:T(8,128)(2,1)S(1)} collective-permute-done((bf16[4,64,896]{2,1,0:T(8,128)(2,1)}, bf16[4,64,896]{2,1,0:T(8,128)(2,1)S(1)}, u32[]{:S(2)}, u32[]{:S(2)}) %collective-permute-start.55) | collective-permute-done | bytes 458784 | tf_op jit(solution)/shard_map/ppermute | solution.py:90
  469.9 3.0 collective-permute-start.51
  472.9 11.4 %collective-permute-done.57 = bf16[4,64,896]{2,1,0:T(8,128)(2,1)} collective-permute-done((bf16[4,64,896]{2,1,0:T(8,128)(2,1)}, bf16[4,64,896]{2,1,0:T(8,128)(2,1)}, u32[]{:S(2)}, u32[]{:S(2)}) %collective-permute-start.57) | collective-permute-done | bytes 458784 | tf_op jit(solution)/shard_map/ppermute | solution.py:90
  494.4 5.2 collective-permute-done.50
  503.1 3.3 collective-permute-start.54
  506.4 4.4 add_convert_fusion.2
  515.0 4.7 collective-permute-done.53
  521.2 5.9 collective-permute-done.43
  527.2 3.4 collective-permute-done.42
  533.0 4.1 collective-permute-start.40
  549.0 3.3 collective-permute-done.48
  553.1 9.2 %collective-permute-start.62 = (bf16[64,3328]{1,0:T(8,128)(2,1)}, bf16[64,3328]{1,0:T(8,128)(2,1)}, u32[]{:S(2)}, u32[]{:S(2)}) collective-permute-start(bf16[64,3328]{1,0:T(8,128)(2,1)} %pad_maximum_fusion.37), channel_id=1, source_target_pairs={{0,2},{2,0},{1,3},{3,1},{4,6},{6,4},{5,7},{7,5},{8,10},{10,8},{9,1... | collective-permute-start | bytes 1277960 | tf_op jit(solution)/shard_map/ppermute | solution.py:59
  569.0 9.8 %collective-permute-done.63 = bf16[64,3328]{1,0:T(8,128)(2,1)S(1)} collective-permute-done((bf16[64,3328]{1,0:T(8,128)(2,1)}, bf16[64,3328]{1,0:T(8,128)(2,1)S(1)}, u32[]{:S(2)}, u32[]{:S(2)}) %collective-permute-start.63) | collective-permute-done | bytes 426016 | tf_op jit(solution)/shard_map/ppermute | solution.py:59
  581.5 5.3 collective-permute-done.64
  (572 shorter events, 260.4 us)
Async XLA Ops:
  7.2 75.3 %all-gather.3.cloned.1.call-start = ((), (), s32[]{:S(2)}) async-start(), calls=%async_computation.1 | async-start | bytes 7241728 | tf_op jit(solution)/shard_map/all_gather | solution.py:341
  15.6 134.1 %all-gather.5.cloned.1.call-start = ((), (), s32[]{:S(2)}) async-start(), calls=%async_computation.2 | async-start | bytes 7241728 | tf_op jit(solution)/shard_map/all_gather | solution.py:341
  16.7 550.0 %reduce-scatter.2.cloned.1.call-start = ((), (), s32[]{:S(2)}) async-start(), calls=%async_computation.3 | async-start | bytes 7241728 | tf_op jit(solution)/shard_map/reduce_scatter | solution.py:132
  86.1 17.8 %collective-permute-start = (bf16[1024,1408]{1,0:T(8,128)(2,1)}, bf16[1024,1408]{1,0:T(8,128)(2,1)S(1)}, u32[]{:S(2)}, u32[]{:S(2)}) collective-permute-start(bf16[1024,1408]{1,0:T(8,128)(2,1)} %slice.811), channel_id=1, source_target_pairs={{0,2},{2,0},{1,3},{3,1},{4,6},{6,4},{5,7},{7,5},{8,10},{10,8},{9,1... | collective-permute-start | bytes 8650760 | tf_op jit(solution)/shard_map/ppermute | solution.py:59
  99.6 63.3 %collective-permute-start.10 = (bf16[1024,1920]{1,0:T(8,128)(2,1)}, bf16[1024,1920]{1,0:T(8,128)(2,1)}, u32[]{:S(2)}, u32[]{:S(2)}) collective-permute-start(bf16[1024,1920]{1,0:T(8,128)(2,1)} %slice.827), channel_id=1, source_target_pairs={{0,2},{2,0},{1,3},{3,1},{4,6},{6,4},{5,7},{7,5},{8,10},{10,8},{9,1... | collective-permute-start | bytes 11796488 | tf_op jit(solution)/shard_map/ppermute | solution.py:59
  112.4 11.7 %collective-permute-start.1 = (bf16[160,640]{1,0:T(8,128)(2,1)S(1)}, bf16[160,640]{1,0:T(8,128)(2,1)S(1)}, u32[]{:S(2)}, u32[]{:S(2)}) collective-permute-start(bf16[160,640]{1,0:T(8,128)(2,1)S(1)} %get-tuple-element.91), channel_id=1, source_target_pairs={{0,1},{1,0},{4,5},{5,4},{2,3},{3,2},{6,7},{7,6},{8,9},{9,8},{12,13... | collective-permute-start | bytes 614408 | tf_op jit(solution)/shard_map/ppermute | solution.py:63
  114.9 9.7 %collective-permute-start.3 = (bf16[160,640]{1,0:T(8,128)(2,1)S(1)}, bf16[160,640]{1,0:T(8,128)(2,1)S(1)}, u32[]{:S(2)}, u32[]{:S(2)}) collective-permute-start(bf16[160,640]{1,0:T(8,128)(2,1)S(1)} %get-tuple-element.91), channel_id=1, source_target_pairs={{0,5},{1,4},{4,0},{5,1},{2,7},{3,6},{6,2},{7,3},{8,13},{9,12},{12,... | collective-permute-start | bytes 614408 | tf_op jit(solution)/shard_map/ppermute | solution.py:63
  116.1 11.1 %collective-permute-start.7 = (s32[160,2]{0,1:T(2,128)S(1)}, s32[160,2]{0,1:T(2,128)S(1)}, u32[]{:S(2)}, u32[]{:S(2)}) collective-permute-start(s32[160,2]{0,1:T(2,128)S(1)} %pad_add_fusion.1), channel_id=1, source_target_pairs={{0,5},{1,4},{4,0},{5,1},{2,7},{3,6},{6,2},{7,3},{8,13},{9,12},{12,... | collective-permute-start | bytes 3848 | tf_op jit(solution)/shard_map/ppermute | solution.py:63
  125.7 11.7 %collective-permute-start.4 = (bf16[640,640]{1,0:T(8,128)(2,1)}, bf16[640,640]{1,0:T(8,128)(2,1)}, u32[]{:S(2)}, u32[]{:S(2)}) collective-permute-start(bf16[640,640]{1,0:T(8,128)(2,1)} %pad_maximum_fusion.20), channel_id=1, source_target_pairs={{0,2},{2,0},{1,3},{3,1},{4,6},{6,4},{5,7},{7,5},{8,10},{10,8},{9,1... | collective-permute-start | bytes 2457608 | tf_op jit(solution)/shard_map/ppermute | solution.py:59
  149.2 10.6 %collective-permute-start.9 = (bf16[160,1024]{1,0:T(8,128)(2,1)S(1)}, bf16[160,1024]{1,0:T(8,128)(2,1)S(1)}, u32[]{:S(2)}, u32[]{:S(2)}) collective-permute-start(bf16[160,1024]{1,0:T(8,128)(2,1)S(1)} %multiply_convert_fusion.18), channel_id=1, source_target_pairs={{0,1},{1,0},{2,3},{3,2},{4,5},{5,4},{6,7},{7,6},{8,9},{9,8},{10,11... | collective-permute-start | bytes 983048 | tf_op jit(solution)/shard_map/ppermute | solution.py:59
  151.7 37.2 %collective-permute-start.12 = (bf16[1024,1408]{1,0:T(8,128)(2,1)S(1)}, bf16[1024,1408]{1,0:T(8,128)(2,1)S(1)}, u32[]{:S(2)}, u32[]{:S(2)}) collective-permute-start(bf16[1024,1408]{1,0:T(8,128)(2,1)S(1)} %slice.846), channel_id=1, source_target_pairs={{0,2},{2,0},{1,3},{3,1},{4,6},{6,4},{5,7},{7,5},{8,10},{10,8},{9,1... | collective-permute-start | bytes 8650760 | tf_op jit(solution)/shard_map/ppermute | solution.py:59
  171.5 16.5 %collective-permute-start.11 = (bf16[160,1024]{1,0:T(8,128)(2,1)S(1)}, bf16[160,1024]{1,0:T(8,128)(2,1)S(1)}, u32[]{:S(2)}, u32[]{:S(2)}) collective-permute-start(bf16[160,1024]{1,0:T(8,128)(2,1)S(1)} %slice.1187), channel_id=1, source_target_pairs={{0,1},{1,0},{2,3},{3,2},{4,5},{5,4},{6,7},{7,6},{8,9},{9,8},{10,11... | collective-permute-start | bytes 983048 | tf_op jit(solution)/shard_map/ppermute | solution.py:59
  174.1 76.6 %collective-permute-start.18 = (bf16[1024,1920]{1,0:T(8,128)(2,1)}, bf16[1024,1920]{1,0:T(8,128)(2,1)}, u32[]{:S(2)}, u32[]{:S(2)}) collective-permute-start(bf16[1024,1920]{1,0:T(8,128)(2,1)} %slice.860), channel_id=1, source_target_pairs={{0,2},{2,0},{1,3},{3,1},{4,6},{6,4},{5,7},{7,5},{8,10},{10,8},{9,1... | collective-permute-start | bytes 11796488 | tf_op jit(solution)/shard_map/ppermute | solution.py:59
  198.0 12.4 %collective-permute-start.13 = (bf16[160,640]{1,0:T(8,128)(2,1)S(1)}, bf16[160,640]{1,0:T(8,128)(2,1)S(1)}, u32[]{:S(2)}, u32[]{:S(2)}) collective-permute-start(bf16[160,640]{1,0:T(8,128)(2,1)S(1)} %get-tuple-element.87), channel_id=1, source_target_pairs={{0,1},{1,0},{4,5},{5,4},{2,3},{3,2},{6,7},{7,6},{8,9},{9,8},{12,13... | collective-permute-start | bytes 614408 | tf_op jit(solution)/shard_map/ppermute | solution.py:63
  200.5 10.0 %collective-permute-start.15 = (bf16[160,640]{1,0:T(8,128)(2,1)S(1)}, bf16[160,640]{1,0:T(8,128)(2,1)S(1)}, u32[]{:S(2)}, u32[]{:S(2)}) collective-permute-start(bf16[160,640]{1,0:T(8,128)(2,1)S(1)} %get-tuple-element.87), channel_id=1, source_target_pairs={{0,5},{1,4},{4,0},{5,1},{2,7},{3,6},{6,2},{7,3},{8,13},{9,12},{12,... | collective-permute-start | bytes 614408 | tf_op jit(solution)/shard_map/ppermute | solution.py:63
  234.7 13.1 %collective-permute-start.17 = (bf16[160,1024]{1,0:T(8,128)(2,1)}, bf16[160,1024]{1,0:T(8,128)(2,1)}, u32[]{:S(2)}, u32[]{:S(2)}) collective-permute-start(bf16[160,1024]{1,0:T(8,128)(2,1)} %multiply_convert_fusion.16), channel_id=1, source_target_pairs={{0,1},{1,0},{2,3},{3,2},{4,5},{5,4},{6,7},{7,6},{8,9},{9,8},{10,11... | collective-permute-start | bytes 983048 | tf_op jit(solution)/shard_map/ppermute | solution.py:59
  246.5 10.6 %collective-permute-start.20 = (bf16[160,1024]{1,0:T(8,128)(2,1)S(1)}, bf16[160,1024]{1,0:T(8,128)(2,1)S(1)}, u32[]{:S(2)}, u32[]{:S(2)}) collective-permute-start(bf16[160,1024]{1,0:T(8,128)(2,1)S(1)} %convert_element_type.548), channel_id=1, source_target_pairs={{0,1},{1,0},{2,3},{3,2},{4,5},{5,4},{6,7},{7,6},{8,9},{9,8},{10,11... | collective-permute-start | bytes 983048 | tf_op jit(solution)/shard_map/ppermute | solution.py:59
  264.1 9.7 %collective-permute-start.21 = (bf16[160,1024]{1,0:T(8,128)(2,1)S(1)}, bf16[160,1024]{1,0:T(8,128)(2,1)S(1)}, u32[]{:S(2)}, u32[]{:S(2)}) collective-permute-start(bf16[160,1024]{1,0:T(8,128)(2,1)S(1)} %slice.1185), channel_id=1, source_target_pairs={{0,1},{1,0},{2,3},{3,2},{4,5},{5,4},{6,7},{7,6},{8,9},{9,8},{10,11... | collective-permute-start | bytes 983048 | tf_op jit(solution)/shard_map/ppermute | solution.py:59
  267.5 13.3 %collective-permute-start.19 = (bf16[160,1024]{1,0:T(8,128)(2,1)S(1)}, bf16[160,1024]{1,0:T(8,128)(2,1)S(1)}, u32[]{:S(2)}, u32[]{:S(2)}) collective-permute-start(bf16[160,1024]{1,0:T(8,128)(2,1)S(1)} %slice.1186), channel_id=1, source_target_pairs={{0,1},{1,0},{2,3},{3,2},{4,5},{5,4},{6,7},{7,6},{8,9},{9,8},{10,11... | collective-permute-start | bytes 983048 | tf_op jit(solution)/shard_map/ppermute | solution.py:59
  295.2 9.0 %collective-permute-start.22 = (bf16[640,640]{1,0:T(8,128)(2,1)S(1)}, bf16[640,640]{1,0:T(8,128)(2,1)S(1)}, u32[]{:S(2)}, u32[]{:S(2)}) collective-permute-start(bf16[640,640]{1,0:T(8,128)(2,1)S(1)} %slice.712), channel_id=1, source_target_pairs={{0,2},{2,0},{1,3},{3,1},{4,6},{6,4},{5,7},{7,5},{8,10},{10,8},{9,1... | collective-permute-start | bytes 2457608 | tf_op jit(solution)/shard_map/ppermute | solution.py:59
  304.5 10.1 %collective-permute-start.23 = (bf16[160,640]{1,0:T(8,128)(2,1)S(1)}, bf16[160,640]{1,0:T(8,128)(2,1)S(1)}, u32[]{:S(2)}, u32[]{:S(2)}) collective-permute-start(bf16[160,640]{1,0:T(8,128)(2,1)S(1)} %get-tuple-element.147), channel_id=1, source_target_pairs={{0,1},{1,0},{4,5},{5,4},{2,3},{3,2},{6,7},{7,6},{8,9},{9,8},{12,13... | collective-permute-start | bytes 614408 | tf_op jit(solution)/shard_map/ppermute | solution.py:63
  305.0 12.5 %collective-permute-start.25 = (bf16[160,640]{1,0:T(8,128)(2,1)S(1)}, bf16[160,640]{1,0:T(8,128)(2,1)S(1)}, u32[]{:S(2)}, u32[]{:S(2)}) collective-permute-start(bf16[160,640]{1,0:T(8,128)(2,1)S(1)} %get-tuple-element.148), channel_id=1, source_target_pairs={{0,4},{1,5},{4,1},{5,0},{2,6},{3,7},{6,3},{7,2},{8,12},{9,13},{12,... | collective-permute-start | bytes 614408 | tf_op jit(solution)/shard_map/ppermute | solution.py:63
  306.4 11.1 %collective-permute-start.24 = (bf16[160,640]{1,0:T(8,128)(2,1)S(1)}, bf16[160,640]{1,0:T(8,128)(2,1)S(1)}, u32[]{:S(2)}, u32[]{:S(2)}) collective-permute-start(bf16[160,640]{1,0:T(8,128)(2,1)S(1)} %get-tuple-element.149), channel_id=1, source_target_pairs={{0,5},{1,4},{4,0},{5,1},{2,7},{3,6},{6,2},{7,3},{8,13},{9,12},{12,... | collective-permute-start | bytes 614408 | tf_op jit(solution)/shard_map/ppermute | solution.py:63
  349.9 34.0 %collective-permute-start.28 = (bf16[1024,3328]{1,0:T(8,128)(2,1)}, bf16[1024,3328]{1,0:T(8,128)(2,1)}, u32[]{:S(2)}, u32[]{:S(2)}) collective-permute-start(bf16[1024,3328]{1,0:T(8,128)(2,1)} %pad_maximum_fusion.1), channel_id=1, source_target_pairs={{0,2},{2,0},{1,3},{3,1},{4,6},{6,4},{5,7},{7,5},{8,10},{10,8},{9,1... | collective-permute-start | bytes 20447240 | tf_op jit(solution)/shard_map/ppermute | solution.py:59
  350.5 11.1 %collective-permute-start.26 = (bf16[160,1024]{1,0:T(8,128)(2,1)S(1)}, bf16[160,1024]{1,0:T(8,128)(2,1)S(1)}, u32[]{:S(2)}, u32[]{:S(2)}) collective-permute-start(bf16[160,1024]{1,0:T(8,128)(2,1)S(1)} %convert_element_type.566), channel_id=1, source_target_pairs={{0,1},{1,0},{2,3},{3,2},{4,5},{5,4},{6,7},{7,6},{8,9},{9,8},{10,11... | collective-permute-start | bytes 983048 | tf_op jit(solution)/shard_map/ppermute | solution.py:59
  373.5 19.9 %collective-permute-start.27 = (bf16[160,1024]{1,0:T(8,128)(2,1)}, bf16[160,1024]{1,0:T(8,128)(2,1)S(1)}, u32[]{:S(2)}, u32[]{:S(2)}) collective-permute-start(bf16[160,1024]{1,0:T(8,128)(2,1)} %slice.1184), channel_id=1, source_target_pairs={{0,1},{1,0},{2,3},{3,2},{4,5},{5,4},{6,7},{7,6},{8,9},{9,8},{10,11... | collective-permute-start | bytes 983048 | tf_op jit(solution)/shard_map/ppermute | solution.py:59
  393.4 19.3 %collective-permute-start.29 = (bf16[1024,1920]{1,0:T(8,128)(2,1)}, bf16[1024,1920]{1,0:T(8,128)(2,1)}, u32[]{:S(2)}, u32[]{:S(2)}) collective-permute-start(bf16[1024,1920]{1,0:T(8,128)(2,1)} %convolution_convert_fusion.4), channel_id=1, source_target_pairs={{0,2},{2,0},{1,3},{3,1},{4,6},{6,4},{5,7},{7,5},{8,10},{10,8},{9,1... | collective-permute-start | bytes 11796488 | tf_op jit(solution)/shard_map/ppermute | solution.py:59
  422.8 11.1 %collective-permute-start.33 = (bf16[160,640]{1,0:T(8,128)(2,1)S(1)}, bf16[160,640]{1,0:T(8,128)(2,1)S(1)}, u32[]{:S(2)}, u32[]{:S(2)}) collective-permute-start(bf16[160,640]{1,0:T(8,128)(2,1)S(1)} %get-tuple-element.145), channel_id=1, source_target_pairs={{0,4},{1,5},{4,1},{5,0},{2,6},{3,7},{6,3},{7,2},{8,12},{9,13},{12,... | collective-permute-start | bytes 614408 | tf_op jit(solution)/shard_map/ppermute | solution.py:63
  423.1 10.7 %collective-permute-start.32 = (bf16[160,640]{1,0:T(8,128)(2,1)S(1)}, bf16[160,640]{1,0:T(8,128)(2,1)S(1)}, u32[]{:S(2)}, u32[]{:S(2)}) collective-permute-start(bf16[160,640]{1,0:T(8,128)(2,1)S(1)} %get-tuple-element.146), channel_id=1, source_target_pairs={{0,5},{1,4},{4,0},{5,1},{2,7},{3,6},{6,2},{7,3},{8,13},{9,12},{12,... | collective-permute-start | bytes 614408 | tf_op jit(solution)/shard_map/ppermute | solution.py:63
  449.2 53.9 %collective-permute-start.34 = (bf16[1024,1408]{1,0:T(8,128)(2,1)}, bf16[1024,1408]{1,0:T(8,128)(2,1)}, u32[]{:S(2)}, u32[]{:S(2)}) collective-permute-start(bf16[1024,1408]{1,0:T(8,128)(2,1)} %convolution_convert_fusion), channel_id=1, source_target_pairs={{0,2},{2,0},{1,3},{3,1},{4,6},{6,4},{5,7},{7,5},{8,10},{10,8},{9,1... | collective-permute-start | bytes 8650760 | tf_op jit(solution)/shard_map/ppermute | solution.py:59
  453.7 16.3 %collective-permute-start.55 = (bf16[4,64,896]{2,1,0:T(8,128)(2,1)}, bf16[4,64,896]{2,1,0:T(8,128)(2,1)S(1)}, u32[]{:S(2)}, u32[]{:S(2)}) collective-permute-start(bf16[4,64,896]{2,1,0:T(8,128)(2,1)} %get-tuple-element.109), channel_id=1, source_target_pairs={{0,64},{32,96},{64,0},{96,32},{1,65},{33,97},{65,1},{97,33},{2,66}... | collective-permute-start | bytes 1376264 | tf_op jit(solution)/shard_map/ppermute | solution.py:90
  456.5 27.8 %collective-permute-start.57 = (bf16[4,64,896]{2,1,0:T(8,128)(2,1)}, bf16[4,64,896]{2,1,0:T(8,128)(2,1)}, u32[]{:S(2)}, u32[]{:S(2)}) collective-permute-start(bf16[4,64,896]{2,1,0:T(8,128)(2,1)} %get-tuple-element.110), channel_id=1, source_target_pairs={{0,96},{32,0},{64,32},{96,64},{1,97},{33,1},{65,33},{97,65},{2,98}... | collective-permute-start | bytes 1376264 | tf_op jit(solution)/shard_map/ppermute | solution.py:90
  457.3 27.3 %collective-permute-start.56 = (bf16[4,64,896]{2,1,0:T(8,128)(2,1)}, bf16[4,64,896]{2,1,0:T(8,128)(2,1)}, u32[]{:S(2)}, u32[]{:S(2)}) collective-permute-start(bf16[4,64,896]{2,1,0:T(8,128)(2,1)} %get-tuple-element.111), channel_id=1, source_target_pairs={{0,32},{32,64},{64,96},{96,0},{1,33},{33,65},{65,97},{97,1},{2,34}... | collective-permute-start | bytes 1376264 | tf_op jit(solution)/shard_map/ppermute | solution.py:90
  461.0 28.1 %collective-permute-start.49 = (bf16[4,64,1024]{2,1,0:T(8,128)(2,1)}, bf16[4,64,1024]{2,1,0:T(8,128)(2,1)}, u32[]{:S(2)}, u32[]{:S(2)}) collective-permute-start(bf16[4,64,1024]{2,1,0:T(8,128)(2,1)} %get-tuple-element.106), channel_id=1, source_target_pairs={{0,16},{8,24},{16,0},{24,8},{1,17},{9,25},{17,1},{25,9},{2,18},{10... | collective-permute-start | bytes 1572872 | tf_op jit(solution)/shard_map/ppermute | solution.py:90
  469.9 21.8 %collective-permute-start.51 = (bf16[4,64,1024]{2,1,0:T(8,128)(2,1)}, bf16[4,64,1024]{2,1,0:T(8,128)(2,1)}, u32[]{:S(2)}, u32[]{:S(2)}) collective-permute-start(bf16[4,64,1024]{2,1,0:T(8,128)(2,1)} %get-tuple-element.107), channel_id=1, source_target_pairs={{0,24},{8,0},{16,8},{24,16},{1,25},{9,1},{17,9},{25,17},{2,26},{10... | collective-permute-start | bytes 1572872 | tf_op jit(solution)/shard_map/ppermute | solution.py:90
  484.3 15.3 %collective-permute-start.50 = (bf16[4,64,1024]{2,1,0:T(8,128)(2,1)}, bf16[4,64,1024]{2,1,0:T(8,128)(2,1)}, u32[]{:S(2)}, u32[]{:S(2)}) collective-permute-start(bf16[4,64,1024]{2,1,0:T(8,128)(2,1)} %get-tuple-element.108), channel_id=1, source_target_pairs={{0,8},{8,16},{16,24},{24,0},{1,9},{9,17},{17,25},{25,1},{2,10},{10... | collective-permute-start | bytes 1572872 | tf_op jit(solution)/shard_map/ppermute | solution.py:90
  486.3 24.8 %collective-permute-start.58 = (bf16[64,896]{1,0:T(8,128)(2,1)S(1)}, bf16[64,896]{1,0:T(8,128)(2,1)S(1)}, u32[]{:S(2)}, u32[]{:S(2)}) collective-permute-start(bf16[64,896]{1,0:T(8,128)(2,1)S(1)} %get-tuple-element.172), channel_id=1, source_target_pairs={{0,16},{8,24},{16,0},{24,8},{1,17},{9,25},{17,1},{25,9},{2,18},{10... | collective-permute-start | bytes 344072 | tf_op jit(solution)/shard_map/ppermute | solution.py:90
  489.1 22.0 %collective-permute-start.60 = (bf16[64,896]{1,0:T(8,128)(2,1)S(1)}, bf16[64,896]{1,0:T(8,128)(2,1)S(1)}, u32[]{:S(2)}, u32[]{:S(2)}) collective-permute-start(bf16[64,896]{1,0:T(8,128)(2,1)S(1)} %get-tuple-element.173), channel_id=1, source_target_pairs={{0,24},{8,0},{16,8},{24,16},{1,25},{9,1},{17,9},{25,17},{2,26},{10... | collective-permute-start | bytes 344072 | tf_op jit(solution)/shard_map/ppermute | solution.py:90
  491.7 20.7 %collective-permute-start.59 = (bf16[64,896]{1,0:T(8,128)(2,1)S(1)}, bf16[64,896]{1,0:T(8,128)(2,1)S(1)}, u32[]{:S(2)}, u32[]{:S(2)}) collective-permute-start(bf16[64,896]{1,0:T(8,128)(2,1)S(1)} %get-tuple-element.174), channel_id=1, source_target_pairs={{0,8},{8,16},{16,24},{24,0},{1,9},{9,17},{17,25},{25,1},{2,10},{10... | collective-permute-start | bytes 344072 | tf_op jit(solution)/shard_map/ppermute | solution.py:90
  501.3 12.8 %collective-permute-start.52 = (bf16[64,1024]{1,0:T(8,128)(2,1)S(1)}, bf16[64,1024]{1,0:T(8,128)(2,1)S(1)}, u32[]{:S(2)}, u32[]{:S(2)}) collective-permute-start(bf16[64,1024]{1,0:T(8,128)(2,1)S(1)} %get-tuple-element.169), channel_id=1, source_target_pairs={{0,64},{32,96},{64,0},{96,32},{1,65},{33,97},{65,1},{97,33},{2,66}... | collective-permute-start | bytes 393224 | tf_op jit(solution)/shard_map/ppermute | solution.py:90
  503.1 11.8 %collective-permute-start.54 = (bf16[64,1024]{1,0:T(8,128)(2,1)S(1)}, bf16[64,1024]{1,0:T(8,128)(2,1)S(1)}, u32[]{:S(2)}, u32[]{:S(2)}) collective-permute-start(bf16[64,1024]{1,0:T(8,128)(2,1)S(1)} %get-tuple-element.170), channel_id=1, source_target_pairs={{0,96},{32,0},{64,32},{96,64},{1,97},{33,1},{65,33},{97,65},{2,98}... | collective-permute-start | bytes 393224 | tf_op jit(solution)/shard_map/ppermute | solution.py:90
  512.6 14.6 %collective-permute-start.43 = (bf16[4,64,640]{2,1,0:T(8,128)(2,1)S(1)}, bf16[4,64,640]{2,1,0:T(8,128)(2,1)S(1)}, u32[]{:S(2)}, u32[]{:S(2)}) collective-permute-start(bf16[4,64,640]{2,1,0:T(8,128)(2,1)S(1)} %get-tuple-element.130), channel_id=1, source_target_pairs={{0,96},{32,0},{64,32},{96,64},{1,97},{33,1},{65,33},{97,65},{2,98}... | collective-permute-start | bytes 983048 | tf_op jit(solution)/shard_map/ppermute | solution.py:90
  514.1 16.5 %collective-permute-start.42 = (bf16[4,64,640]{2,1,0:T(8,128)(2,1)S(1)}, bf16[4,64,640]{2,1,0:T(8,128)(2,1)S(1)}, u32[]{:S(2)}, u32[]{:S(2)}) collective-permute-start(bf16[4,64,640]{2,1,0:T(8,128)(2,1)S(1)} %get-tuple-element.131), channel_id=1, source_target_pairs={{0,32},{32,64},{64,96},{96,0},{1,33},{33,65},{65,97},{97,1},{2,34}... | collective-permute-start | bytes 983048 | tf_op jit(solution)/shard_map/ppermute | solution.py:90
  514.9 16.1 %collective-permute-start.35 = (bf16[4,64,768]{2,1,0:T(8,128)(2,1)S(1)}, bf16[4,64,768]{2,1,0:T(8,128)(2,1)S(1)}, u32[]{:S(2)}, u32[]{:S(2)}) collective-permute-start(bf16[4,64,768]{2,1,0:T(8,128)(2,1)S(1)} %get-tuple-element.114), channel_id=1, source_target_pairs={{0,16},{8,24},{16,0},{24,8},{1,17},{9,25},{17,1},{25,9},{2,18},{10... | collective-permute-start | bytes 1179656 | tf_op jit(solution)/shard_map/ppermute | solution.py:90
  519.7 12.8 %collective-permute-start.37 = (bf16[4,64,768]{2,1,0:T(8,128)(2,1)S(1)}, bf16[4,64,768]{2,1,0:T(8,128)(2,1)S(1)}, u32[]{:S(2)}, u32[]{:S(2)}) collective-permute-start(bf16[4,64,768]{2,1,0:T(8,128)(2,1)S(1)} %get-tuple-element.115), channel_id=1, source_target_pairs={{0,24},{8,0},{16,8},{24,16},{1,25},{9,1},{17,9},{25,17},{2,26},{10... | collective-permute-start | bytes 1179656 | tf_op jit(solution)/shard_map/ppermute | solution.py:90
  520.1 12.5 %collective-permute-start.36 = (bf16[4,64,768]{2,1,0:T(8,128)(2,1)S(1)}, bf16[4,64,768]{2,1,0:T(8,128)(2,1)S(1)}, u32[]{:S(2)}, u32[]{:S(2)}) collective-permute-start(bf16[4,64,768]{2,1,0:T(8,128)(2,1)S(1)} %get-tuple-element.116), channel_id=1, source_target_pairs={{0,8},{8,16},{16,24},{24,0},{1,9},{9,17},{17,25},{25,1},{2,10},{10... | collective-permute-start | bytes 1179656 | tf_op jit(solution)/shard_map/ppermute | solution.py:90
  553.1 12.7 %collective-permute-start.62 = (bf16[64,3328]{1,0:T(8,128)(2,1)}, bf16[64,3328]{1,0:T(8,128)(2,1)}, u32[]{:S(2)}, u32[]{:S(2)}) collective-permute-start(bf16[64,3328]{1,0:T(8,128)(2,1)} %pad_maximum_fusion.37), channel_id=1, source_target_pairs={{0,2},{2,0},{1,3},{3,1},{4,6},{6,4},{5,7},{7,5},{8,10},{10,8},{9,1... | collective-permute-start | bytes 1277960 | tf_op jit(solution)/shard_map/ppermute | solution.py:59
  566.8 12.0 %collective-permute-start.63 = (bf16[64,3328]{1,0:T(8,128)(2,1)}, bf16[64,3328]{1,0:T(8,128)(2,1)S(1)}, u32[]{:S(2)}, u32[]{:S(2)}) collective-permute-start(bf16[64,3328]{1,0:T(8,128)(2,1)} %reduce-scatter.2.cloned.1.call-done), channel_id=1, source_target_pairs={{0,4},{4,0},{1,5},{5,1},{2,6},{6,2},{3,7},{7,3},{8,12},{12,8},{9,1... | collective-permute-start | bytes 1277960 | tf_op jit(solution)/shard_map/ppermute | solution.py:59
  (123 other events, 811.6 us)
Sparse Core Ops, SparseCore 0:
  15.7 66.6 all-gather.2
  85.1 63.2 all-gather.4
  395.1 89.4 reduce-scatter.1

commit v3 on v2

--- a/solution.py
+++ b/solution.py
@@ -27,6 +27,7 @@
 OUT_PAD = 512
 ATT = QKV_PAD + OUT_PAD
 BF = jnp.bfloat16
+VM = pl.BlockSpec(memory_space=pltpu.VMEM)
 F32 = jnp.float32
 
 
@@ -109,6 +110,75 @@
     return (part.astype(F32) + swap(part, "zl").astype(F32)).astype(BF)
 
 
+def z_sum(part):
+    part = part.astype(BF)
+    two, one, three = (z_send(part, step).astype(F32) for step in STEPS)
+    return ((part.astype(F32) + two) + (one + three)).astype(BF)
+
+
+def merge_kernel(a_ref, b_ref, c_ref, d_ref, out_ref):
+    width = a_ref.shape[1]
+    out_ref[:, :width] = (a_ref[...].astype(F32) + b_ref[...].astype(F32)).astype(BF)
+    out_ref[:, width:] = (c_ref[...].astype(F32) + d_ref[...].astype(F32)).astype(BF)
+
+
+def merge_sum(first, second):
+    left, right = first[0].shape[1], second[0].shape[1]
+    block = 128
+    narrow = pl.BlockSpec((block, left), lambda i: (i, 0))
+    broad = pl.BlockSpec((block, right), lambda i: (i, 0))
+    return pl.pallas_call(
+        merge_kernel,
+        grid=(DP // block,),
+        out_shape=jax.ShapeDtypeStruct((DP, left + right), BF),
+        in_specs=[narrow, narrow, broad, broad],
+        out_specs=pl.BlockSpec((block, left + right), lambda i: (i, 0)),
+        cost_estimate=pl.CostEstimate(
+            flops=2 * DP * (left + right),
+            bytes_accessed=6 * DP * (left + right),
+            transcendentals=0,
+        ),
+        name="merge_sum",
+    )(first[0], swap(first[1], "core"), second[0], swap(second[1], "core"))
+
+
+def write_kernel(flag_ref, m0, o0, m1, o1, q_ref, k_ref, v_ref, w_ref, gain_ref, qkv_ref, out_ref):
+    first = flag_ref[0] == 0
+    chooser = (
+        lax.broadcasted_iota(jnp.int32, (8, OUT_PAD - OUT_HALF), 0)
+        == lax.broadcasted_iota(jnp.int32, (8, OUT_PAD - OUT_HALF), 1)
+    ).astype(BF)
+    for layer, (mine, other) in enumerate(((m0, o0), (m1, o1))):
+        low = jnp.where(first, mine[...], other[...]).astype(F32)
+        high = jnp.where(first, other[...], mine[...]).astype(F32)
+        qkv_ref[:, :QKV_HALF] = low[:, :QKV_HALF]
+        qkv_ref[:, QKV_HALF:] = high[:, :QKV_HALF]
+        out_ref[:, :OUT_HALF] = low[:, QKV_PAD : QKV_PAD + OUT_HALF]
+        out_ref[:, OUT_HALF:] = high[:, QKV_PAD : QKV_PAD + OUT_HALF]
+        q_ref[layer] = qkv_ref[:PER, :QW]
+        k_ref[layer] = qkv_ref[:PER, QW : QW + KVW]
+        v_ref[layer] = qkv_ref[:PER, QW + KVW :]
+        w_ref[layer] = out_ref[:PER, :]
+        low = low.astype(BF)
+        for at, start in enumerate((QKV_HALF, QKV_PAD + OUT_HALF)):
+            gain_ref[at * 2 + layer] = by_columns(
+                chooser, low[:, start : start + OUT_PAD - OUT_HALF]
+            )
+
+
+def write_grads(flag, parts):
+    shapes = [(2, PER, QW), (2, PER, KVW), (2, PER, KVW), (2, PER, QW), (4, 8, PAD)]
+    return pl.pallas_call(
+        write_kernel,
+        out_shape=tuple(jax.ShapeDtypeStruct(shape, F32) for shape in shapes),
+        in_specs=[pl.BlockSpec(memory_space=pltpu.SMEM)] + [VM] * 4,
+        out_specs=(VM,) * 5,
+        scratch_shapes=[pltpu.VMEM((PAD, QW + 2 * KVW), F32), pltpu.VMEM((PAD, QW), F32)],
+        compiler_params=pltpu.CompilerParams(vmem_limit_bytes=32 * 2**20),
+        name="write_grads",
+    )(flag, *parts)
+
+
 def diagonal(lefts, rights):
     tall = jnp.concatenate(lefts, axis=0)
     width = sum(right.shape[1] for right in rights)
@@ -118,14 +188,6 @@
         blocks.append(jnp.pad(right, ((0, 0), (at, left_over))))
         at += right.shape[1]
     return by_rows(tall, jnp.concatenate(blocks, axis=0)).astype(BF)
-
-
-def finish(total, tp_width):
-    part = total[:, :tp_width]
-    part = (part.astype(F32) + swap(part, "tp").astype(F32)).astype(BF)
-    if tp_width < total.shape[1]:
-        part = jnp.concatenate([part, total[:, tp_width:]], axis=1)
-    return part, swap(part, "core")
 
 
 def scatter_plane(total):
@@ -170,7 +232,6 @@
 
 
 SHARE = HEADS // KV_HEADS
-VM = pl.BlockSpec(memory_space=pltpu.VMEM)
 
 
 def head_stack(ref, group):
@@ -457,10 +518,11 @@
             partial = partial + by_columns(grad_gu, gu)
             ffn_grads.append(diagonal([normed_pair, grad_pair], [grad_gu, hidden]))
         arrived = swap(partial[rows:].astype(BF), "tp")
-        if layer == 0:
-            arrived, ffn_grads, pending = lax.optimization_barrier((arrived, ffn_grads, pending))
-            later = scatter_plane(pending)
+        arrived, ffn_grads = lax.optimization_barrier((arrived, ffn_grads))
+        if layer > 0:
             ffn_sum = core_sum(ffn_grads[0], ffn_grads[1])
+        else:
+            later_sum = merge_sum(att_pair, ffn_grads)
         grad_normed_two = partial[:rows] + arrived.astype(F32)
         grad_mixed_norm, gain_two_terms = rms_backward(
             mixed, scale_two, gain_twos[layer], grad_normed_two
@@ -470,12 +532,17 @@
         grad_attended_b = join(
             product(grad_mixed_b, out_m)[:, :OUT_HALF], product(grad_mixed_b, out_o)[:, :OUT_HALF]
         ).astype(BF)
+        if layer > 0:
+            ffn_sum, grad_attended_b = lax.optimization_barrier((ffn_sum, grad_attended_b))
+            ffn_done = scatter_plane(ffn_sum)
+        else:
+            later_sum, grad_attended_b, ffn_done = lax.optimization_barrier(
+                (later_sum, grad_attended_b, ffn_done)
+            )
+            later = scatter_plane(later_sum)
         grad_query, key_value_terms = attention_back(
             query, key_value, grad_attended_b, log_totals, codes
         )
-        if layer == 0:
-            ffn_sum, key_value_terms = lax.optimization_barrier((ffn_sum, key_value_terms))
-            ffn_sum = plane_scatter(ffn_sum, 1024)
         key_value_grad = scatter_group(key_value_terms)
         grad_qkv = jnp.concatenate(
             [
@@ -511,51 +578,41 @@
             for grad_part, att_part in ((grad_m, att_m), (grad_o, att_o))
         ]
         if layer > 0:
-            grad_stream, keep, give = lax.optimization_barrier(
-                (
-                    grad_stream,
-                    jnp.concatenate([att_grads[0], ffn_grads[0]], axis=1),
-                    jnp.concatenate([att_grads[1], ffn_grads[1]], axis=1),
-                )
-            )
-            pending = core_sum(keep, give)
+            grad_stream, att_pair = lax.optimization_barrier((grad_stream, att_grads))
         else:
-            later = low_sum(later)
-            ffn_sum = low_sum(ffn_sum)
-            att_sum = low_sum(plane_scatter(core_sum(att_grads[0], att_grads[1]), 768))
-            results[1] = finish(later, ATT)
-            results[0] = finish(jnp.concatenate([att_sum, ffn_sum], axis=1), ATT)
-
-    stacked = [[] for _ in range(9)]
-    for layer in range(layers):
-        mine, other = results[layer]
-        mine, other = mine[:PER], other[:PER]
-        qkv = join(mine[:, :QKV_HALF], other[:, :QKV_HALF]).astype(F32)
-        out = join(
-            mine[:, QKV_PAD : QKV_PAD + OUT_HALF], other[:, QKV_PAD : QKV_PAD + OUT_HALF]
-        ).astype(F32)
-        gain_one = pick(mine[:, QKV_HALF], other[:, QKV_HALF])[0]
-        gain_two = pick(mine[:, QKV_PAD + OUT_HALF], other[:, QKV_PAD + OUT_HALF])[0]
-        ffn = [
-            join(
-                mine[:, ATT + at * hid : ATT + (at + 1) * hid],
-                other[:, ATT + at * hid : ATT + (at + 1) * hid],
-            ).astype(F32)
-            for at in range(3)
-        ]
-        for at, value in enumerate(
+            ffn_one = low_sum(ffn_done)
+            ffn_one = (ffn_one, swap(ffn_one, "core"))
+            att_grads, ffn_one = lax.optimization_barrier((att_grads, ffn_one))
+            att_zero = z_sum(plane_scatter(core_sum(att_grads[0], att_grads[1]), 768))
+            att_one = z_sum(later[:, :ATT])
+            ffn_zero = low_sum(later[:, ATT:])
+            ffn_zero = (ffn_zero, swap(ffn_zero, "core"))
+
+    query_grads, key_grads, value_grads, out_grads, gain_grads = write_grads(
+        lax.axis_index("core").astype(jnp.int32).reshape(1),
+        (att_zero, swap(att_zero, "core"), att_one, swap(att_one, "core")),
+    )
+    ffn_outs = [
+        jnp.stack(
             [
-                gain_one.astype(F32),
-                qkv[:, :QW],
-                qkv[:, QW : QW + KVW],
-                qkv[:, QW + KVW :],
-                out,
-                gain_two.astype(F32),
+                join(
+                    mine[:PER, at * hid : (at + 1) * hid], other[:PER, at * hid : (at + 1) * hid]
+                ).astype(F32)
+                for mine, other in (ffn_zero, ffn_one)
             ]
-            + ffn
-        ):
-            stacked[at].append(value)
-    return (block_out, cut_features(grad_stream)) + tuple(jnp.stack(part) for part in stacked)
+        )
+        for at in range(3)
+    ]
+    return (
+        block_out,
+        cut_features(grad_stream),
+        gain_grads[:2, 0, :PER],
+        query_grads,
+        key_grads,
+        value_grads,
+        out_grads,
+        gain_grads[2:, 0, :PER],
+    ) + tuple(ffn_outs)
 
 
 def solution(mesh):

time: 618 us -> 539 us (0.87)
  other arithmetic: 70.9 us -> 38 us
  starting transfers between devices: 100 us -> 75.1 us
  waiting for transfers between devices: 195 us -> 181 us
  matrix products: 101 us -> 90.2 us
  Pallas kernels: 32.8 us -> 43 us
  local copies, waits for them, and re-layouts: 90.4 us -> 84.1 us
    ppermute x24 -> x12, waiting for transfers between devices: 45.8 us -> 23.7 us  [line_scatter(): out = out + lax.ppermute(block, axis, ring(4, step)).astype(F32)]
    ppermute x24 -> x12, starting transfers between devices: 30.1 us -> 12.7 us  [line_scatter(): out = out + lax.ppermute(block, axis, ring(4, step)).astype(F32)]
    ppermute x27, starting transfers between devices: 51.9 us -> 38.4 us  [swap(): return lax.ppermute(values, axis, [(0, 1), (1, 0)])]
    concatenate x4 -> x0, other arithmetic: 12.3 us -> none  [the longest x1 6.42 us: shards(): jnp.concatenate([att_grads[0], ffn_grads[0]], axis=1)]
    pallas_call x0 -> x2, Pallas kernels: none -> 10.3 us  [the longest x1 9.94 us: merge_sum(): pl.pallas_call(merge_kernel, grid=(DP // block,), out_shape=jax.ShapeDtyp...]
    convert_element_type x2, other arithmetic: 14.6 us -> 6.28 us  [core_sum(): (keep.astype(F32) + swap(give.astype(BF), 'core').astype(F32)).astype(BF)]
    ppermute x15 -> x21, waiting for transfers between devices: 28 us -> 33.8 us  [z_send(): return lax.ppermute(values, ('zl', 'tp'), z_ring(step))]
    ppermute x15 -> x21, starting transfers between devices: 18.2 us -> 23.9 us  [z_send(): return lax.ppermute(values, ('zl', 'tp'), z_ring(step))]
  transfers between devices with their start and end apart: 69 -> 64, of which waited for: 34 -> 31; matrix products, arithmetic and copies ran while one was open for 31% -> 32% of each run, Pallas kernels for 4% -> 6%
where the time goes in v3:
time: 539 us; the launch traced here: 528 us
  waiting for transfers between devices  181 us (34%)
  matrix products  90.2 us (17%)
  local copies, waits for them, and re-layouts  84.1 us (16%)
  starting transfers between devices  75.1 us (14%)
  Pallas kernels  43 us (8%)
  other arithmetic  38 us (7%)
  between operations  16.3 us (3%)
    all_gather x2, waiting for transfers between devices, shards(): lax.all_gather(jnp.concatenate(packs[2 * layer:2 * layer + 2], axis=1), X...  66.5 us
    ppermute x27, waiting for transfers between devices, swap(): return lax.ppermute(values, axis, [(0, 1), (1, 0)])  57.1 us
    ppermute x27, starting transfers between devices, swap(): return lax.ppermute(values, axis, [(0, 1), (1, 0)])  38.4 us
    dot_general x8, matrix products, by_rows(): lax.dot_general(left, right, (((0,), (0,)), ((), ())), preferred_element_...  35.3 us
    ppermute x21, waiting for transfers between devices, z_send(): return lax.ppermute(values, ('zl', 'tp'), z_ring(step))  33.8 us
    unnamed x221, local copies, waits for them, and re-layouts  33.5 us
    dot_general x17, matrix products, by_columns(): lax.dot_general(left, right, (((1,), (1,)), ((), ())), preferred_element_...  30.5 us
    dot_general x16, matrix products, product(): return jnp.dot(left, right, preferred_element_type=F32)  24.4 us
  transfers between devices with their start and end apart: 64, of which 31 were waited for; matrix products, arithmetic and copies ran while one was open for 32% of the time, Pallas kernels for 6%

profile of v3, /device:TPU:1, one launch (start us, length us, event | category | flops | bytes accessed | tf_op | source)
XLA Modules:
  0.0 528.0 jit_solution(16687379371193241865)
XLA Ops:
  16.8 65.7 %all-gather.3.cloned.1.call-done = bf16[1024,3328]{1,0:T(8,128)(2,1)} async-done(((bf16[64,3328]{1,0:T(8,128)(2,1)}), bf16[1024,3328]{1,0:T(8,128)(2,1)}) %all-gather.3.cloned.1.call-update) | async-done | bytes 6815760 | tf_op jit(solution)/shard_map/all_gather | solution.py:402
  82.5 3.7 slice.674
  89.0 3.2 multiply_reduce_fusion
  95.4 4.4 slice.690
  115.5 5.5 %collective-permute-done.1 = bf16[160,640]{1,0:T(8,128)(2,1)S(1)} collective-permute-done((bf16[160,640]{1,0:T(8,128)(2,1)S(1)}, bf16[160,640]{1,0:T(8,128)(2,1)S(1)}, u32[]{:S(2)}, u32[]{:S(2)}) %collective-permute-start.1) | collective-permute-done | bytes 204832 | tf_op jit(solution)/shard_map/ppermute | solution.py:64
  125.0 2.8 collective-permute-start.8
  136.7 5.9 %attend.2 = (bf16[160,960]{1,0:T(8,128)(2,1)S(1)}, f32[8,480]{1,0:T(8,128)S(1)}) custom-call(bf16[160,960]{1,0:T(8,128)(2,1)S(1)} %copy.131.q_ref, bf16[1280,640]{1,0:T(8,128)(2,1)S(1)} %constant_dynamic-update-slice_fusion.kv_ref, s32[1,480]{1,0:T(1,128)S(1)} %broadcast_in_dim_tile.6.sq, s32[1,480]{1,0:T(1,128)S(1)} %broadcast_in_dim_tile.7.pq, ...), custom_call_target="tpu_custom_call" | custom-call | flops 3145728000 | bytes 4194304 | tf_op jit(solution)/shard_map/attend/pallas_call | solution.py:299
  151.3 6.4 %collective-permute-done.9 = bf16[160,1024]{1,0:T(8,128)(2,1)S(1)} collective-permute-done((bf16[160,1024]{1,0:T(8,128)(2,1)S(1)}, bf16[160,1024]{1,0:T(8,128)(2,1)S(1)}, u32[]{:S(2)}, u32[]{:S(2)}) %collective-permute-start.9) | collective-permute-done | bytes 327712 | tf_op jit(solution)/shard_map/ppermute | solution.py:60
  158.4 2.8 fusion.51
  162.4 2.9 fusion.47
  165.6 2.9 fusion.122
  175.0 5.2 collective-permute-done.11
  190.5 8.5 %collective-permute-done.14 = bf16[160,640]{1,0:T(8,128)(2,1)S(1)} collective-permute-done((bf16[160,640]{1,0:T(8,128)(2,1)S(1)}, bf16[160,640]{1,0:T(8,128)(2,1)S(1)}, u32[]{:S(2)}, u32[]{:S(2)}) %collective-permute-start.14) | collective-permute-done | bytes 204832 | tf_op jit(solution)/shard_map/ppermute | solution.py:64
  213.1 5.8 %attend.3 = (bf16[160,960]{1,0:T(8,128)(2,1)S(1)}, f32[8,480]{1,0:T(8,128)S(1)}) custom-call(bf16[160,960]{1,0:T(8,128)(2,1)S(1)} %copy.142.q_ref, bf16[1280,640]{1,0:T(8,128)(2,1)S(1)} %copy-done.2, s32[1,480]{1,0:T(1,128)S(1)} %broadcast_in_dim_tile.6.sq, s32[1,480]{1,0:T(1,128)S(1)} %broadcast_in_dim_tile.7.pq, s32[1280,1]{1,0:T(8,128)S(1)} %copy.133.sk, ...), custom_call_target="tpu_custom_call" | custom-call | flops 3145728000 | bytes 4194304 | tf_op jit(solution)/shard_map/attend/pallas_call | solution.py:299
  224.2 3.2 reshape.418
  231.5 2.7 collective-permute-start.20
  234.8 3.1 fusion.39
  237.9 4.5 collective-permute-done.20
  248.7 2.8 fusion.96
  254.0 5.5 %convolution_convert_fusion.6 = bf16[1024,1920]{1,0:T(8,128)(2,1)S(1)} fusion(bf16[320,640]{1,0:T(8,128)(2,1)S(1)} %get-tuple-element.130, bf16[320,1280]{1,0:T(8,128)(2,1)S(1)} %pad_maximum_fusion.21, bf16[160,1024]{1,0:T(8,128)(2,1)S(1)} %collective-permute-done.20, bf16[160,1024]{1,0:T(8,128)(2,1)S(1)} %convert_element_type.409, ...), kind=kOutput, calls=%fused_computation.28 | convolution fusion | flops 2533621760 | bytes 6471680 | tf_op jit(solution)/shard_map/dot_general | solution.py:39
  259.5 5.5 %convolution_convert_fusion.7 = bf16[1024,1920]{1,0:T(8,128)(2,1)S(1)} fusion(bf16[320,640]{1,0:T(8,128)(2,1)S(1)} %get-tuple-element.131, bf16[320,1280]{1,0:T(8,128)(2,1)S(1)} %pad_maximum_fusion.20, bf16[160,1024]{1,0:T(8,128)(2,1)S(1)} %collective-permute-done.20, bf16[160,1024]{1,0:T(8,128)(2,1)S(1)} %convert_element_type.409, ...), kind=kOutput, calls=%fused_computation.29 | convolution fusion | flops 2533621760 | bytes 6471680 | tf_op jit(solution)/shard_map/dot_general | solution.py:39
  270.6 10.0 %collective-permute-done.19 = bf16[160,1024]{1,0:T(8,128)(2,1)S(1)} collective-permute-done((bf16[160,1024]{1,0:T(8,128)(2,1)S(1)}, bf16[160,1024]{1,0:T(8,128)(2,1)S(1)}, u32[]{:S(2)}, u32[]{:S(2)}) %collective-permute-start.19) | collective-permute-done | bytes 327712 | tf_op jit(solution)/shard_map/ppermute | solution.py:60
  284.4 2.8 add_convert_fusion
  288.6 10.5 %attend_back.2 = (f32[160,960]{1,0:T(8,128)S(1)}, bf16[1280,640]{1,0:T(8,128)(2,1)S(1)}) custom-call(bf16[160,960]{1,0:T(8,128)(2,1)S(1)} %copy.142.q_ref, bf16[1280,640]{1,0:T(8,128)(2,1)S(1)} %copy-done.3, bf16[160,960]{1,0:T(8,128)(2,1)S(1)} %pad_maximum_fusion.42.da_ref, f32[8,480]{1,0:T(8,128)S(1)} %get-tuple-element.48.lse_ref, ...), custom_call_target="tpu_custom_call" | custom-call | flops 7864320000 | bytes 6291456 | tf_op jit(solution)/shard_map/attend_back/pallas_call | solution.py:320
  307.3 4.4 collective-permute-done.24
  311.7 5.1 collective-permute-done.26
  329.0 4.2 convolution_convert_fusion.3.a_ref
  334.2 9.7 %collective-permute-done.27 = bf16[160,1024]{1,0:T(8,128)(2,1)S(1)} collective-permute-done((bf16[160,1024]{1,0:T(8,128)(2,1)S(1)}, bf16[160,1024]{1,0:T(8,128)(2,1)S(1)}, u32[]{:S(2)}, u32[]{:S(2)}) %collective-permute-start.27) | collective-permute-done | bytes 327712 | tf_op jit(solution)/shard_map/ppermute | solution.py:60
  348.4 2.8 fusion.93
  352.4 4.6 convolution_convert_fusion.5.c_ref
  357.0 4.5 convolution_convert_fusion.4
  366.8 6.9 %collective-permute-done.29.b_ref = bf16[1024,1408]{1,0:T(8,128)(2,1)} collective-permute-done((bf16[1024,1408]{1,0:T(8,128)(2,1)S(1)}, bf16[1024,1408]{1,0:T(8,128)(2,1)}, u32[]{:S(2)}, u32[]{:S(2)}) %collective-permute-start.29) | collective-permute-done | bytes 2883616 | tf_op jit(solution)/shard_map/ppermute | solution.py:60
  373.7 9.9 %merge_sum.1 = bf16[1024,3328]{1,0:T(8,128)(2,1)} custom-call(bf16[1024,1408]{1,0:T(8,128)(2,1)} %convolution_convert_fusion.3.a_ref, bf16[1024,1408]{1,0:T(8,128)(2,1)} %collective-permute-done.29.b_ref, bf16[1024,1920]{1,0:T(8,128)(2,1)} %convolution_convert_fusion.5.c_ref, bf16[1024,1920]{1,0:T(8,128)(2,1)} %collective-permute-done.30.d_ref), custom_call_target="tpu_custom_call" | custom-call | flops 6815744 | bytes 20447232 | tf_op jit(solution)/shard_map/merge_sum/pallas_call | solution.py:130
  385.1 10.6 %attend_back.3 = (f32[160,960]{1,0:T(8,128)S(1)}, bf16[1280,640]{1,0:T(8,128)(2,1)S(1)}) custom-call(bf16[160,960]{1,0:T(8,128)(2,1)S(1)} %copy.131.q_ref, bf16[1280,640]{1,0:T(8,128)(2,1)S(1)} %copy-done.1, bf16[160,960]{1,0:T(8,128)(2,1)S(1)} %pad_maximum_fusion.43.da_ref, f32[8,480]{1,0:T(8,128)S(1)} %get-tuple-element.59.lse_ref, ...), custom_call_target="tpu_custom_call" | custom-call | flops 7864320000 | bytes 6291456 | tf_op jit(solution)/shard_map/attend_back/pallas_call | solution.py:320
  406.2 3.8 collective-permute-done.32
  419.9 4.2 convolution_convert_fusion
  424.2 4.2 convolution_convert_fusion.1
  428.9 5.3 collective-permute-done.37
  434.2 3.5 add_convert_fusion.1
  439.8 3.0 collective-permute-start.44
  448.3 3.5 collective-permute-done.44
  452.1 6.0 %collective-permute-done.46 = bf16[4,64,640]{2,1,0:T(8,128)(2,1)} collective-permute-done((bf16[4,64,640]{2,1,0:T(8,128)(2,1)}, bf16[4,64,640]{2,1,0:T(8,128)(2,1)}, u32[]{:S(2)}, u32[]{:S(2)}) %collective-permute-start.46) | collective-permute-done | bytes 327712 | tf_op jit(solution)/shard_map/ppermute | solution.py:91
  464.4 3.5 collective-permute-done.40
  467.9 2.8 collective-permute-done.39
  474.7 4.2 collective-permute-done.41
  491.6 5.3 %collective-permute-start.53 = (bf16[64,1408]{1,0:T(8,128)(2,1)S(1)}, bf16[64,1408]{1,0:T(8,128)(2,1)S(1)}, u32[]{:S(2)}, u32[]{:S(2)}) collective-permute-start(bf16[64,1408]{1,0:T(8,128)(2,1)S(1)} %add_convert_fusion.9.m0), channel_id=1, source_target_pairs={{0,2},{2,0},{1,3},{3,1},{4,6},{6,4},{5,7},{7,5},{8,10},{10,8},{9,1... | collective-permute-start | bytes 540680 | tf_op jit(solution)/shard_map/ppermute | solution.py:60
  497.9 3.0 collective-permute-start.58
  502.3 4.9 collective-permute-done.58
  (517 shorter events, 215.8 us)
Async XLA Ops:
  7.2 75.3 %all-gather.3.cloned.1.call-start = ((), (), s32[]{:S(2)}) async-start(), calls=%async_computation.2 | async-start | bytes 7241728 | tf_op jit(solution)/shard_map/all_gather | solution.py:402
  15.6 132.9 %all-gather.5.cloned.1.call-start = ((), (), s32[]{:S(2)}) async-start(), calls=%async_computation.3 | async-start | bytes 7241728 | tf_op jit(solution)/shard_map/all_gather | solution.py:402
  16.8 366.8 %reduce-scatter.3.cloned.1.call-start = ((), (), s32[]{:S(2)}) async-start(), calls=%async_computation.4 | async-start | bytes 4177920 | tf_op jit(solution)/shard_map/reduce_scatter | solution.py:194
  86.2 17.8 %collective-permute-start = (bf16[1024,1408]{1,0:T(8,128)(2,1)}, bf16[1024,1408]{1,0:T(8,128)(2,1)S(1)}, u32[]{:S(2)}, u32[]{:S(2)}) collective-permute-start(bf16[1024,1408]{1,0:T(8,128)(2,1)} %slice.674), channel_id=1, source_target_pairs={{0,2},{2,0},{1,3},{3,1},{4,6},{6,4},{5,7},{7,5},{8,10},{10,8},{9,1... | collective-permute-start | bytes 8650760 | tf_op jit(solution)/shard_map/ppermute | solution.py:60
  99.8 61.7 %collective-permute-start.10 = (bf16[1024,1920]{1,0:T(8,128)(2,1)}, bf16[1024,1920]{1,0:T(8,128)(2,1)}, u32[]{:S(2)}, u32[]{:S(2)}) collective-permute-start(bf16[1024,1920]{1,0:T(8,128)(2,1)} %slice.690), channel_id=1, source_target_pairs={{0,2},{2,0},{1,3},{3,1},{4,6},{6,4},{5,7},{7,5},{8,10},{10,8},{9,1... | collective-permute-start | bytes 11796488 | tf_op jit(solution)/shard_map/ppermute | solution.py:60
  109.3 11.7 %collective-permute-start.1 = (bf16[160,640]{1,0:T(8,128)(2,1)S(1)}, bf16[160,640]{1,0:T(8,128)(2,1)S(1)}, u32[]{:S(2)}, u32[]{:S(2)}) collective-permute-start(bf16[160,640]{1,0:T(8,128)(2,1)S(1)} %get-tuple-element.115), channel_id=1, source_target_pairs={{0,1},{1,0},{4,5},{5,4},{2,3},{3,2},{6,7},{7,6},{8,9},{9,8},{12,13... | collective-permute-start | bytes 614408 | tf_op jit(solution)/shard_map/ppermute | solution.py:64
  111.8 9.6 %collective-permute-start.3 = (bf16[160,640]{1,0:T(8,128)(2,1)S(1)}, bf16[160,640]{1,0:T(8,128)(2,1)S(1)}, u32[]{:S(2)}, u32[]{:S(2)}) collective-permute-start(bf16[160,640]{1,0:T(8,128)(2,1)S(1)} %get-tuple-element.115), channel_id=1, source_target_pairs={{0,5},{1,4},{4,0},{5,1},{2,7},{3,6},{6,2},{7,3},{8,13},{9,12},{12,... | collective-permute-start | bytes 614408 | tf_op jit(solution)/shard_map/ppermute | solution.py:64
  112.9 11.2 %collective-permute-start.7 = (s32[160,2]{0,1:T(2,128)S(1)}, s32[160,2]{0,1:T(2,128)S(1)}, u32[]{:S(2)}, u32[]{:S(2)}) collective-permute-start(s32[160,2]{0,1:T(2,128)S(1)} %pad_add_fusion.1), channel_id=1, source_target_pairs={{0,5},{1,4},{4,0},{5,1},{2,7},{3,6},{6,2},{7,3},{8,13},{9,12},{12,... | collective-permute-start | bytes 3848 | tf_op jit(solution)/shard_map/ppermute | solution.py:64
  122.5 12.8 %collective-permute-start.4 = (bf16[640,640]{1,0:T(8,128)(2,1)}, bf16[640,640]{1,0:T(8,128)(2,1)}, u32[]{:S(2)}, u32[]{:S(2)}) collective-permute-start(bf16[640,640]{1,0:T(8,128)(2,1)} %pad_maximum_fusion.18), channel_id=1, source_target_pairs={{0,2},{2,0},{1,3},{3,1},{4,6},{6,4},{5,7},{7,5},{8,10},{10,8},{9,1... | collective-permute-start | bytes 2457608 | tf_op jit(solution)/shard_map/ppermute | solution.py:60
  147.1 10.5 %collective-permute-start.9 = (bf16[160,1024]{1,0:T(8,128)(2,1)S(1)}, bf16[160,1024]{1,0:T(8,128)(2,1)S(1)}, u32[]{:S(2)}, u32[]{:S(2)}) collective-permute-start(bf16[160,1024]{1,0:T(8,128)(2,1)S(1)} %multiply_convert_fusion.18), channel_id=1, source_target_pairs={{0,1},{1,0},{2,3},{3,2},{4,5},{5,4},{6,7},{7,6},{8,9},{9,8},{10,11... | collective-permute-start | bytes 983048 | tf_op jit(solution)/shard_map/ppermute | solution.py:60
  150.6 30.5 %collective-permute-start.12 = (bf16[1024,1408]{1,0:T(8,128)(2,1)S(1)}, bf16[1024,1408]{1,0:T(8,128)(2,1)S(1)}, u32[]{:S(2)}, u32[]{:S(2)}) collective-permute-start(bf16[1024,1408]{1,0:T(8,128)(2,1)S(1)} %slice.709), channel_id=1, source_target_pairs={{0,2},{2,0},{1,3},{3,1},{4,6},{6,4},{5,7},{7,5},{8,10},{10,8},{9,1... | collective-permute-start | bytes 8650760 | tf_op jit(solution)/shard_map/ppermute | solution.py:60
  170.6 9.6 %collective-permute-start.11 = (bf16[160,1024]{1,0:T(8,128)(2,1)S(1)}, bf16[160,1024]{1,0:T(8,128)(2,1)S(1)}, u32[]{:S(2)}, u32[]{:S(2)}) collective-permute-start(bf16[160,1024]{1,0:T(8,128)(2,1)S(1)} %slice.991), channel_id=1, source_target_pairs={{0,1},{1,0},{2,3},{3,2},{4,5},{5,4},{6,7},{7,6},{8,9},{9,8},{10,11... | collective-permute-start | bytes 983048 | tf_op jit(solution)/shard_map/ppermute | solution.py:60
  173.4 60.9 %collective-permute-start.18 = (bf16[1024,1920]{1,0:T(8,128)(2,1)}, bf16[1024,1920]{1,0:T(8,128)(2,1)}, u32[]{:S(2)}, u32[]{:S(2)}) collective-permute-start(bf16[1024,1920]{1,0:T(8,128)(2,1)} %slice.723), channel_id=1, source_target_pairs={{0,2},{2,0},{1,3},{3,1},{4,6},{6,4},{5,7},{7,5},{8,10},{10,8},{9,1... | collective-permute-start | bytes 11796488 | tf_op jit(solution)/shard_map/ppermute | solution.py:60
  187.8 11.2 %collective-permute-start.14 = (bf16[160,640]{1,0:T(8,128)(2,1)S(1)}, bf16[160,640]{1,0:T(8,128)(2,1)S(1)}, u32[]{:S(2)}, u32[]{:S(2)}) collective-permute-start(bf16[160,640]{1,0:T(8,128)(2,1)S(1)} %get-tuple-element.111), channel_id=1, source_target_pairs={{0,4},{1,5},{4,1},{5,0},{2,6},{3,7},{6,3},{7,2},{8,12},{9,13},{12,... | collective-permute-start | bytes 614408 | tf_op jit(solution)/shard_map/ppermute | solution.py:64
  187.8 11.2 %collective-permute-start.13 = (bf16[160,640]{1,0:T(8,128)(2,1)S(1)}, bf16[160,640]{1,0:T(8,128)(2,1)S(1)}, u32[]{:S(2)}, u32[]{:S(2)}) collective-permute-start(bf16[160,640]{1,0:T(8,128)(2,1)S(1)} %get-tuple-element.111), channel_id=1, source_target_pairs={{0,1},{1,0},{4,5},{5,4},{2,3},{3,2},{6,7},{7,6},{8,9},{9,8},{12,13... | collective-permute-start | bytes 614408 | tf_op jit(solution)/shard_map/ppermute | solution.py:64
  188.2 10.8 %collective-permute-start.15 = (bf16[160,640]{1,0:T(8,128)(2,1)S(1)}, bf16[160,640]{1,0:T(8,128)(2,1)S(1)}, u32[]{:S(2)}, u32[]{:S(2)}) collective-permute-start(bf16[160,640]{1,0:T(8,128)(2,1)S(1)} %get-tuple-element.111), channel_id=1, source_target_pairs={{0,5},{1,4},{4,0},{5,1},{2,7},{3,6},{6,2},{7,3},{8,13},{9,12},{12,... | collective-permute-start | bytes 614408 | tf_op jit(solution)/shard_map/ppermute | solution.py:64
  200.1 9.3 %collective-permute-start.16 = (bf16[640,640]{1,0:T(8,128)(2,1)}, bf16[640,640]{1,0:T(8,128)(2,1)}, u32[]{:S(2)}, u32[]{:S(2)}) collective-permute-start(bf16[640,640]{1,0:T(8,128)(2,1)} %pad_maximum_fusion.19), channel_id=1, source_target_pairs={{0,2},{2,0},{1,3},{3,1},{4,6},{6,4},{5,7},{7,5},{8,10},{10,8},{9,1... | collective-permute-start | bytes 2457608 | tf_op jit(solution)/shard_map/ppermute | solution.py:60
  223.6 11.2 %collective-permute-start.17 = (bf16[160,1024]{1,0:T(8,128)(2,1)}, bf16[160,1024]{1,0:T(8,128)(2,1)}, u32[]{:S(2)}, u32[]{:S(2)}) collective-permute-start(bf16[160,1024]{1,0:T(8,128)(2,1)} %multiply_convert_fusion.16), channel_id=1, source_target_pairs={{0,1},{1,0},{2,3},{3,2},{4,5},{5,4},{6,7},{7,6},{8,9},{9,8},{10,11... | collective-permute-start | bytes 983048 | tf_op jit(solution)/shard_map/ppermute | solution.py:60
  231.5 10.8 %collective-permute-start.20 = (bf16[160,1024]{1,0:T(8,128)(2,1)S(1)}, bf16[160,1024]{1,0:T(8,128)(2,1)S(1)}, u32[]{:S(2)}, u32[]{:S(2)}) collective-permute-start(bf16[160,1024]{1,0:T(8,128)(2,1)S(1)} %convert_element_type.409), channel_id=1, source_target_pairs={{0,1},{1,0},{2,3},{3,2},{4,5},{5,4},{6,7},{7,6},{8,9},{9,8},{10,11... | collective-permute-start | bytes 983048 | tf_op jit(solution)/shard_map/ppermute | solution.py:60
  251.5 13.5 %collective-permute-start.21 = (bf16[160,1024]{1,0:T(8,128)(2,1)S(1)}, bf16[160,1024]{1,0:T(8,128)(2,1)S(1)}, u32[]{:S(2)}, u32[]{:S(2)}) collective-permute-start(bf16[160,1024]{1,0:T(8,128)(2,1)S(1)} %slice.989), channel_id=1, source_target_pairs={{0,1},{1,0},{2,3},{3,2},{4,5},{5,4},{6,7},{7,6},{8,9},{9,8},{10,11... | collective-permute-start | bytes 983048 | tf_op jit(solution)/shard_map/ppermute | solution.py:60
  265.0 19.3 %collective-permute-start.22 = (bf16[1024,1920]{1,0:T(8,128)(2,1)S(1)}, bf16[1024,1920]{1,0:T(8,128)(2,1)S(1)}, u32[]{:S(2)}, u32[]{:S(2)}) collective-permute-start(bf16[1024,1920]{1,0:T(8,128)(2,1)S(1)} %convolution_convert_fusion.6), channel_id=1, source_target_pairs={{0,2},{2,0},{1,3},{3,1},{4,6},{6,4},{5,7},{7,5},{8,10},{10,8},{9,1... | collective-permute-start | bytes 11796488 | tf_op jit(solution)/shard_map/ppermute | solution.py:60
  269.3 11.3 %collective-permute-start.19 = (bf16[160,1024]{1,0:T(8,128)(2,1)S(1)}, bf16[160,1024]{1,0:T(8,128)(2,1)S(1)}, u32[]{:S(2)}, u32[]{:S(2)}) collective-permute-start(bf16[160,1024]{1,0:T(8,128)(2,1)S(1)} %slice.990), channel_id=1, source_target_pairs={{0,1},{1,0},{2,3},{3,2},{4,5},{5,4},{6,7},{7,6},{8,9},{9,8},{10,11... | collective-permute-start | bytes 983048 | tf_op jit(solution)/shard_map/ppermute | solution.py:60
  304.4 12.3 %collective-permute-start.26 = (bf16[160,640]{1,0:T(8,128)(2,1)S(1)}, bf16[160,640]{1,0:T(8,128)(2,1)S(1)}, u32[]{:S(2)}, u32[]{:S(2)}) collective-permute-start(bf16[160,640]{1,0:T(8,128)(2,1)S(1)} %get-tuple-element.160), channel_id=1, source_target_pairs={{0,4},{1,5},{4,1},{5,0},{2,6},{3,7},{6,3},{7,2},{8,12},{9,13},{12,... | collective-permute-start | bytes 614408 | tf_op jit(solution)/shard_map/ppermute | solution.py:64
  306.5 10.3 %collective-permute-start.25 = (bf16[160,640]{1,0:T(8,128)(2,1)S(1)}, bf16[160,640]{1,0:T(8,128)(2,1)}, u32[]{:S(2)}, u32[]{:S(2)}) collective-permute-start(bf16[160,640]{1,0:T(8,128)(2,1)S(1)} %get-tuple-element.161), channel_id=1, source_target_pairs={{0,5},{1,4},{4,0},{5,1},{2,7},{3,6},{6,2},{7,3},{8,13},{9,12},{12,... | collective-permute-start | bytes 614408 | tf_op jit(solution)/shard_map/ppermute | solution.py:64
  307.3 179.7 %reduce-scatter.5.cloned.1.call-start = ((), (), s32[]{:S(2)}) async-start(), calls=%async_computation.5 | async-start | bytes 7241728 | tf_op jit(solution)/shard_map/reduce_scatter | solution.py:194
  333.2 10.6 %collective-permute-start.27 = (bf16[160,1024]{1,0:T(8,128)(2,1)S(1)}, bf16[160,1024]{1,0:T(8,128)(2,1)S(1)}, u32[]{:S(2)}, u32[]{:S(2)}) collective-permute-start(bf16[160,1024]{1,0:T(8,128)(2,1)S(1)} %convert_element_type.430), channel_id=1, source_target_pairs={{0,1},{1,0},{2,3},{3,2},{4,5},{5,4},{6,7},{7,6},{8,9},{9,8},{10,11... | collective-permute-start | bytes 983048 | tf_op jit(solution)/shard_map/ppermute | solution.py:60
  351.3 10.2 %collective-permute-start.28 = (bf16[160,1024]{1,0:T(8,128)(2,1)S(1)}, bf16[160,1024]{1,0:T(8,128)(2,1)S(1)}, u32[]{:S(2)}, u32[]{:S(2)}) collective-permute-start(bf16[160,1024]{1,0:T(8,128)(2,1)S(1)} %slice.988), channel_id=1, source_target_pairs={{0,1},{1,0},{2,3},{3,2},{4,5},{5,4},{6,7},{7,6},{8,9},{9,8},{10,11... | collective-permute-start | bytes 983048 | tf_op jit(solution)/shard_map/ppermute | solution.py:60
  361.5 12.2 %collective-permute-start.30 = (bf16[1024,1920]{1,0:T(8,128)(2,1)S(1)}, bf16[1024,1920]{1,0:T(8,128)(2,1)}, u32[]{:S(2)}, u32[]{:S(2)}) collective-permute-start(bf16[1024,1920]{1,0:T(8,128)(2,1)S(1)} %convolution_convert_fusion.4), channel_id=1, source_target_pairs={{0,2},{2,0},{1,3},{3,1},{4,6},{6,4},{5,7},{7,5},{8,10},{10,8},{9,1... | collective-permute-start | bytes 11796488 | tf_op jit(solution)/shard_map/ppermute | solution.py:60
  363.0 10.7 %collective-permute-start.29 = (bf16[1024,1408]{1,0:T(8,128)(2,1)S(1)}, bf16[1024,1408]{1,0:T(8,128)(2,1)}, u32[]{:S(2)}, u32[]{:S(2)}) collective-permute-start(bf16[1024,1408]{1,0:T(8,128)(2,1)S(1)} %convolution_convert_fusion.2), channel_id=1, source_target_pairs={{0,2},{2,0},{1,3},{3,1},{4,6},{6,4},{5,7},{7,5},{8,10},{10,8},{9,1... | collective-permute-start | bytes 8650760 | tf_op jit(solution)/shard_map/ppermute | solution.py:60
  398.6 11.5 %collective-permute-start.32 = (bf16[160,640]{1,0:T(8,128)(2,1)S(1)}, bf16[160,640]{1,0:T(8,128)(2,1)S(1)}, u32[]{:S(2)}, u32[]{:S(2)}) collective-permute-start(bf16[160,640]{1,0:T(8,128)(2,1)S(1)} %get-tuple-element.156), channel_id=1, source_target_pairs={{0,1},{1,0},{4,5},{5,4},{2,3},{3,2},{6,7},{7,6},{8,9},{9,8},{12,13... | collective-permute-start | bytes 614408 | tf_op jit(solution)/shard_map/ppermute | solution.py:64
  400.8 11.8 %collective-permute-start.34 = (bf16[160,640]{1,0:T(8,128)(2,1)S(1)}, bf16[160,640]{1,0:T(8,128)(2,1)S(1)}, u32[]{:S(2)}, u32[]{:S(2)}) collective-permute-start(bf16[160,640]{1,0:T(8,128)(2,1)S(1)} %get-tuple-element.157), channel_id=1, source_target_pairs={{0,4},{1,5},{4,1},{5,0},{2,6},{3,7},{6,3},{7,2},{8,12},{9,13},{12,... | collective-permute-start | bytes 614408 | tf_op jit(solution)/shard_map/ppermute | solution.py:64
  401.2 12.3 %collective-permute-start.33 = (bf16[160,640]{1,0:T(8,128)(2,1)S(1)}, bf16[160,640]{1,0:T(8,128)(2,1)S(1)}, u32[]{:S(2)}, u32[]{:S(2)}) collective-permute-start(bf16[160,640]{1,0:T(8,128)(2,1)S(1)} %get-tuple-element.158), channel_id=1, source_target_pairs={{0,5},{1,4},{4,0},{5,1},{2,7},{3,6},{6,2},{7,3},{8,13},{9,12},{12,... | collective-permute-start | bytes 614408 | tf_op jit(solution)/shard_map/ppermute | solution.py:64
  405.4 23.0 %collective-permute-start.36 = (bf16[64,1920]{1,0:T(8,128)(2,1)}, bf16[64,1920]{1,0:T(8,128)(2,1)}, u32[]{:S(2)}, u32[]{:S(2)}) collective-permute-start(bf16[64,1920]{1,0:T(8,128)(2,1)} %add_convert_fusion.7), channel_id=1, source_target_pairs={{0,2},{2,0},{1,3},{3,1},{4,6},{6,4},{5,7},{7,5},{8,10},{10,8},{9,1... | collective-permute-start | bytes 737288 | tf_op jit(solution)/shard_map/ppermute | solution.py:60
  439.8 12.0 %collective-permute-start.44 = (bf16[4,64,640]{2,1,0:T(8,128)(2,1)}, bf16[4,64,640]{2,1,0:T(8,128)(2,1)}, u32[]{:S(2)}, u32[]{:S(2)}) collective-permute-start(bf16[4,64,640]{2,1,0:T(8,128)(2,1)} %get-tuple-element.147), channel_id=1, source_target_pairs={{0,64},{32,96},{64,0},{96,32},{1,65},{33,97},{65,1},{97,33},{2,66}... | collective-permute-start | bytes 983048 | tf_op jit(solution)/shard_map/ppermute | solution.py:91
  442.8 15.3 %collective-permute-start.46 = (bf16[4,64,640]{2,1,0:T(8,128)(2,1)}, bf16[4,64,640]{2,1,0:T(8,128)(2,1)}, u32[]{:S(2)}, u32[]{:S(2)}) collective-permute-start(bf16[4,64,640]{2,1,0:T(8,128)(2,1)} %get-tuple-element.148), channel_id=1, source_target_pairs={{0,96},{32,0},{64,32},{96,64},{1,97},{33,1},{65,33},{97,65},{2,98}... | collective-permute-start | bytes 983048 | tf_op jit(solution)/shard_map/ppermute | solution.py:91
  443.6 15.6 %collective-permute-start.45 = (bf16[4,64,640]{2,1,0:T(8,128)(2,1)}, bf16[4,64,640]{2,1,0:T(8,128)(2,1)}, u32[]{:S(2)}, u32[]{:S(2)}) collective-permute-start(bf16[4,64,640]{2,1,0:T(8,128)(2,1)} %get-tuple-element.149), channel_id=1, source_target_pairs={{0,32},{32,64},{64,96},{96,0},{1,33},{33,65},{65,97},{97,1},{2,34}... | collective-permute-start | bytes 983048 | tf_op jit(solution)/shard_map/ppermute | solution.py:91
  445.7 18.0 %collective-permute-start.38 = (bf16[4,64,768]{2,1,0:T(8,128)(2,1)S(1)}, bf16[4,64,768]{2,1,0:T(8,128)(2,1)S(1)}, u32[]{:S(2)}, u32[]{:S(2)}) collective-permute-start(bf16[4,64,768]{2,1,0:T(8,128)(2,1)S(1)} %get-tuple-element.132), channel_id=1, source_target_pairs={{0,16},{8,24},{16,0},{24,8},{1,17},{9,25},{17,1},{25,9},{2,18},{10... | collective-permute-start | bytes 1179656 | tf_op jit(solution)/shard_map/ppermute | solution.py:91
  447.2 20.8 %collective-permute-start.40 = (bf16[4,64,768]{2,1,0:T(8,128)(2,1)S(1)}, bf16[4,64,768]{2,1,0:T(8,128)(2,1)}, u32[]{:S(2)}, u32[]{:S(2)}) collective-permute-start(bf16[4,64,768]{2,1,0:T(8,128)(2,1)S(1)} %get-tuple-element.133), channel_id=1, source_target_pairs={{0,24},{8,0},{16,8},{24,16},{1,25},{9,1},{17,9},{25,17},{2,26},{10... | collective-permute-start | bytes 1179656 | tf_op jit(solution)/shard_map/ppermute | solution.py:91
  451.8 18.9 %collective-permute-start.39 = (bf16[4,64,768]{2,1,0:T(8,128)(2,1)S(1)}, bf16[4,64,768]{2,1,0:T(8,128)(2,1)}, u32[]{:S(2)}, u32[]{:S(2)}) collective-permute-start(bf16[4,64,768]{2,1,0:T(8,128)(2,1)S(1)} %get-tuple-element.134), channel_id=1, source_target_pairs={{0,8},{8,16},{16,24},{24,0},{1,9},{9,17},{17,25},{25,1},{2,10},{10... | collective-permute-start | bytes 1179656 | tf_op jit(solution)/shard_map/ppermute | solution.py:91
  460.7 13.1 %collective-permute-start.47 = (bf16[64,640]{1,0:T(8,128)(2,1)S(1)}, bf16[64,640]{1,0:T(8,128)(2,1)S(1)}, u32[]{:S(2)}, u32[]{:S(2)}) collective-permute-start(bf16[64,640]{1,0:T(8,128)(2,1)S(1)} %get-tuple-element.182), channel_id=1, source_target_pairs={{0,16},{8,24},{16,0},{24,8},{1,17},{9,25},{17,1},{25,9},{2,18},{10... | collective-permute-start | bytes 245768 | tf_op jit(solution)/shard_map/ppermute | solution.py:91
  462.9 10.9 %collective-permute-start.49 = (bf16[64,640]{1,0:T(8,128)(2,1)S(1)}, bf16[64,640]{1,0:T(8,128)(2,1)S(1)}, u32[]{:S(2)}, u32[]{:S(2)}) collective-permute-start(bf16[64,640]{1,0:T(8,128)(2,1)S(1)} %get-tuple-element.183), channel_id=1, source_target_pairs={{0,24},{8,0},{16,8},{24,16},{1,25},{9,1},{17,9},{25,17},{2,26},{10... | collective-permute-start | bytes 245768 | tf_op jit(solution)/shard_map/ppermute | solution.py:91
  463.7 10.9 %collective-permute-start.48 = (bf16[64,640]{1,0:T(8,128)(2,1)S(1)}, bf16[64,640]{1,0:T(8,128)(2,1)S(1)}, u32[]{:S(2)}, u32[]{:S(2)}) collective-permute-start(bf16[64,640]{1,0:T(8,128)(2,1)S(1)} %get-tuple-element.184), channel_id=1, source_target_pairs={{0,8},{8,16},{16,24},{24,0},{1,9},{9,17},{17,25},{25,1},{2,10},{10... | collective-permute-start | bytes 245768 | tf_op jit(solution)/shard_map/ppermute | solution.py:91
  488.1 12.8 %collective-permute-start.55 = (bf16[64,1408]{1,0:T(8,128)(2,1)S(1)}, bf16[64,1408]{1,0:T(8,128)(2,1)S(1)}, u32[]{:S(2)}, u32[]{:S(2)}) collective-permute-start(bf16[64,1408]{1,0:T(8,128)(2,1)S(1)} %slice.764), channel_id=1, source_target_pairs={{0,4},{1,5},{4,1},{5,0},{2,6},{3,7},{6,3},{7,2},{8,12},{9,13},{12,... | collective-permute-start | bytes 540680 | tf_op jit(solution)/shard_map/ppermute | solution.py:64
  489.1 11.8 %collective-permute-start.54 = (bf16[64,1408]{1,0:T(8,128)(2,1)S(1)}, bf16[64,1408]{1,0:T(8,128)(2,1)S(1)}, u32[]{:S(2)}, u32[]{:S(2)}) collective-permute-start(bf16[64,1408]{1,0:T(8,128)(2,1)S(1)} %slice.764), channel_id=1, source_target_pairs={{0,1},{1,0},{4,5},{5,4},{2,3},{3,2},{6,7},{7,6},{8,9},{9,8},{12,13... | collective-permute-start | bytes 540680 | tf_op jit(solution)/shard_map/ppermute | solution.py:64
  490.2 10.7 %collective-permute-start.56 = (bf16[64,1408]{1,0:T(8,128)(2,1)S(1)}, bf16[64,1408]{1,0:T(8,128)(2,1)S(1)}, u32[]{:S(2)}, u32[]{:S(2)}) collective-permute-start(bf16[64,1408]{1,0:T(8,128)(2,1)S(1)} %slice.764), channel_id=1, source_target_pairs={{0,5},{1,4},{4,0},{5,1},{2,7},{3,6},{6,2},{7,3},{8,13},{9,12},{12,... | collective-permute-start | bytes 540680 | tf_op jit(solution)/shard_map/ppermute | solution.py:64
  491.6 19.4 %collective-permute-start.53 = (bf16[64,1408]{1,0:T(8,128)(2,1)S(1)}, bf16[64,1408]{1,0:T(8,128)(2,1)S(1)}, u32[]{:S(2)}, u32[]{:S(2)}) collective-permute-start(bf16[64,1408]{1,0:T(8,128)(2,1)S(1)} %add_convert_fusion.9.m0), channel_id=1, source_target_pairs={{0,2},{2,0},{1,3},{3,1},{4,6},{6,4},{5,7},{7,5},{8,10},{10,8},{9,1... | collective-permute-start | bytes 540680 | tf_op jit(solution)/shard_map/ppermute | solution.py:60
  497.9 9.3 %collective-permute-start.58 = (bf16[64,1920]{1,0:T(8,128)(2,1)S(1)}, bf16[64,1920]{1,0:T(8,128)(2,1)S(1)}, u32[]{:S(2)}, u32[]{:S(2)}) collective-permute-start(bf16[64,1920]{1,0:T(8,128)(2,1)S(1)} %slice.765), channel_id=1, source_target_pairs={{0,4},{4,0},{1,5},{5,1},{2,6},{6,2},{3,7},{7,3},{8,12},{12,8},{9,1... | collective-permute-start | bytes 737288 | tf_op jit(solution)/shard_map/ppermute | solution.py:60
  501.0 10.1 %collective-permute-start.57 = (bf16[64,1408]{1,0:T(8,128)(2,1)S(1)}, bf16[64,1408]{1,0:T(8,128)(2,1)S(1)}, u32[]{:S(2)}, u32[]{:S(2)}) collective-permute-start(bf16[64,1408]{1,0:T(8,128)(2,1)S(1)} %add_convert_fusion.8.m1), channel_id=1, source_target_pairs={{0,2},{2,0},{1,3},{3,1},{4,6},{6,4},{5,7},{7,5},{8,10},{10,8},{9,1... | collective-permute-start | bytes 540680 | tf_op jit(solution)/shard_map/ppermute | solution.py:60
  (110 other events, 688.6 us)
Sparse Core Ops, SparseCore 0:
  15.8 66.6 all-gather.2
  85.2 63.2 all-gather.4
  307.4 73.6 reduce-scatter.2
  384.4 96.0 reduce-scatter.4

commit v4 on v3

--- a/solution.py
+++ b/solution.py
@@ -101,10 +101,6 @@
     return jnp.concatenate([first, second], axis=1)
 
 
-def core_sum(keep, give):
-    return (keep.astype(F32) + swap(give.astype(BF), "core").astype(F32)).astype(BF)
-
-
 def low_sum(part):
     part = part.astype(BF)
     return (part.astype(F32) + swap(part, "zl").astype(F32)).astype(BF)
@@ -116,78 +112,97 @@
     return ((part.astype(F32) + two) + (one + three)).astype(BF)
 
 
-def merge_kernel(a_ref, b_ref, c_ref, d_ref, out_ref):
-    width = a_ref.shape[1]
-    out_ref[:, :width] = (a_ref[...].astype(F32) + b_ref[...].astype(F32)).astype(BF)
-    out_ref[:, width:] = (c_ref[...].astype(F32) + d_ref[...].astype(F32)).astype(BF)
-
-
-def merge_sum(first, second):
-    left, right = first[0].shape[1], second[0].shape[1]
-    block = 128
-    narrow = pl.BlockSpec((block, left), lambda i: (i, 0))
-    broad = pl.BlockSpec((block, right), lambda i: (i, 0))
+def grads_kernel(plan, *refs):
+    out_ref = refs[-1]
+    for at, start, stop in plan["dots"]:
+        part = by_rows(refs[at][...], refs[at + 1][...])
+        for low, high, extra in plan["spans"]:
+            if extra is not None and low <= start and stop <= high:
+                part = part + refs[extra][:, start - low : stop - low].astype(F32)
+        out_ref[:, start:stop] = part.astype(BF)
+
+
+def weight_grads(sections):
+    operands, dots, spans, base = [], [], [], 0
+    for pairs, extra in sections:
+        start = base
+        for left, right in pairs:
+            dots.append((len(operands), base, base + right.shape[1]))
+            operands += [left, right]
+            base += right.shape[1]
+        spans.append((start, base, None if extra is None else len(operands)))
+        if extra is not None:
+            operands.append(extra)
+    plan = {"dots": dots, "spans": spans}
+
+    def kernel(*refs):
+        grads_kernel(plan, *refs)
+
     return pl.pallas_call(
-        merge_kernel,
-        grid=(DP // block,),
-        out_shape=jax.ShapeDtypeStruct((DP, left + right), BF),
-        in_specs=[narrow, narrow, broad, broad],
-        out_specs=pl.BlockSpec((block, left + right), lambda i: (i, 0)),
+        kernel,
+        out_shape=jax.ShapeDtypeStruct((DP, base), BF),
+        in_specs=[VM] * len(operands),
+        out_specs=VM,
+        compiler_params=pltpu.CompilerParams(vmem_limit_bytes=48 * 2**20),
         cost_estimate=pl.CostEstimate(
-            flops=2 * DP * (left + right),
-            bytes_accessed=6 * DP * (left + right),
-            transcendentals=0,
+            flops=2 * DP * base * 640, bytes_accessed=4 * DP * base, transcendentals=0
         ),
-        name="merge_sum",
-    )(first[0], swap(first[1], "core"), second[0], swap(second[1], "core"))
-
-
-def write_kernel(flag_ref, m0, o0, m1, o1, q_ref, k_ref, v_ref, w_ref, gain_ref, qkv_ref, out_ref):
+        name="weight_grads",
+    )(*operands)
+
+
+def write_kernel(flag_ref, *refs):
+    ins, outs, gain_ref, qkv_ref, out_ref = refs[:10], refs[10:17], *refs[17:]
     first = flag_ref[0] == 0
+    shape = (8, OUT_PAD - OUT_HALF)
     chooser = (
-        lax.broadcasted_iota(jnp.int32, (8, OUT_PAD - OUT_HALF), 0)
-        == lax.broadcasted_iota(jnp.int32, (8, OUT_PAD - OUT_HALF), 1)
+        lax.broadcasted_iota(jnp.int32, shape, 0) == lax.broadcasted_iota(jnp.int32, shape, 1)
     ).astype(BF)
-    for layer, (mine, other) in enumerate(((m0, o0), (m1, o1))):
-        low = jnp.where(first, mine[...], other[...]).astype(F32)
-        high = jnp.where(first, other[...], mine[...]).astype(F32)
-        qkv_ref[:, :QKV_HALF] = low[:, :QKV_HALF]
-        qkv_ref[:, QKV_HALF:] = high[:, :QKV_HALF]
-        out_ref[:, :OUT_HALF] = low[:, QKV_PAD : QKV_PAD + OUT_HALF]
-        out_ref[:, OUT_HALF:] = high[:, QKV_PAD : QKV_PAD + OUT_HALF]
-        q_ref[layer] = qkv_ref[:PER, :QW]
-        k_ref[layer] = qkv_ref[:PER, QW : QW + KVW]
-        v_ref[layer] = qkv_ref[:PER, QW + KVW :]
-        w_ref[layer] = out_ref[:PER, :]
-        low = low.astype(BF)
-        for at, start in enumerate((QKV_HALF, QKV_PAD + OUT_HALF)):
-            gain_ref[at * 2 + layer] = by_columns(
-                chooser, low[:, start : start + OUT_PAD - OUT_HALF]
-            )
+    hid = ins[4].shape[1] // 3
+
+    def both(pair, start, width):
+        mine, other = ins[pair][:, start : start + width], ins[pair + 1][:, start : start + width]
+        low, high = jnp.where(first, mine, other), jnp.where(first, other, mine)
+        return low.astype(F32), high.astype(F32)
+
+    def gain(slot, pair, start):
+        low = both(pair, start, OUT_PAD - OUT_HALF)[0]
+        gain_ref[slot] = by_columns(chooser, low.astype(BF))
+
+    for layer, (pair, start) in enumerate(((4, 0), (8, 0))):
+        for at in range(3):
+            low, high = both(pair, at * hid, hid)
+            outs[4 + at][:, layer, :hid] = low[:PER]
+            outs[4 + at][:, layer, hid:] = high[:PER]
+    for layer, (pair, start) in enumerate(((2, QKV_PAD), (6, 0))):
+        low, high = both(pair, start, OUT_HALF)
+        out_ref[:, :OUT_HALF] = low
+        out_ref[:, OUT_HALF:] = high
+        outs[3][:, layer, :] = out_ref[:PER, :]
+        gain(2 + layer, pair, start + OUT_HALF)
+    for layer, pair in enumerate((0, 2)):
+        low, high = both(pair, 0, QKV_HALF)
+        qkv_ref[:, :QKV_HALF] = low
+        qkv_ref[:, QKV_HALF:] = high
+        outs[0][:, layer, :] = qkv_ref[:PER, :QW]
+        outs[1][:, layer, :] = qkv_ref[:PER, QW : QW + KVW]
+        outs[2][:, layer, :] = qkv_ref[:PER, QW + KVW :]
+        gain(layer, pair, QKV_HALF)
 
 
 def write_grads(flag, parts):
-    shapes = [(2, PER, QW), (2, PER, KVW), (2, PER, KVW), (2, PER, QW), (4, 8, PAD)]
-    return pl.pallas_call(
+    hid = parts[4].shape[1] // 3
+    shapes = [(PER, 2, width) for width in (QW, KVW, KVW, QW, 2 * hid, 2 * hid, 2 * hid)]
+    outs = pl.pallas_call(
         write_kernel,
-        out_shape=tuple(jax.ShapeDtypeStruct(shape, F32) for shape in shapes),
-        in_specs=[pl.BlockSpec(memory_space=pltpu.SMEM)] + [VM] * 4,
-        out_specs=(VM,) * 5,
+        out_shape=tuple(jax.ShapeDtypeStruct(shape, F32) for shape in shapes + [(4, 8, PAD)]),
+        in_specs=[pl.BlockSpec(memory_space=pltpu.SMEM)] + [VM] * 10,
+        out_specs=(VM,) * 8,
         scratch_shapes=[pltpu.VMEM((PAD, QW + 2 * KVW), F32), pltpu.VMEM((PAD, QW), F32)],
-        compiler_params=pltpu.CompilerParams(vmem_limit_bytes=32 * 2**20),
+        compiler_params=pltpu.CompilerParams(vmem_limit_bytes=40 * 2**20),
         name="write_grads",
     )(flag, *parts)
-
-
-def diagonal(lefts, rights):
-    tall = jnp.concatenate(lefts, axis=0)
-    width = sum(right.shape[1] for right in rights)
-    blocks, at = [], 0
-    for right in rights:
-        left_over = width - at - right.shape[1]
-        blocks.append(jnp.pad(right, ((0, 0), (at, left_over))))
-        at += right.shape[1]
-    return by_rows(tall, jnp.concatenate(blocks, axis=0)).astype(BF)
+    return [jnp.swapaxes(out, 0, 1) for out in outs[:7]] + [outs[7]]
 
 
 def scatter_plane(total):
@@ -516,13 +531,11 @@
             ).astype(BF)
             grad_gu = jnp.concatenate([grad_gate_in, grad_up_in], axis=1)
             partial = partial + by_columns(grad_gu, gu)
-            ffn_grads.append(diagonal([normed_pair, grad_pair], [grad_gu, hidden]))
+            ffn_grads.append([(normed_pair, grad_gu), (grad_pair, hidden)])
         arrived = swap(partial[rows:].astype(BF), "tp")
-        arrived, ffn_grads = lax.optimization_barrier((arrived, ffn_grads))
-        if layer > 0:
-            ffn_sum = core_sum(ffn_grads[0], ffn_grads[1])
-        else:
-            later_sum = merge_sum(att_pair, ffn_grads)
+        ffn_give = weight_grads([(ffn_grads[1], None)])
+        arrived, ffn_give = lax.optimization_barrier((arrived, ffn_give))
+        ffn_got = swap(ffn_give, "core")
         grad_normed_two = partial[:rows] + arrived.astype(F32)
         grad_mixed_norm, gain_two_terms = rms_backward(
             mixed, scale_two, gain_twos[layer], grad_normed_two
@@ -532,18 +545,33 @@
         grad_attended_b = join(
             product(grad_mixed_b, out_m)[:, :OUT_HALF], product(grad_mixed_b, out_o)[:, :OUT_HALF]
         ).astype(BF)
-        if layer > 0:
-            ffn_sum, grad_attended_b = lax.optimization_barrier((ffn_sum, grad_attended_b))
-            ffn_done = scatter_plane(ffn_sum)
-        else:
-            later_sum, grad_attended_b, ffn_done = lax.optimization_barrier(
-                (later_sum, grad_attended_b, ffn_done)
-            )
-            later = scatter_plane(later_sum)
+        ones = jnp.ones((rows, OUT_PAD - OUT_HALF), BF)
+        out_pairs = [
+            [(grad_mixed_b, att_part), (gain_two_terms, ones)] for att_part in (att_m, att_o)
+        ]
+        out_give = weight_grads([(out_pairs[1], None)])
+        out_give, grad_attended_b = lax.optimization_barrier((out_give, grad_attended_b))
+        out_got = swap(out_give, "core")
         grad_query, key_value_terms = attention_back(
             query, key_value, grad_attended_b, log_totals, codes
         )
+        key_value_terms, out_got, ffn_got = lax.optimization_barrier(
+            (key_value_terms, out_got, ffn_got)
+        )
+        sections = [(out_pairs[0], out_got), (ffn_grads[0], ffn_got)]
+        if layer > 0:
+            group_one = weight_grads(sections)
+        else:
+            group_two = weight_grads([(pairs_one[0], got_one)] + sections)
         key_value_grad = scatter_group(key_value_terms)
+        if layer > 0:
+            key_value_grad, group_one = lax.optimization_barrier((key_value_grad, group_one))
+            done_one = scatter_plane(group_one)
+        else:
+            key_value_grad, group_two, done_one = lax.optimization_barrier(
+                (key_value_grad, group_two, done_one)
+            )
+            done_two = scatter_plane(group_two)
         grad_qkv = jnp.concatenate(
             [
                 rotate(
@@ -564,45 +592,37 @@
             layer_input, scale_one, gain_ones[layer], grad_normed_one
         )
         grad_stream = grad_mixed + grad_input_norm
-        ones = jnp.ones((rows, OUT_PAD - OUT_HALF), BF)
-        att_grads = [
-            diagonal(
-                [normed_one, gain_one_terms, grad_mixed_b, gain_two_terms],
-                [
-                    grad_part[:, :QKV_HALF],
-                    jnp.ones((rows, QKV_PAD - QKV_HALF), BF),
-                    att_part,
-                    ones,
-                ],
-            )
-            for grad_part, att_part in ((grad_m, att_m), (grad_o, att_o))
+        wide_ones = jnp.ones((rows, QKV_PAD - QKV_HALF), BF)
+        pairs = [
+            [(normed_one, part[:, :QKV_HALF]), (gain_one_terms, wide_ones)]
+            for part in (grad_m, grad_o)
         ]
+        give = weight_grads([(pairs[1], None)])
+        grad_stream, give = lax.optimization_barrier((grad_stream, give))
+        got = swap(give, "core")
         if layer > 0:
-            grad_stream, att_pair = lax.optimization_barrier((grad_stream, att_grads))
-        else:
-            ffn_one = low_sum(ffn_done)
-            ffn_one = (ffn_one, swap(ffn_one, "core"))
-            att_grads, ffn_one = lax.optimization_barrier((att_grads, ffn_one))
-            att_zero = z_sum(plane_scatter(core_sum(att_grads[0], att_grads[1]), 768))
-            att_one = z_sum(later[:, :ATT])
-            ffn_zero = low_sum(later[:, ATT:])
-            ffn_zero = (ffn_zero, swap(ffn_zero, "core"))
-
-    query_grads, key_grads, value_grads, out_grads, gain_grads = write_grads(
-        lax.axis_index("core").astype(jnp.int32).reshape(1),
-        (att_zero, swap(att_zero, "core"), att_one, swap(att_one, "core")),
-    )
-    ffn_outs = [
-        jnp.stack(
-            [
-                join(
-                    mine[:PER, at * hid : (at + 1) * hid], other[:PER, at * hid : (at + 1) * hid]
-                ).astype(F32)
-                for mine, other in (ffn_zero, ffn_one)
-            ]
-        )
-        for at in range(3)
-    ]
+            pairs_one, got_one = pairs, got
+
+    out_one = z_sum(done_one[:, :OUT_PAD])
+    ffn_one = low_sum(done_one[:, OUT_PAD:])
+    total = weight_grads([(pairs[0], got)])
+    total, out_one, ffn_one = lax.optimization_barrier((total, out_one, ffn_one))
+    att_zero = z_sum(plane_scatter(total, 512))
+    att_one = z_sum(done_two[:, :ATT])
+    ffn_zero = low_sum(done_two[:, ATT:])
+    parts = []
+    for part in (att_zero, att_one, ffn_zero, out_one, ffn_one):
+        parts += [part, swap(part, "core")]
+    (
+        query_grads,
+        key_grads,
+        value_grads,
+        out_grads,
+        gate_grads,
+        up_grads,
+        down_grads,
+        gain_grads,
+    ) = write_grads(lax.axis_index("core").astype(jnp.int32).reshape(1), parts)
     return (
         block_out,
         cut_features(grad_stream),
@@ -612,7 +632,10 @@
         value_grads,
         out_grads,
         gain_grads[2:, 0, :PER],
-    ) + tuple(ffn_outs)
+        gate_grads,
+        up_grads,
+        down_grads,
+    )
 
 
 def solution(mesh):

time: 539 us -> 549 us (1.019)
  matrix products: 90.2 us -> 62.1 us
  Pallas kernels: 43 us -> 64.8 us
  starting transfers between devices: 75.1 us -> 87.7 us
    dot_general x8 -> x0, matrix products: 35.3 us -> none  [by_rows(): lax.dot_general(left, right, (((0,), (0,)), ((), ())), preferred_element_...]
    reduce_scatter x2, waiting for transfers between devices: 0.01 us -> 24.2 us  [scatter_plane(): return lax.psum_scatter(total, XY, scatter_dimension=0, tiled=True)]
    pallas_call x1 -> x9, Pallas kernels: 9.94 us -> 30.1 us  [weight_grads(): pl.pallas_call(kernel, out_shape=jax.ShapeDtypeStruct((DP, base), BF), in...]
    ppermute x21 -> x24, waiting for transfers between devices: 33.8 us -> 23 us  [z_send(): return lax.ppermute(values, ('zl', 'tp'), z_ring(step))]
    ppermute x12, waiting for transfers between devices: 23.7 us -> 14.1 us  [line_scatter(): out = out + lax.ppermute(block, axis, ring(4, step)).astype(F32)]
    ppermute x27 -> x30, waiting for transfers between devices: 57.1 us -> 50.5 us  [swap(): return lax.ppermute(values, axis, [(0, 1), (1, 0)])]
    convert_element_type x2 -> x0, other arithmetic: 6.28 us -> none  [core_sum(): (keep.astype(F32) + swap(give.astype(BF), 'core').astype(F32)).astype(BF)]
    ppermute x21 -> x24, starting transfers between devices: 23.9 us -> 28.9 us  [z_send(): return lax.ppermute(values, ('zl', 'tp'), z_ring(step))]
  transfers between devices with their start and end apart: 64 -> 70, of which waited for: 31 -> 29; matrix products, arithmetic and copies ran while one was open for 32% -> 28% of each run, Pallas kernels for 6% -> 12%
where the time goes in v4:
time: 549 us; the launch traced here: 538 us
  waiting for transfers between devices  180 us (33%)
  local copies, waits for them, and re-layouts  88.7 us (16%)
  starting transfers between devices  87.7 us (16%)
  Pallas kernels  64.8 us (12%)
  matrix products  62.1 us (11%)
  other arithmetic  38.8 us (7%)
  between operations  16.1 us (3%)
    all_gather x2, waiting for transfers between devices, shards(): lax.all_gather(jnp.concatenate(packs[2 * layer:2 * layer + 2], axis=1), X...  68.2 us
    ppermute x30, waiting for transfers between devices, swap(): return lax.ppermute(values, axis, [(0, 1), (1, 0)])  50.5 us
    ppermute x30, starting transfers between devices, swap(): return lax.ppermute(values, axis, [(0, 1), (1, 0)])  41.6 us
    dot_general x17, matrix products, by_columns(): lax.dot_general(left, right, (((1,), (1,)), ((), ())), preferred_element_...  33 us
    pallas_call x9, Pallas kernels, weight_grads(): pl.pallas_call(kernel, out_shape=jax.ShapeDtypeStruct((DP, base), BF), in...  30.1 us
    dot_general x16, matrix products, product(): return jnp.dot(left, right, preferred_element_type=F32)  29.1 us
    unnamed x195, local copies, waits for them, and re-layouts  29 us
    ppermute x24, starting transfers between devices, z_send(): return lax.ppermute(values, ('zl', 'tp'), z_ring(step))  28.9 us
  transfers between devices with their start and end apart: 70, of which 29 were waited for; matrix products, arithmetic and copies ran while one was open for 28% of the time, Pallas kernels for 12%

profile of v4, /device:TPU:1, one launch (start us, length us, event | category | flops | bytes accessed | tf_op | source)
XLA Modules:
  0.0 538.3 jit_solution(11219804902588654194)
XLA Ops:
  16.0 65.7 %all-gather.3.cloned.1.call-done = bf16[1024,3328]{1,0:T(8,128)(2,1)} async-done(((bf16[64,3328]{1,0:T(8,128)(2,1)}), bf16[1024,3328]{1,0:T(8,128)(2,1)}) %all-gather.3.cloned.1.call-update) | async-done | bytes 6815760 | tf_op jit(solution)/shard_map/all_gather | solution.py:417
  81.7 3.6 slice.634
  89.9 4.3 slice.650
  104.1 2.6 collective-permute-start.1
  110.4 5.4 %collective-permute-done.1 = bf16[160,640]{1,0:T(8,128)(2,1)S(1)} collective-permute-done((bf16[160,640]{1,0:T(8,128)(2,1)S(1)}, bf16[160,640]{1,0:T(8,128)(2,1)S(1)}, u32[]{:S(2)}, u32[]{:S(2)}) %collective-permute-start.1) | collective-permute-done | bytes 204832 | tf_op jit(solution)/shard_map/ppermute | solution.py:64
  119.8 2.7 collective-permute-start.8
  133.9 5.8 %attend.2 = (bf16[160,960]{1,0:T(8,128)(2,1)S(1)}, f32[8,480]{1,0:T(8,128)S(1)}) custom-call(bf16[160,960]{1,0:T(8,128)(2,1)S(1)} %copy.106.q_ref, bf16[1280,640]{1,0:T(8,128)(2,1)S(1)} %copy-done.10, s32[1,480]{1,0:T(1,128)S(1)} %broadcast_in_dim_tile.6.sq, s32[1,480]{1,0:T(1,128)S(1)} %broadcast_in_dim_tile.7.pq, s32[1280,1]{1,0:T(8,128)S(1)} %copy.108.sk, ...), custom_call_target="tpu_custom_call" | custom-call | flops 3145728000 | bytes 4194304 | tf_op jit(solution)/shard_map/attend/pallas_call | solution.py:314
  145.0 2.6 all-gather.5.cloned.1.call-done
  150.4 4.4 collective-permute-done.9
  154.8 2.9 fusion.14
  158.0 3.1 fusion.10
  171.3 4.8 collective-permute-done.11
  180.6 2.7 copy.90
  192.6 8.5 %collective-permute-done.14 = bf16[160,640]{1,0:T(8,128)(2,1)S(1)} collective-permute-done((bf16[160,640]{1,0:T(8,128)(2,1)S(1)}, bf16[160,640]{1,0:T(8,128)(2,1)S(1)}, u32[]{:S(2)}, u32[]{:S(2)}) %collective-permute-start.14) | collective-permute-done | bytes 204832 | tf_op jit(solution)/shard_map/ppermute | solution.py:64
  205.7 3.2 reshape.244
  228.6 5.8 %attend.3 = (bf16[160,960]{1,0:T(8,128)(2,1)S(1)}, f32[8,480]{1,0:T(8,128)S(1)}) custom-call(bf16[160,960]{1,0:T(8,128)(2,1)S(1)} %copy-done.9, bf16[1280,640]{1,0:T(8,128)(2,1)S(1)} %copy-done.12, s32[1,480]{1,0:T(1,128)S(1)} %broadcast_in_dim_tile.6.sq, s32[1,480]{1,0:T(1,128)S(1)} %broadcast_in_dim_tile.7.pq, s32[1280,1]{1,0:T(8,128)S(1)} %copy.108.sk, ...), custom_call_target="tpu_custom_call" | custom-call | flops 3145728000 | bytes 4194304 | tf_op jit(solution)/shard_map/attend/pallas_call | solution.py:314
  237.5 2.7 collective-permute-start.17
  241.4 6.9 %collective-permute-done.17 = bf16[160,1024]{1,0:T(8,128)(2,1)S(1)} collective-permute-done((bf16[160,1024]{1,0:T(8,128)(2,1)S(1)}, bf16[160,1024]{1,0:T(8,128)(2,1)S(1)}, u32[]{:S(2)}, u32[]{:S(2)}) %collective-permute-start.17) | collective-permute-done | bytes 327712 | tf_op jit(solution)/shard_map/ppermute | solution.py:60
  248.3 2.9 fusion.2
  257.9 2.8 fusion.35
  263.4 4.2 weight_grads.9
  267.6 2.9 collective-permute-done.21
  276.6 2.5 collective-permute-start.19
  279.4 8.2 %collective-permute-done.19 = bf16[160,1024]{1,0:T(8,128)(2,1)S(1)} collective-permute-done((bf16[160,1024]{1,0:T(8,128)(2,1)S(1)}, bf16[160,1024]{1,0:T(8,128)(2,1)S(1)}, u32[]{:S(2)}, u32[]{:S(2)}) %collective-permute-start.19) | collective-permute-done | bytes 327712 | tf_op jit(solution)/shard_map/ppermute | solution.py:60
  293.0 10.6 %attend_back.2 = (f32[160,960]{1,0:T(8,128)S(1)}, bf16[1280,640]{1,0:T(8,128)(2,1)S(1)}) custom-call(bf16[160,960]{1,0:T(8,128)(2,1)S(1)} %copy-done.9, bf16[1280,640]{1,0:T(8,128)(2,1)S(1)} %copy-done.13, bf16[160,960]{1,0:T(8,128)(2,1)S(1)} %pad_maximum_fusion.18.da_ref, f32[8,480]{1,0:T(8,128)S(1)} %get-tuple-element.57.lse_ref, ...), custom_call_target="tpu_custom_call" | custom-call | flops 7864320000 | bytes 6291456 | tf_op jit(solution)/shard_map/attend_back/pallas_call | solution.py:335
  310.8 3.1 collective-permute-start.26
  314.0 7.1 %weight_grads.11 = bf16[1024,2432]{1,0:T(8,128)(2,1)} custom-call(bf16[160,1024]{1,0:T(8,128)(2,1)S(1)} %get-tuple-element.97.refs_0_, bf16[160,480]{1,0:T(8,128)(2,1)S(1)} %get-tuple-element.160.refs_1_, bf16[160,1024]{1,0:T(8,128)(2,1)S(1)} %get-tuple-element.118.refs_2_, bf16[160,32]{1,0:T(8,128)(2,1)S(1)} %broadcast_8_refs_3__refs_8_.2.refs_3_.refs_8_, ...), custom_call_target="tpu_custom_call" | custom-call | flops 3187671040 | bytes 9961472 | tf_op jit(solution)/shard_map/weight_grads/pallas_call | solution.py:141
  325.9 2.7 copy.93
  340.9 8.1 %collective-permute-done.28 = bf16[160,1024]{1,0:T(8,128)(2,1)S(1)} collective-permute-done((bf16[160,1024]{1,0:T(8,128)(2,1)S(1)}, bf16[160,1024]{1,0:T(8,128)(2,1)S(1)}, u32[]{:S(2)}, u32[]{:S(2)}) %collective-permute-start.28) | collective-permute-done | bytes 327712 | tf_op jit(solution)/shard_map/ppermute | solution.py:60
  351.2 3.0 fusion.12
  356.4 2.8 fusion.32
  361.1 4.4 weight_grads.13
  365.4 3.3 collective-permute-done.29
  377.3 10.5 %attend_back.3 = (f32[160,960]{1,0:T(8,128)S(1)}, bf16[1280,640]{1,0:T(8,128)(2,1)S(1)}) custom-call(bf16[160,960]{1,0:T(8,128)(2,1)S(1)} %copy.106.q_ref, bf16[1280,640]{1,0:T(8,128)(2,1)S(1)} %copy-done.11, bf16[160,960]{1,0:T(8,128)(2,1)S(1)} %pad_maximum_fusion.19.da_ref, f32[8,480]{1,0:T(8,128)S(1)} %get-tuple-element.69.lse_ref, ...), custom_call_target="tpu_custom_call" | custom-call | flops 7864320000 | bytes 6291456 | tf_op jit(solution)/shard_map/attend_back/pallas_call | solution.py:335
  397.8 9.0 %weight_grads.15 = bf16[1024,3328]{1,0:T(8,128)(2,1)} custom-call(bf16[160,1024]{1,0:T(8,128)(2,1)S(1)} %multiply_convert_fusion.17.refs_0_, bf16[160,800]{1,0:T(8,128)(2,1)S(1)} %get-tuple-element.155.refs_1_, bf16[160,1024]{1,0:T(8,128)(2,1)S(1)} %get-tuple-element.131.refs_2_, bf16[160,96]{1,0:T(8,128)(2,1)S(1)} %broadcast_6_refs_3_.2.refs_3_, ...), custom_call_target="tpu_custom_call" | custom-call | flops 4362076160 | bytes 13631488 | tf_op jit(solution)/shard_map/weight_grads/pallas_call | solution.py:141
  428.9 4.3 collective-permute-done.41
  438.8 2.9 collective-permute-start.48
  446.4 4.1 collective-permute-done.48
  450.7 4.4 collective-permute-done.50
  457.4 2.7 collective-permute-start.51
  460.7 4.8 collective-permute-done.44
  468.6 4.9 collective-permute-start.47
  473.5 24.1 %reduce-scatter.5.cloned.1.call-done = bf16[64,3328]{1,0:T(8,128)(2,1)} async-done(((bf16[1024,3328]{1,0:T(8,128)(2,1)}), bf16[64,3328]{1,0:T(8,128)(2,1)}) %reduce-scatter.5.cloned.1.call-update) | async-done | bytes 426000 | tf_op jit(solution)/shard_map/reduce_scatter | solution.py:209
  500.0 2.6 collective-permute-start.58
  506.1 2.8 collective-permute-done.58
  508.9 3.5 collective-permute-start.62
  513.4 4.0 collective-permute-done.62
  517.4 4.8 collective-permute-start.61
  (497 shorter events, 226.7 us)
Async XLA Ops:
  7.2 74.5 %all-gather.3.cloned.1.call-start = ((), (), s32[]{:S(2)}) async-start(), calls=%async_computation.2 | async-start | bytes 7241728 | tf_op jit(solution)/shard_map/all_gather | solution.py:417
  14.8 132.8 %all-gather.5.cloned.1.call-start = ((), (), s32[]{:S(2)}) async-start(), calls=%async_computation.3 | async-start | bytes 7241728 | tf_op jit(solution)/shard_map/all_gather | solution.py:417
  16.0 392.7 %reduce-scatter.3.cloned.1.call-start = ((), (), s32[]{:S(2)}) async-start(), calls=%async_computation.4 | async-start | bytes 5292032 | tf_op jit(solution)/shard_map/reduce_scatter | solution.py:209
  85.3 13.5 %collective-permute-start = (bf16[1024,1408]{1,0:T(8,128)(2,1)}, bf16[1024,1408]{1,0:T(8,128)(2,1)}, u32[]{:S(2)}, u32[]{:S(2)}) collective-permute-start(bf16[1024,1408]{1,0:T(8,128)(2,1)} %slice.634), channel_id=1, source_target_pairs={{0,2},{2,0},{1,3},{3,1},{4,6},{6,4},{5,7},{7,5},{8,10},{10,8},{9,1... | collective-permute-start | bytes 8650760 | tf_op jit(solution)/shard_map/ppermute | solution.py:60
  94.2 63.8 %collective-permute-start.10 = (bf16[1024,1920]{1,0:T(8,128)(2,1)}, bf16[1024,1920]{1,0:T(8,128)(2,1)}, u32[]{:S(2)}, u32[]{:S(2)}) collective-permute-start(bf16[1024,1920]{1,0:T(8,128)(2,1)} %slice.650), channel_id=1, source_target_pairs={{0,2},{2,0},{1,3},{3,1},{4,6},{6,4},{5,7},{7,5},{8,10},{10,8},{9,1... | collective-permute-start | bytes 11796488 | tf_op jit(solution)/shard_map/ppermute | solution.py:60
  104.1 11.7 %collective-permute-start.1 = (bf16[160,640]{1,0:T(8,128)(2,1)S(1)}, bf16[160,640]{1,0:T(8,128)(2,1)S(1)}, u32[]{:S(2)}, u32[]{:S(2)}) collective-permute-start(bf16[160,640]{1,0:T(8,128)(2,1)S(1)} %get-tuple-element.104), channel_id=1, source_target_pairs={{0,1},{1,0},{4,5},{5,4},{2,3},{3,2},{6,7},{7,6},{8,9},{9,8},{12,13... | collective-permute-start | bytes 614408 | tf_op jit(solution)/shard_map/ppermute | solution.py:64
  107.8 11.1 %collective-permute-start.7 = (s32[160,2]{0,1:T(2,128)S(1)}, s32[160,2]{0,1:T(2,128)S(1)}, u32[]{:S(2)}, u32[]{:S(2)}) collective-permute-start(s32[160,2]{0,1:T(2,128)S(1)} %pad_add_fusion.1), channel_id=1, source_target_pairs={{0,5},{1,4},{4,0},{5,1},{2,7},{3,6},{6,2},{7,3},{8,13},{9,12},{12,... | collective-permute-start | bytes 3848 | tf_op jit(solution)/shard_map/ppermute | solution.py:64
  117.2 13.1 %collective-permute-start.4 = (bf16[640,640]{1,0:T(8,128)(2,1)}, bf16[640,640]{1,0:T(8,128)(2,1)}, u32[]{:S(2)}, u32[]{:S(2)}) collective-permute-start(bf16[640,640]{1,0:T(8,128)(2,1)} %pad_maximum_fusion.2), channel_id=1, source_target_pairs={{0,2},{2,0},{1,3},{3,1},{4,6},{6,4},{5,7},{7,5},{8,10},{10,8},{9,1... | collective-permute-start | bytes 2457608 | tf_op jit(solution)/shard_map/ppermute | solution.py:60
  144.4 10.4 %collective-permute-start.9 = (bf16[160,1024]{1,0:T(8,128)(2,1)S(1)}, bf16[160,1024]{1,0:T(8,128)(2,1)S(1)}, u32[]{:S(2)}, u32[]{:S(2)}) collective-permute-start(bf16[160,1024]{1,0:T(8,128)(2,1)S(1)} %multiply_convert_fusion.18), channel_id=1, source_target_pairs={{0,1},{1,0},{2,3},{3,2},{4,5},{5,4},{6,7},{7,6},{8,9},{9,8},{10,11... | collective-permute-start | bytes 983048 | tf_op jit(solution)/shard_map/ppermute | solution.py:60
  149.7 27.6 %collective-permute-start.12 = (bf16[1024,1408]{1,0:T(8,128)(2,1)S(1)}, bf16[1024,1408]{1,0:T(8,128)(2,1)S(1)}, u32[]{:S(2)}, u32[]{:S(2)}) collective-permute-start(bf16[1024,1408]{1,0:T(8,128)(2,1)S(1)} %slice.669), channel_id=1, source_target_pairs={{0,2},{2,0},{1,3},{3,1},{4,6},{6,4},{5,7},{7,5},{8,10},{10,8},{9,1... | collective-permute-start | bytes 8650760 | tf_op jit(solution)/shard_map/ppermute | solution.py:60
  169.4 71.9 %collective-permute-start.18 = (bf16[1024,1920]{1,0:T(8,128)(2,1)}, bf16[1024,1920]{1,0:T(8,128)(2,1)}, u32[]{:S(2)}, u32[]{:S(2)}) collective-permute-start(bf16[1024,1920]{1,0:T(8,128)(2,1)} %slice.683), channel_id=1, source_target_pairs={{0,2},{2,0},{1,3},{3,1},{4,6},{6,4},{5,7},{7,5},{8,10},{10,8},{9,1... | collective-permute-start | bytes 11796488 | tf_op jit(solution)/shard_map/ppermute | solution.py:60
  189.9 11.2 %collective-permute-start.14 = (bf16[160,640]{1,0:T(8,128)(2,1)S(1)}, bf16[160,640]{1,0:T(8,128)(2,1)S(1)}, u32[]{:S(2)}, u32[]{:S(2)}) collective-permute-start(bf16[160,640]{1,0:T(8,128)(2,1)S(1)} %get-tuple-element.100), channel_id=1, source_target_pairs={{0,4},{1,5},{4,1},{5,0},{2,6},{3,7},{6,3},{7,2},{8,12},{9,13},{12,... | collective-permute-start | bytes 614408 | tf_op jit(solution)/shard_map/ppermute | solution.py:64
  189.9 11.2 %collective-permute-start.13 = (bf16[160,640]{1,0:T(8,128)(2,1)S(1)}, bf16[160,640]{1,0:T(8,128)(2,1)S(1)}, u32[]{:S(2)}, u32[]{:S(2)}) collective-permute-start(bf16[160,640]{1,0:T(8,128)(2,1)S(1)} %get-tuple-element.100), channel_id=1, source_target_pairs={{0,1},{1,0},{4,5},{5,4},{2,3},{3,2},{6,7},{7,6},{8,9},{9,8},{12,13... | collective-permute-start | bytes 614408 | tf_op jit(solution)/shard_map/ppermute | solution.py:64
  190.4 10.6 %collective-permute-start.15 = (bf16[160,640]{1,0:T(8,128)(2,1)S(1)}, bf16[160,640]{1,0:T(8,128)(2,1)S(1)}, u32[]{:S(2)}, u32[]{:S(2)}) collective-permute-start(bf16[160,640]{1,0:T(8,128)(2,1)S(1)} %get-tuple-element.100), channel_id=1, source_target_pairs={{0,5},{1,4},{4,0},{5,1},{2,7},{3,6},{6,2},{7,3},{8,13},{9,12},{12,... | collective-permute-start | bytes 614408 | tf_op jit(solution)/shard_map/ppermute | solution.py:64
  203.8 21.2 %collective-permute-start.16 = (bf16[640,640]{1,0:T(8,128)(2,1)}, bf16[640,640]{1,0:T(8,128)(2,1)}, u32[]{:S(2)}, u32[]{:S(2)}) collective-permute-start(bf16[640,640]{1,0:T(8,128)(2,1)} %pad_maximum_fusion.3), channel_id=1, source_target_pairs={{0,2},{2,0},{1,3},{3,1},{4,6},{6,4},{5,7},{7,5},{8,10},{10,8},{9,1... | collective-permute-start | bytes 2457608 | tf_op jit(solution)/shard_map/ppermute | solution.py:60
  215.8 24.5 %collective-permute-start.20 = (bf16[160,1024]{1,0:T(8,128)(2,1)}, bf16[160,1024]{1,0:T(8,128)(2,1)}, u32[]{:S(2)}, u32[]{:S(2)}) collective-permute-start(bf16[160,1024]{1,0:T(8,128)(2,1)} %convert_element_type.304), channel_id=1, source_target_pairs={{0,1},{1,0},{2,3},{3,2},{4,5},{5,4},{6,7},{7,6},{8,9},{9,8},{10,11... | collective-permute-start | bytes 983048 | tf_op jit(solution)/shard_map/ppermute | solution.py:60
  237.5 10.8 %collective-permute-start.17 = (bf16[160,1024]{1,0:T(8,128)(2,1)S(1)}, bf16[160,1024]{1,0:T(8,128)(2,1)S(1)}, u32[]{:S(2)}, u32[]{:S(2)}) collective-permute-start(bf16[160,1024]{1,0:T(8,128)(2,1)S(1)} %multiply_convert_fusion.16), channel_id=1, source_target_pairs={{0,1},{1,0},{2,3},{3,2},{4,5},{5,4},{6,7},{7,6},{8,9},{9,8},{10,11... | collective-permute-start | bytes 983048 | tf_op jit(solution)/shard_map/ppermute | solution.py:60
  270.4 33.2 %collective-permute-start.23 = (bf16[1024,1920]{1,0:T(8,128)(2,1)}, bf16[1024,1920]{1,0:T(8,128)(2,1)}, u32[]{:S(2)}, u32[]{:S(2)}) collective-permute-start(bf16[1024,1920]{1,0:T(8,128)(2,1)} %weight_grads.9), channel_id=1, source_target_pairs={{0,2},{2,0},{1,3},{3,1},{4,6},{6,4},{5,7},{7,5},{8,10},{10,8},{9,1... | collective-permute-start | bytes 11796488 | tf_op jit(solution)/shard_map/ppermute | solution.py:60
  276.6 10.9 %collective-permute-start.19 = (bf16[160,1024]{1,0:T(8,128)(2,1)S(1)}, bf16[160,1024]{1,0:T(8,128)(2,1)S(1)}, u32[]{:S(2)}, u32[]{:S(2)}) collective-permute-start(bf16[160,1024]{1,0:T(8,128)(2,1)S(1)} %slice.920), channel_id=1, source_target_pairs={{0,1},{1,0},{2,3},{3,2},{4,5},{5,4},{6,7},{7,6},{8,9},{9,8},{10,11... | collective-permute-start | bytes 983048 | tf_op jit(solution)/shard_map/ppermute | solution.py:60
  291.9 11.8 %collective-permute-start.22 = (bf16[1024,512]{1,0:T(8,128)(2,1)S(1)}, bf16[1024,512]{1,0:T(8,128)(2,1)S(1)}, u32[]{:S(2)}, u32[]{:S(2)}) collective-permute-start(bf16[1024,512]{1,0:T(8,128)(2,1)S(1)} %weight_grads.10), channel_id=1, source_target_pairs={{0,2},{2,0},{1,3},{3,1},{4,6},{6,4},{5,7},{7,5},{8,10},{10,8},{9,1... | collective-permute-start | bytes 3145736 | tf_op jit(solution)/shard_map/ppermute | solution.py:60
  308.4 12.7 %collective-permute-start.25 = (bf16[160,640]{1,0:T(8,128)(2,1)}, bf16[160,640]{1,0:T(8,128)(2,1)}, u32[]{:S(2)}, u32[]{:S(2)}) collective-permute-start(bf16[160,640]{1,0:T(8,128)(2,1)} %get-tuple-element.145), channel_id=1, source_target_pairs={{0,1},{1,0},{4,5},{5,4},{2,3},{3,2},{6,7},{7,6},{8,9},{9,8},{12,13... | collective-permute-start | bytes 614408 | tf_op jit(solution)/shard_map/ppermute | solution.py:64
  310.8 10.8 %collective-permute-start.27 = (bf16[160,640]{1,0:T(8,128)(2,1)}, bf16[160,640]{1,0:T(8,128)(2,1)}, u32[]{:S(2)}, u32[]{:S(2)}) collective-permute-start(bf16[160,640]{1,0:T(8,128)(2,1)} %get-tuple-element.146), channel_id=1, source_target_pairs={{0,4},{1,5},{4,1},{5,0},{2,6},{3,7},{6,3},{7,2},{8,12},{9,13},{12,... | collective-permute-start | bytes 614408 | tf_op jit(solution)/shard_map/ppermute | solution.py:64
  310.8 10.8 %collective-permute-start.26 = (bf16[160,640]{1,0:T(8,128)(2,1)}, bf16[160,640]{1,0:T(8,128)(2,1)}, u32[]{:S(2)}, u32[]{:S(2)}) collective-permute-start(bf16[160,640]{1,0:T(8,128)(2,1)} %get-tuple-element.147), channel_id=1, source_target_pairs={{0,5},{1,4},{4,0},{5,1},{2,7},{3,6},{6,2},{7,3},{8,13},{9,12},{12,... | collective-permute-start | bytes 614408 | tf_op jit(solution)/shard_map/ppermute | solution.py:64
  323.7 173.9 %reduce-scatter.5.cloned.1.call-start = ((), (), s32[]{:S(2)}) async-start(), calls=%async_computation.5 | async-start | bytes 7241728 | tf_op jit(solution)/shard_map/reduce_scatter | solution.py:209
  338.7 10.4 %collective-permute-start.28 = (bf16[160,1024]{1,0:T(8,128)(2,1)S(1)}, bf16[160,1024]{1,0:T(8,128)(2,1)S(1)}, u32[]{:S(2)}, u32[]{:S(2)}) collective-permute-start(bf16[160,1024]{1,0:T(8,128)(2,1)S(1)} %convert_element_type.318), channel_id=1, source_target_pairs={{0,1},{1,0},{2,3},{3,2},{4,5},{5,4},{6,7},{7,6},{8,9},{9,8},{10,11... | collective-permute-start | bytes 983048 | tf_op jit(solution)/shard_map/ppermute | solution.py:60
  368.7 19.1 %collective-permute-start.31 = (bf16[1024,1920]{1,0:T(8,128)(2,1)}, bf16[1024,1920]{1,0:T(8,128)(2,1)}, u32[]{:S(2)}, u32[]{:S(2)}) collective-permute-start(bf16[1024,1920]{1,0:T(8,128)(2,1)} %weight_grads.13), channel_id=1, source_target_pairs={{0,2},{2,0},{1,3},{3,1},{4,6},{6,4},{5,7},{7,5},{8,10},{10,8},{9,1... | collective-permute-start | bytes 11796488 | tf_op jit(solution)/shard_map/ppermute | solution.py:60
  376.7 11.1 %collective-permute-start.30 = (bf16[1024,512]{1,0:T(8,128)(2,1)S(1)}, bf16[1024,512]{1,0:T(8,128)(2,1)S(1)}, u32[]{:S(2)}, u32[]{:S(2)}) collective-permute-start(bf16[1024,512]{1,0:T(8,128)(2,1)S(1)} %weight_grads.14), channel_id=1, source_target_pairs={{0,2},{2,0},{1,3},{3,1},{4,6},{6,4},{5,7},{7,5},{8,10},{10,8},{9,1... | collective-permute-start | bytes 3145736 | tf_op jit(solution)/shard_map/ppermute | solution.py:60
  376.8 21.0 %collective-permute-start.36 = (bf16[1024,896]{1,0:T(8,128)(2,1)S(1)}, bf16[1024,896]{1,0:T(8,128)(2,1)}, u32[]{:S(2)}, u32[]{:S(2)}) collective-permute-start(bf16[1024,896]{1,0:T(8,128)(2,1)S(1)} %weight_grads.12), channel_id=1, source_target_pairs={{0,2},{2,0},{1,3},{3,1},{4,6},{6,4},{5,7},{7,5},{8,10},{10,8},{9,1... | collective-permute-start | bytes 5505032 | tf_op jit(solution)/shard_map/ppermute | solution.py:60
  393.2 13.7 %collective-permute-start.33 = (bf16[160,640]{1,0:T(8,128)(2,1)}, bf16[160,640]{1,0:T(8,128)(2,1)S(1)}, u32[]{:S(2)}, u32[]{:S(2)}) collective-permute-start(bf16[160,640]{1,0:T(8,128)(2,1)} %get-tuple-element.142), channel_id=1, source_target_pairs={{0,1},{1,0},{4,5},{5,4},{2,3},{3,2},{6,7},{7,6},{8,9},{9,8},{12,13... | collective-permute-start | bytes 614408 | tf_op jit(solution)/shard_map/ppermute | solution.py:64
  394.8 12.1 %collective-permute-start.35 = (bf16[160,640]{1,0:T(8,128)(2,1)}, bf16[160,640]{1,0:T(8,128)(2,1)S(1)}, u32[]{:S(2)}, u32[]{:S(2)}) collective-permute-start(bf16[160,640]{1,0:T(8,128)(2,1)} %get-tuple-element.143), channel_id=1, source_target_pairs={{0,4},{1,5},{4,1},{5,0},{2,6},{3,7},{6,3},{7,2},{8,12},{9,13},{12,... | collective-permute-start | bytes 614408 | tf_op jit(solution)/shard_map/ppermute | solution.py:64
  395.3 11.5 %collective-permute-start.34 = (bf16[160,640]{1,0:T(8,128)(2,1)S(1)}, bf16[160,640]{1,0:T(8,128)(2,1)S(1)}, u32[]{:S(2)}, u32[]{:S(2)}) collective-permute-start(bf16[160,640]{1,0:T(8,128)(2,1)S(1)} %get-tuple-element.144), channel_id=1, source_target_pairs={{0,5},{1,4},{4,0},{5,1},{2,7},{3,6},{6,2},{7,3},{8,13},{9,12},{12,... | collective-permute-start | bytes 614408 | tf_op jit(solution)/shard_map/ppermute | solution.py:64
  419.5 14.7 %collective-permute-start.37 = (bf16[1024,896]{1,0:T(8,128)(2,1)}, bf16[1024,896]{1,0:T(8,128)(2,1)S(1)}, u32[]{:S(2)}, u32[]{:S(2)}) collective-permute-start(bf16[1024,896]{1,0:T(8,128)(2,1)} %weight_grads.16), channel_id=1, source_target_pairs={{0,2},{2,0},{1,3},{3,1},{4,6},{6,4},{5,7},{7,5},{8,10},{10,8},{9,1... | collective-permute-start | bytes 5505032 | tf_op jit(solution)/shard_map/ppermute | solution.py:60
  438.8 11.7 %collective-permute-start.48 = (bf16[4,64,384]{2,1,0:T(8,128)(2,1)}, bf16[4,64,384]{2,1,0:T(8,128)(2,1)S(1)}, u32[]{:S(2)}, u32[]{:S(2)}) collective-permute-start(bf16[4,64,384]{2,1,0:T(8,128)(2,1)} %get-tuple-element.148), channel_id=1, source_target_pairs={{0,64},{32,96},{64,0},{96,32},{1,65},{33,97},{65,1},{97,33},{2,66}... | collective-permute-start | bytes 589832 | tf_op jit(solution)/shard_map/ppermute | solution.py:91
  441.7 13.4 %collective-permute-start.50 = (bf16[4,64,384]{2,1,0:T(8,128)(2,1)}, bf16[4,64,384]{2,1,0:T(8,128)(2,1)}, u32[]{:S(2)}, u32[]{:S(2)}) collective-permute-start(bf16[4,64,384]{2,1,0:T(8,128)(2,1)} %get-tuple-element.149), channel_id=1, source_target_pairs={{0,96},{32,0},{64,32},{96,64},{1,97},{33,1},{65,33},{97,65},{2,98}... | collective-permute-start | bytes 589832 | tf_op jit(solution)/shard_map/ppermute | solution.py:91
  442.5 13.8 %collective-permute-start.49 = (bf16[4,64,384]{2,1,0:T(8,128)(2,1)S(1)}, bf16[4,64,384]{2,1,0:T(8,128)(2,1)}, u32[]{:S(2)}, u32[]{:S(2)}) collective-permute-start(bf16[4,64,384]{2,1,0:T(8,128)(2,1)S(1)} %get-tuple-element.150), channel_id=1, source_target_pairs={{0,32},{32,64},{64,96},{96,0},{1,33},{33,65},{65,97},{97,1},{2,34}... | collective-permute-start | bytes 589832 | tf_op jit(solution)/shard_map/ppermute | solution.py:91
  443.3 85.5 %collective-permute-start.65 = (bf16[64,1920]{1,0:T(8,128)(2,1)S(1)}, bf16[64,1920]{1,0:T(8,128)(2,1)S(1)}, u32[]{:S(2)}, u32[]{:S(2)}) collective-permute-start(bf16[64,1920]{1,0:T(8,128)(2,1)S(1)} %add_convert_fusion.5.refs_8_), channel_id=1, source_target_pairs={{0,2},{2,0},{1,3},{3,1},{4,6},{6,4},{5,7},{7,5},{8,10},{10,8},{9,1... | collective-permute-start | bytes 737288 | tf_op jit(solution)/shard_map/ppermute | solution.py:60
  445.2 14.9 %collective-permute-start.42 = (bf16[4,64,512]{2,1,0:T(8,128)(2,1)S(1)}, bf16[4,64,512]{2,1,0:T(8,128)(2,1)S(1)}, u32[]{:S(2)}, u32[]{:S(2)}) collective-permute-start(bf16[4,64,512]{2,1,0:T(8,128)(2,1)S(1)} %get-tuple-element.139), channel_id=1, source_target_pairs={{0,16},{8,24},{16,0},{24,8},{1,17},{9,25},{17,1},{25,9},{2,18},{10... | collective-permute-start | bytes 786440 | tf_op jit(solution)/shard_map/ppermute | solution.py:91
  450.5 14.9 %collective-permute-start.44 = (bf16[4,64,512]{2,1,0:T(8,128)(2,1)S(1)}, bf16[4,64,512]{2,1,0:T(8,128)(2,1)S(1)}, u32[]{:S(2)}, u32[]{:S(2)}) collective-permute-start(bf16[4,64,512]{2,1,0:T(8,128)(2,1)S(1)} %get-tuple-element.140), channel_id=1, source_target_pairs={{0,24},{8,0},{16,8},{24,16},{1,25},{9,1},{17,9},{25,17},{2,26},{10... | collective-permute-start | bytes 786440 | tf_op jit(solution)/shard_map/ppermute | solution.py:91
  455.1 11.8 %collective-permute-start.43 = (bf16[4,64,512]{2,1,0:T(8,128)(2,1)S(1)}, bf16[4,64,512]{2,1,0:T(8,128)(2,1)S(1)}, u32[]{:S(2)}, u32[]{:S(2)}) collective-permute-start(bf16[4,64,512]{2,1,0:T(8,128)(2,1)S(1)} %get-tuple-element.141), channel_id=1, source_target_pairs={{0,8},{8,16},{16,24},{24,0},{1,9},{9,17},{17,25},{25,1},{2,10},{10... | collective-permute-start | bytes 786440 | tf_op jit(solution)/shard_map/ppermute | solution.py:91
  457.4 11.2 %collective-permute-start.51 = (bf16[64,384]{1,0:T(8,128)(2,1)S(1)}, bf16[64,384]{1,0:T(8,128)(2,1)S(1)}, u32[]{:S(2)}, u32[]{:S(2)}) collective-permute-start(bf16[64,384]{1,0:T(8,128)(2,1)S(1)} %get-tuple-element.177), channel_id=1, source_target_pairs={{0,16},{8,24},{16,0},{24,8},{1,17},{9,25},{17,1},{25,9},{2,18},{10... | collective-permute-start | bytes 147464 | tf_op jit(solution)/shard_map/ppermute | solution.py:91
  460.1 13.3 %collective-permute-start.53 = (bf16[64,384]{1,0:T(8,128)(2,1)S(1)}, bf16[64,384]{1,0:T(8,128)(2,1)S(1)}, u32[]{:S(2)}, u32[]{:S(2)}) collective-permute-start(bf16[64,384]{1,0:T(8,128)(2,1)S(1)} %get-tuple-element.178), channel_id=1, source_target_pairs={{0,24},{8,0},{16,8},{24,16},{1,25},{9,1},{17,9},{25,17},{2,26},{10... | collective-permute-start | bytes 147464 | tf_op jit(solution)/shard_map/ppermute | solution.py:91
  467.1 32.9 %collective-permute-start.45 = (bf16[64,512]{1,0:T(8,128)(2,1)S(1)}, bf16[64,512]{1,0:T(8,128)(2,1)S(1)}, u32[]{:S(2)}, u32[]{:S(2)}) collective-permute-start(bf16[64,512]{1,0:T(8,128)(2,1)S(1)} %get-tuple-element.170), channel_id=1, source_target_pairs={{0,64},{32,96},{64,0},{96,32},{1,65},{33,97},{65,1},{97,33},{2,66}... | collective-permute-start | bytes 196616 | tf_op jit(solution)/shard_map/ppermute | solution.py:91
  468.6 34.0 %collective-permute-start.47 = (bf16[64,512]{1,0:T(8,128)(2,1)S(1)}, bf16[64,512]{1,0:T(8,128)(2,1)S(1)}, u32[]{:S(2)}, u32[]{:S(2)}) collective-permute-start(bf16[64,512]{1,0:T(8,128)(2,1)S(1)} %get-tuple-element.171), channel_id=1, source_target_pairs={{0,96},{32,0},{64,32},{96,64},{1,97},{33,1},{65,33},{97,65},{2,98}... | collective-permute-start | bytes 196616 | tf_op jit(solution)/shard_map/ppermute | solution.py:91
  473.5 30.3 %collective-permute-start.46 = (bf16[64,512]{1,0:T(8,128)(2,1)S(1)}, bf16[64,512]{1,0:T(8,128)(2,1)S(1)}, u32[]{:S(2)}, u32[]{:S(2)}) collective-permute-start(bf16[64,512]{1,0:T(8,128)(2,1)S(1)} %get-tuple-element.172), channel_id=1, source_target_pairs={{0,32},{32,64},{64,96},{96,0},{1,33},{33,65},{65,97},{97,1},{2,34}... | collective-permute-start | bytes 196616 | tf_op jit(solution)/shard_map/ppermute | solution.py:91
  503.8 18.5 %collective-permute-start.55 = (bf16[64,896]{1,0:T(8,128)(2,1)S(1)}, bf16[64,896]{1,0:T(8,128)(2,1)S(1)}, u32[]{:S(2)}, u32[]{:S(2)}) collective-permute-start(bf16[64,896]{1,0:T(8,128)(2,1)S(1)} %pad_maximum_fusion.24), channel_id=1, source_target_pairs={{0,4},{1,5},{4,1},{5,0},{2,6},{3,7},{6,3},{7,2},{8,12},{9,13},{12,... | collective-permute-start | bytes 344072 | tf_op jit(solution)/shard_map/ppermute | solution.py:64
  505.2 17.2 %collective-permute-start.54 = (bf16[64,896]{1,0:T(8,128)(2,1)S(1)}, bf16[64,896]{1,0:T(8,128)(2,1)S(1)}, u32[]{:S(2)}, u32[]{:S(2)}) collective-permute-start(bf16[64,896]{1,0:T(8,128)(2,1)S(1)} %pad_maximum_fusion.24), channel_id=1, source_target_pairs={{0,1},{1,0},{4,5},{5,4},{2,3},{3,2},{6,7},{7,6},{8,9},{9,8},{12,13... | collective-permute-start | bytes 344072 | tf_op jit(solution)/shard_map/ppermute | solution.py:64
  508.9 13.4 %collective-permute-start.56 = (bf16[64,896]{1,0:T(8,128)(2,1)S(1)}, bf16[64,896]{1,0:T(8,128)(2,1)S(1)}, u32[]{:S(2)}, u32[]{:S(2)}) collective-permute-start(bf16[64,896]{1,0:T(8,128)(2,1)S(1)} %pad_maximum_fusion.24), channel_id=1, source_target_pairs={{0,5},{1,4},{4,0},{5,1},{2,7},{3,6},{6,2},{7,3},{8,13},{9,12},{12,... | collective-permute-start | bytes 344072 | tf_op jit(solution)/shard_map/ppermute | solution.py:64
  517.4 11.4 %collective-permute-start.61 = (bf16[64,1408]{1,0:T(8,128)(2,1)S(1)}, bf16[64,1408]{1,0:T(8,128)(2,1)S(1)}, u32[]{:S(2)}, u32[]{:S(2)}) collective-permute-start(bf16[64,1408]{1,0:T(8,128)(2,1)S(1)} %add_convert_fusion.6.refs_2_), channel_id=1, source_target_pairs={{0,2},{2,0},{1,3},{3,1},{4,6},{6,4},{5,7},{7,5},{8,10},{10,8},{9,1... | collective-permute-start | bytes 540680 | tf_op jit(solution)/shard_map/ppermute | solution.py:60
  (106 other events, 754.3 us)
Sparse Core Ops, SparseCore 0:
  15.0 66.6 all-gather.2
  84.4 63.1 all-gather.4
  323.8 76.7 reduce-scatter.2
  408.9 88.7 reduce-scatter.4
